TPU v7x, 256 devices: a whole 4x4x8 slice. The times are simulated.
256 devices in a mesh: blk: 64 (over y, x, z_hi), rep: 4 (over z_lo, core).
Axes of the slice: x: 4, y: 4, z: 8 (z_hi: 4, z_lo: 2; z = z_hi * 2 + z_lo), core: 2. Of those that a mesh axis runs over, the one named last changes fastest.
Arguments:
- coords: float32 [3, 1200, 16384], P(None, 'rep', 'blk'), may hold values from -40 to 40
- frame_count: int32 [64], P('blk'), may hold values from 64 to 256, as said below
Outputs:
- deviation_behind: float32 [3, 16384, 256], P(None, ('blk', 'rep'))
- deviation_ahead: float32 [3, 16384, 256], P(None, ('blk', 'rep'))
Inputs may be any that keep to these rules, and one draw needn't show every extreme that they name: `frame_count`: at least one block is full and at least one holds exactly 64 frames.
All inputs are finite; a program needn't handle non-finite values.
Results may differ from a plain program's by a relative error of at most 0.0003.
Values sent between devices are 32-bit elements; how exact they have to be, the bound alone decides.
No kernel may reach another device: no remote copies, remote signals or barrier semaphores. Data moves between devices by JAX's collectives and lax.ppermute only.
A program may use at most 64 MiB of HBM per device.

v0:
```python
import jax
import jax.numpy as jnp
from jax import lax
from jax.sharding import PartitionSpec as P

NATOM = 1200
ROUNDS = 3
NEWTON = 4


def from_behind(block, axis, distance):
    devices = range(lax.axis_size(axis))
    route = [((i - distance) % len(devices), i) for i in devices]
    return lax.ppermute(block, axis, route)


def pair_minor(upper, lower, left, right):
    return upper[left] * lower[right] - upper[right] * lower[left]


def deviation(covariance, own_sq, other_sq):
    m = [[covariance[first, :, second, :] for second in range(3)] for first in range(3)]
    keyed = [
        [m[0][0] + m[1][1] + m[2][2], m[1][2] - m[2][1], m[2][0] - m[0][2], m[0][1] - m[1][0]],
        [m[1][2] - m[2][1], m[0][0] - m[1][1] - m[2][2], m[0][1] + m[1][0], m[2][0] + m[0][2]],
        [m[2][0] - m[0][2], m[0][1] + m[1][0], -m[0][0] + m[1][1] - m[2][2], m[1][2] + m[2][1]],
        [m[0][1] - m[1][0], m[2][0] + m[0][2], m[1][2] + m[2][1], -m[0][0] - m[1][1] + m[2][2]],
    ]
    top_one, top_two, low_one, low_two = keyed
    det_key = (
        pair_minor(top_one, top_two, 0, 1) * pair_minor(low_one, low_two, 2, 3)
        - pair_minor(top_one, top_two, 0, 2) * pair_minor(low_one, low_two, 1, 3)
        + pair_minor(top_one, top_two, 0, 3) * pair_minor(low_one, low_two, 1, 2)
        + pair_minor(top_one, top_two, 1, 2) * pair_minor(low_one, low_two, 0, 3)
        - pair_minor(top_one, top_two, 1, 3) * pair_minor(low_one, low_two, 0, 2)
        + pair_minor(top_one, top_two, 2, 3) * pair_minor(low_one, low_two, 0, 1)
    )
    det_three = (
        m[0][0] * (m[1][1] * m[2][2] - m[1][2] * m[2][1])
        - m[0][1] * (m[1][0] * m[2][2] - m[1][2] * m[2][0])
        + m[0][2] * (m[1][0] * m[2][1] - m[1][1] * m[2][0])
    )
    square_sum = m[0][0] * m[0][0]
    for first in range(3):
        for second in range(3):
            if first + second > 0:
                square_sum = square_sum + m[first][second] * m[first][second]
    second_coef = -2.0 * square_sum
    first_coef = -8.0 * det_three
    total = own_sq[:, None] + other_sq[None, :]
    largest = 0.5 * total
    for newton_step in range(NEWTON):
        squared = largest * largest
        polynomial = squared * squared + second_coef * squared + first_coef * largest + det_key
        derivative = 4.0 * squared * largest + 2.0 * second_coef * largest + first_coef
        largest = largest - polynomial / derivative
    return total - 2.0 * largest


def shards(coords, frame_count):
    block_rows = coords.shape[2]
    rep_count = lax.axis_size("rep")
    quarter = block_rows // rep_count
    start = lax.axis_index("rep") * quarter
    atom_sums = lax.psum(jnp.sum(coords, axis=1), "rep")
    centroid = atom_sums / NATOM
    centered = coords - centroid[:, None, :]
    self_sq = lax.psum(jnp.sum(centered * centered, axis=(0, 1)), "rep") / NATOM
    block_count = frame_count.astype(jnp.float32)
    columns = jnp.arange(block_rows, dtype=jnp.float32)
    own_valid = columns < block_count[0]
    mine = (centered, self_sq, block_count)
    held = mine
    behind_list = []
    ahead_list = []
    for distance in range(1, ROUNDS + 1):
        held = from_behind((mine[0], mine[1], mine[2]), "blk", distance)
        partner_coords, partner_sq, partner_count = held
        other_valid = columns < partner_count[0]
        partial_value = lax.dot_general(
            centered, partner_coords, (((1,), (1,)), ((), ())), precision=lax.Precision.HIGHEST
        )
        covariance = lax.psum(partial_value, "rep") / NATOM
        mask = own_valid[:, None] & other_valid[None, :]
        whole_block = jnp.where(mask, deviation(covariance, self_sq, partner_sq), 0.0)
        behind = lax.dynamic_slice_in_dim(whole_block, start, quarter, 0)
        outgoing = lax.dynamic_slice_in_dim(whole_block, start, quarter, 1).T
        ahead = from_behind(outgoing, "blk", -distance)
        behind_list.append(behind)
        ahead_list.append(ahead)
    return (jnp.stack(behind_list, 0), jnp.stack(ahead_list, 0))


def solution(mesh):
    in_specs = (P(None, "rep", "blk"), P("blk"))
    out_specs = (P(None, ("blk", "rep"), None), P(None, ("blk", "rep"), None))
    return jax.shard_map(shards, mesh=mesh, in_specs=in_specs, out_specs=out_specs, check_vma=False)
```

profile of v0, /device:TPU:1, one launch (start us, length us, event | category | flops | bytes accessed | tf_op | source)
XLA Modules:
  0.0 294.5 jit_solution(2338195299669401793)
XLA Ops:
  7.2 0.0 all-reduce.3.cloned.1.call-start
  7.2 1.3 reduce_sum.18
  8.5 8.3 %psum.35 = f32[3,256]{1,0:T(4,128)S(1)} all-reduce(f32[3,256]{1,0:T(4,128)S(1)} %reduce_sum.18), channel_id=1, replica_groups=mesh['blk'=64,'rep'=4] {'rep'}, use_global_device_ids=true, to_apply=%region_1.0 | all-reduce | flops 768 | bytes 6144 | tf_op jit(solution)/shard_map/psum | solution.py:65
  16.7 1.3 multiply_reduce_fusion
  18.1 5.3 %collective-permute-start.5 = (f32[3,300,256]{2,1,0:T(8,128)S(1)}, f32[3,300,256]{2,1,0:T(8,128)S(1)}, u32[]{:S(2)}, u32[]{:S(2)}) collective-permute-start(f32[3,300,256]{2,1,0:T(8,128)S(1)} %get-tuple-element.8), channel_id=1, source_target_pairs={{248,0},{252,4},{0,8},{4,12},{8,16},{12,20},{16,24},{20,28},{24,32... | collective-permute-start | bytes 2764808 | tf_op jit(solution)/shard_map/ppermute | solution.py:14
  23.4 1.2 collective-permute-start.2
  24.5 3.3 %collective-permute-start.8 = (f32[3,300,256]{2,1,0:T(8,128)S(1)}, f32[3,300,256]{2,1,0:T(8,128)S(1)}, u32[]{:S(2)}, u32[]{:S(2)}) collective-permute-start(f32[3,300,256]{2,1,0:T(8,128)S(1)} %get-tuple-element.8), channel_id=1, source_target_pairs={{244,0},{248,4},{252,8},{0,12},{4,16},{8,20},{12,24},{16,28},{20,3... | collective-permute-start | bytes 2764808 | tf_op jit(solution)/shard_map/ppermute | solution.py:14
  27.9 27.0 %collective-permute-done.5 = f32[3,300,256]{2,1,0:T(8,128)S(1)} collective-permute-done((f32[3,300,256]{2,1,0:T(8,128)S(1)}, f32[3,300,256]{2,1,0:T(8,128)S(1)}, u32[]{:S(2)}, u32[]{:S(2)}) %collective-permute-start.5) | collective-permute-done | bytes 921632 | tf_op jit(solution)/shard_map/ppermute | solution.py:14
  54.9 5.3 %fusion.2 = f32[3,256,3,256]{3,1,2,0:T(8,128)} fusion(f32[3,300,256]{2,1,0:T(8,128)S(1)} %collective-permute-done.5, f32[3,300,256]{2,1,0:T(8,128)S(1)} %get-tuple-element.8), kind=kOutput, calls=%fused_computation.5 | convolution fusion | flops 2123366400 | bytes 4202496 | tf_op jit(solution)/shard_map/dot_general | solution.py:80
  60.2 31.5 %collective-permute-done.2 = f32[3,300,256]{2,1,0:T(8,128)S(1)} collective-permute-done((f32[3,300,256]{2,1,0:T(8,128)S(1)}, f32[3,300,256]{2,1,0:T(8,128)S(1)}, u32[]{:S(2)}, u32[]{:S(2)}) %collective-permute-start.2) | collective-permute-done | bytes 921632 | tf_op jit(solution)/shard_map/ppermute | solution.py:14
  91.7 5.5 %fusion.6 = f32[3,256,3,256]{3,1,2,0:T(8,128)} fusion(f32[3,300,256]{2,1,0:T(8,128)S(1)} %get-tuple-element.8, f32[3,300,256]{2,1,0:T(8,128)S(1)} %collective-permute-done.2), kind=kOutput, calls=%fused_computation.9 | convolution fusion | flops 2123366400 | bytes 4202496 | tf_op jit(solution)/shard_map/dot_general | solution.py:80
  97.2 14.2 %collective-permute-done.8 = f32[3,300,256]{2,1,0:T(8,128)S(1)} collective-permute-done((f32[3,300,256]{2,1,0:T(8,128)S(1)}, f32[3,300,256]{2,1,0:T(8,128)S(1)}, u32[]{:S(2)}, u32[]{:S(2)}) %collective-permute-start.8) | collective-permute-done | bytes 921632 | tf_op jit(solution)/shard_map/ppermute | solution.py:14
  111.4 5.6 %fusion = f32[3,256,3,256]{3,1,2,0:T(8,128)} fusion(f32[3,300,256]{2,1,0:T(8,128)S(1)} %collective-permute-done.8, f32[3,300,256]{2,1,0:T(8,128)S(1)} %get-tuple-element.8), kind=kOutput, calls=%fused_computation.3 | convolution fusion | flops 2123366400 | bytes 4202496 | tf_op jit(solution)/shard_map/dot_general | solution.py:80
  117.0 0.0 all-reduce.3.cloned.1.call-update
  117.0 7.9 %psum.36 = f32[256]{0:T(256)S(1)} all-reduce(f32[256]{0:T(256)S(1)} %get-tuple-element.7), channel_id=1, replica_groups=mesh['blk'=64,'rep'=4] {'rep'}, use_global_device_ids=true, to_apply=%region_3.0 | all-reduce | flops 256 | bytes 2048 | tf_op jit(solution)/shard_map/psum | solution.py:68
  125.0 0.1 collective-permute-start.1
  125.1 0.2 collective-permute-start.4
  125.9 3.4 %collective-permute-start = (f32[1]{0:T(128)}, f32[1]{0:T(128)}, u32[]{:S(2)}, u32[]{:S(2)}) collective-permute-start(f32[1]{0:T(128)} %convert_element_type.3), channel_id=1, source_target_pairs={{252,0},{0,4},{4,8},{8,12},{12,16},{16,20},{20,24},{24,28},{28,32}... | collective-permute-start | bytes 20 | tf_op jit(solution)/shard_map/ppermute | solution.py:14
  129.3 4.6 %collective-permute-start.3 = (f32[1]{0:T(128)}, f32[1]{0:T(128)}, u32[]{:S(2)}, u32[]{:S(2)}) collective-permute-start(f32[1]{0:T(128)} %convert_element_type.3), channel_id=1, source_target_pairs={{248,0},{252,4},{0,8},{4,12},{8,16},{12,20},{16,24},{20,28},{24,32... | collective-permute-start | bytes 20 | tf_op jit(solution)/shard_map/ppermute | solution.py:14
  133.9 2.8 collective-permute-start.7
  136.7 0.0 collective-permute-done
  136.7 1.9 collective-permute-start.6
  138.6 0.6 iota_compare_fusion.2
  139.3 0.7 collective-permute-done.3
  139.9 0.7 iota_compare_fusion.1
  140.6 3.8 %collective-permute-done.6 = f32[1]{0:T(128)} collective-permute-done((f32[1]{0:T(128)}, f32[1]{0:T(128)}, u32[]{:S(2)}, u32[]{:S(2)}) %collective-permute-start.6) | collective-permute-done | bytes 36 | tf_op jit(solution)/shard_map/ppermute | solution.py:14
  144.4 0.6 iota_compare_fusion
  145.1 114.6 %all-reduce.3.cloned.1.call-done = (f32[3,256,3,256]{3,1,2,0:T(8,128)}, f32[3,256,3,256]{3,1,2,0:T(8,128)}, f32[3,256,3,256]{3,1,2,0:T(8,128)}) async-done(((f32[3,256,3,256]{3,1,2,0:T(8,128)}, f32[3,256,3,256]{3,1,2,0:T(8,128)}, f32[3,256,3,256]{3,1,2,0:T(8,128)}), (f32[3,256,3,256]{3,1,2,0:T(8,128)}, f32[3,256,3,256]{3,1,2,0:T(8,128)}, f32[3,256,3,256]{3,1,2,0:T(8,128)})) %all-reduce.3.cloned.1.call-update) | async-done | bytes 7077904 | tf_op jit(solution)/shard_map/psum | solution.py:83
  259.7 0.0 copy-start.1
  259.7 2.0 broadcast_multiply_fusion.2
  261.7 0.3 copy-done.1
  262.1 0.2 broadcast_multiply_fusion.1
  262.3 0.0 copy-start
  262.3 0.0 collective-permute-done.4
  262.3 1.4 fusion.36
  263.7 0.1 dynamic-slice_bitcast_fusion.1
  263.8 0.0 collective-permute-done.1
  263.9 1.4 fusion.31
  265.3 0.1 dynamic-slice_bitcast_fusion.2
  265.4 0.0 copy-done
  265.4 0.2 broadcast_multiply_fusion
  265.6 0.0 collective-permute-done.7
  265.6 1.4 fusion.41
  267.0 0.1 dynamic-slice_bitcast_fusion
  267.2 7.3 %collective-permute-start.9 = (f32[64,256]{0,1:T(8,128)S(1)}, f32[64,256]{0,1:T(8,128)S(1)}, u32[]{:S(2)}, u32[]{:S(2)}) collective-permute-start(f32[64,256]{0,1:T(8,128)S(1)} %dynamic-slice_bitcast_fusion.2), channel_id=1, source_target_pairs={{4,0},{8,4},{12,8},{16,12},{20,16},{24,20},{28,24},{32,28},{36,32}... | collective-permute-start | bytes 196616 | tf_op jit(solution)/shard_map/ppermute | solution.py:14
  274.5 2.6 collective-permute-start.10
  277.1 1.7 collective-permute-start.11
  278.8 0.7 pad_maximum_fusion.1
  279.5 5.7 %collective-permute-done.9 = f32[64,256]{0,1:T(8,128)S(1)} collective-permute-done((f32[64,256]{0,1:T(8,128)S(1)}, f32[64,256]{0,1:T(8,128)S(1)}, u32[]{:S(2)}, u32[]{:S(2)}) %collective-permute-start.9) | collective-permute-done | bytes 65568 | tf_op jit(solution)/shard_map/ppermute | solution.py:14
  285.1 0.0 collective-permute-done.10
  285.1 1.7 collective-permute-done.11
  286.8 0.8 copy.4
  (7 shorter events, 0.1 us)
Async XLA Ops:
  7.2 252.5 %all-reduce.3.cloned.1.call-start = ((), (), s32[]{:S(2)}) async-start(), calls=%async_computation | async-start | bytes 14155776 | tf_op jit(solution)/shard_map/psum | solution.py:83
  18.1 36.8 %collective-permute-start.5 = (f32[3,300,256]{2,1,0:T(8,128)S(1)}, f32[3,300,256]{2,1,0:T(8,128)S(1)}, u32[]{:S(2)}, u32[]{:S(2)}) collective-permute-start(f32[3,300,256]{2,1,0:T(8,128)S(1)} %get-tuple-element.8), channel_id=1, source_target_pairs={{248,0},{252,4},{0,8},{4,12},{8,16},{12,20},{16,24},{20,28},{24,32... | collective-permute-start | bytes 2764808 | tf_op jit(solution)/shard_map/ppermute | solution.py:14
  23.4 68.3 %collective-permute-start.2 = (f32[3,300,256]{2,1,0:T(8,128)S(1)}, f32[3,300,256]{2,1,0:T(8,128)S(1)}, u32[]{:S(2)}, u32[]{:S(2)}) collective-permute-start(f32[3,300,256]{2,1,0:T(8,128)S(1)} %get-tuple-element.8), channel_id=1, source_target_pairs={{252,0},{0,4},{4,8},{8,12},{12,16},{16,20},{20,24},{24,28},{28,32}... | collective-permute-start | bytes 2764808 | tf_op jit(solution)/shard_map/ppermute | solution.py:14
  24.5 86.8 %collective-permute-start.8 = (f32[3,300,256]{2,1,0:T(8,128)S(1)}, f32[3,300,256]{2,1,0:T(8,128)S(1)}, u32[]{:S(2)}, u32[]{:S(2)}) collective-permute-start(f32[3,300,256]{2,1,0:T(8,128)S(1)} %get-tuple-element.8), channel_id=1, source_target_pairs={{244,0},{248,4},{252,8},{0,12},{4,16},{8,20},{12,24},{16,28},{20,3... | collective-permute-start | bytes 2764808 | tf_op jit(solution)/shard_map/ppermute | solution.py:14
  125.0 138.8 %collective-permute-start.1 = (f32[256]{0:T(256)S(1)}, f32[256]{0:T(256)S(1)}, u32[]{:S(2)}, u32[]{:S(2)}) collective-permute-start(f32[256]{0:T(256)S(1)} %broadcast_multiply_fusion.4), channel_id=1, source_target_pairs={{252,0},{0,4},{4,8},{8,12},{12,16},{16,20},{20,24},{24,28},{28,32}... | collective-permute-start | bytes 3080 | tf_op jit(solution)/shard_map/ppermute | solution.py:14
  125.1 137.2 %collective-permute-start.4 = (f32[256]{0:T(256)S(1)}, f32[256]{0:T(256)S(1)}, u32[]{:S(2)}, u32[]{:S(2)}) collective-permute-start(f32[256]{0:T(256)S(1)} %broadcast_multiply_fusion.4), channel_id=1, source_target_pairs={{248,0},{252,4},{0,8},{4,12},{8,16},{12,20},{16,24},{20,28},{24,32... | collective-permute-start | bytes 3080 | tf_op jit(solution)/shard_map/ppermute | solution.py:14
  125.9 10.9 %collective-permute-start = (f32[1]{0:T(128)}, f32[1]{0:T(128)}, u32[]{:S(2)}, u32[]{:S(2)}) collective-permute-start(f32[1]{0:T(128)} %convert_element_type.3), channel_id=1, source_target_pairs={{252,0},{0,4},{4,8},{8,12},{12,16},{16,20},{20,24},{24,28},{28,32}... | collective-permute-start | bytes 20 | tf_op jit(solution)/shard_map/ppermute | solution.py:14
  129.3 10.6 %collective-permute-start.3 = (f32[1]{0:T(128)}, f32[1]{0:T(128)}, u32[]{:S(2)}, u32[]{:S(2)}) collective-permute-start(f32[1]{0:T(128)} %convert_element_type.3), channel_id=1, source_target_pairs={{248,0},{252,4},{0,8},{4,12},{8,16},{12,20},{16,24},{20,28},{24,32... | collective-permute-start | bytes 20 | tf_op jit(solution)/shard_map/ppermute | solution.py:14
  133.9 131.7 %collective-permute-start.7 = (f32[256]{0:T(256)S(1)}, f32[256]{0:T(256)S(1)}, u32[]{:S(2)}, u32[]{:S(2)}) collective-permute-start(f32[256]{0:T(256)S(1)} %broadcast_multiply_fusion.4), channel_id=1, source_target_pairs={{244,0},{248,4},{252,8},{0,12},{4,16},{8,20},{12,24},{16,28},{20,3... | collective-permute-start | bytes 3080 | tf_op jit(solution)/shard_map/ppermute | solution.py:14
  136.7 7.7 %collective-permute-start.6 = (f32[1]{0:T(128)}, f32[1]{0:T(128)}, u32[]{:S(2)}, u32[]{:S(2)}) collective-permute-start(f32[1]{0:T(128)} %convert_element_type.3), channel_id=1, source_target_pairs={{244,0},{248,4},{252,8},{0,12},{4,16},{8,20},{12,24},{16,28},{20,3... | collective-permute-start | bytes 20 | tf_op jit(solution)/shard_map/ppermute | solution.py:14
  259.7 2.4 copy-start.1
  262.3 3.1 %copy-start = (f32[3,256,3,256]{3,1,2,0:T(8,128)S(1)}, f32[3,256,3,256]{3,1,2,0:T(8,128)}, u32[]{:S(2)}) copy-start(f32[3,256,3,256]{3,1,2,0:T(8,128)} %get-tuple-element.4) | copy-start | bytes 7077892
  267.2 17.9 %collective-permute-start.9 = (f32[64,256]{0,1:T(8,128)S(1)}, f32[64,256]{0,1:T(8,128)S(1)}, u32[]{:S(2)}, u32[]{:S(2)}) collective-permute-start(f32[64,256]{0,1:T(8,128)S(1)} %dynamic-slice_bitcast_fusion.2), channel_id=1, source_target_pairs={{4,0},{8,4},{12,8},{16,12},{20,16},{24,20},{28,24},{32,28},{36,32}... | collective-permute-start | bytes 196616 | tf_op jit(solution)/shard_map/ppermute | solution.py:14
  274.5 10.6 %collective-permute-start.10 = (f32[64,256]{0,1:T(8,128)S(1)}, f32[64,256]{0,1:T(8,128)S(1)}, u32[]{:S(2)}, u32[]{:S(2)}) collective-permute-start(f32[64,256]{0,1:T(8,128)S(1)} %dynamic-slice_bitcast_fusion.1), channel_id=1, source_target_pairs={{8,0},{12,4},{16,8},{20,12},{24,16},{28,20},{32,24},{36,28},{40,32... | collective-permute-start | bytes 196616 | tf_op jit(solution)/shard_map/ppermute | solution.py:14
  277.1 9.7 %collective-permute-start.11 = (f32[64,256]{0,1:T(8,128)S(1)}, f32[64,256]{0,1:T(8,128)S(1)}, u32[]{:S(2)}, u32[]{:S(2)}) collective-permute-start(f32[64,256]{0,1:T(8,128)S(1)} %dynamic-slice_bitcast_fusion), channel_id=1, source_target_pairs={{12,0},{16,4},{20,8},{24,12},{28,16},{32,20},{36,24},{40,28},{44,3... | collective-permute-start | bytes 196616 | tf_op jit(solution)/shard_map/ppermute | solution.py:14
Sparse Core Ops, SparseCore 0:
  117.2 142.4 all-reduce.2
where the time goes:
time: 296 us; the launch traced here: 294 us
  waiting for transfers between devices  199 us (67%)
  starting transfers between devices  34.4 us (12%)
  matrix products  16.4 us (6%)
  blocking collectives  16.2 us (5%)
  between operations  14.8 us (5%)
  other arithmetic  12 us (4%)
    psum x1, waiting for transfers between devices, shards(): covariance = lax.psum(partial_value, 'rep') / NATOM  115 us
    ppermute x12, waiting for transfers between devices, from_behind(): return lax.ppermute(block, axis, route)  84.5 us
    ppermute x12, starting transfers between devices, from_behind(): return lax.ppermute(block, axis, route)  34.3 us
    dot_general x3, matrix products, shards(): lax.dot_general(centered, partner_coords, (((1,), (1,)), ((), ())), preci...  16.4 us
    psum x1, blocking collectives, shards(): atom_sums = lax.psum(jnp.sum(coords, axis=1), 'rep')  8.26 us
    psum x1, blocking collectives, shards(): self_sq = lax.psum(jnp.sum(centered * centered, axis=(0, 1)), 'rep') / NATOM  7.95 us
  transfers between devices with their start and end apart: 13, of which 8 were waited for; matrix products, arithmetic and copies ran while one was open for 6% of the time, Pallas kernels for 0%

commit v1 on v0

v1 whole, which is shorter than its diff:
```python
import functools

import jax
import jax.numpy as jnp
from jax import lax
from jax.experimental import pallas as pl
from jax.experimental.pallas import tpu as pltpu
from jax.sharding import PartitionSpec as P

NATOM = 1200
NEWTON = 4
PIECE = 320
DEPTH = 4 * PIECE
VMEM_LIMIT = 50 * 1024 * 1024


def route(array, target):
    blocks, reps = lax.axis_size("blk"), lax.axis_size("rep")
    pairs = []
    for block in range(blocks):
        for rep in range(reps):
            to_block, to_rep = target(block, rep)
            pairs.append((block * reps + rep, (to_block % blocks) * reps + to_rep))
    return lax.ppermute(array, ("blk", "rep"), pairs)


def other_core(block, rep):
    return block, rep ^ 1


def other_chip(block, rep):
    return block, rep ^ 2


def to_neighbour(block, rep):
    return (block - 1, rep + 2) if rep < 2 else (block - 3, rep - 2)


def onward(block, rep):
    return (block + 1, rep) if rep < 2 else (block - 1, rep)


def pair_minor(upper, lower, left, right):
    return upper[left] * lower[right] - upper[right] * lower[left]


def deviation(m, total):
    keyed = [
        [m[0][0] + m[1][1] + m[2][2], m[1][2] - m[2][1], m[2][0] - m[0][2], m[0][1] - m[1][0]],
        [m[1][2] - m[2][1], m[0][0] - m[1][1] - m[2][2], m[0][1] + m[1][0], m[2][0] + m[0][2]],
        [m[2][0] - m[0][2], m[0][1] + m[1][0], -m[0][0] + m[1][1] - m[2][2], m[1][2] + m[2][1]],
        [m[0][1] - m[1][0], m[2][0] + m[0][2], m[1][2] + m[2][1], -m[0][0] - m[1][1] + m[2][2]],
    ]
    top_one, top_two, low_one, low_two = keyed
    det_key = (
        pair_minor(top_one, top_two, 0, 1) * pair_minor(low_one, low_two, 2, 3)
        - pair_minor(top_one, top_two, 0, 2) * pair_minor(low_one, low_two, 1, 3)
        + pair_minor(top_one, top_two, 0, 3) * pair_minor(low_one, low_two, 1, 2)
        + pair_minor(top_one, top_two, 1, 2) * pair_minor(low_one, low_two, 0, 3)
        - pair_minor(top_one, top_two, 1, 3) * pair_minor(low_one, low_two, 0, 2)
        + pair_minor(top_one, top_two, 2, 3) * pair_minor(low_one, low_two, 0, 1)
    )
    det_three = (
        m[0][0] * (m[1][1] * m[2][2] - m[1][2] * m[2][1])
        - m[0][1] * (m[1][0] * m[2][2] - m[1][2] * m[2][0])
        + m[0][2] * (m[1][0] * m[2][1] - m[1][1] * m[2][0])
    )
    square_sum = m[0][0] * m[0][0]
    for first in range(3):
        for second in range(3):
            if first + second > 0:
                square_sum = square_sum + m[first][second] * m[first][second]
    second_coef = -2.0 * square_sum
    first_coef = -8.0 * det_three
    largest = 0.5 * total
    for _ in range(NEWTON):
        squared = largest * largest
        polynomial = squared * squared + second_coef * squared + first_coef * largest + det_key
        derivative = 4.0 * squared * largest + 2.0 * second_coef * largest + first_coef
        largest = largest - polynomial / derivative
    return total - 2.0 * largest


def padded(value):
    return jnp.concatenate([value, jnp.zeros((PIECE - value.shape[0], value.shape[1]), value.dtype)], 0)


def halves(value):
    high = value.astype(jnp.bfloat16)
    return high, (value - high.astype(jnp.float32)).astype(jnp.bfloat16)


def prepare_kernel(a_ref, b_ref, c_ref, d_ref, high_ref, low_ref, square_ref):
    frames = a_ref.shape[2]
    square = jnp.zeros((1, frames), jnp.float32)
    for comp in range(3):
        pieces = [ref[comp] for ref in (a_ref, b_ref, c_ref, d_ref)]
        centroid = sum(jnp.sum(piece, axis=0, keepdims=True) for piece in pieces) / NATOM
        for place, piece in enumerate(pieces):
            centered = piece - centroid
            square = square + jnp.sum(centered * centered, axis=0, keepdims=True)
            high, low = halves(padded(centered))
            high_ref[place * PIECE:(place + 1) * PIECE, comp * frames:(comp + 1) * frames] = high
            low_ref[place * PIECE:(place + 1) * PIECE, comp * frames:(comp + 1) * frames] = low
    square_ref[...] = jnp.broadcast_to(square / NATOM, square_ref.shape)


def covariance(refs, lane, row, rows, high_ref, low_ref, turned, left_high, left_low, acc, other_sq):
    square = jnp.zeros((turned.shape[0], 1), jnp.float32)
    for comp in range(3):
        pieces = [ref[comp, :, pl.ds(lane, 128)] for ref in refs]
        centroid = sum(jnp.sum(piece, axis=0, keepdims=True) for piece in pieces) / NATOM
        stacked = jnp.concatenate([padded(piece - centroid) for piece in pieces], 0)
        turned[...] = stacked.T
        used = turned[pl.ds(row, rows), :]
        square = jnp.sum(used * used, axis=1, keepdims=True) + (square if comp else 0.0)
        high, low = halves(used)
        left_high[comp * rows:(comp + 1) * rows, :] = high
        left_low[comp * rows:(comp + 1) * rows, :] = low
    dot = functools.partial(jnp.dot, preferred_element_type=jnp.float32)
    acc[...] = (
        dot(left_high[...], high_ref[...])
        + dot(left_high[...], low_ref[...])
        + dot(left_low[...], high_ref[...])
    )
    other_sq[...] = jnp.broadcast_to(square / NATOM, other_sq.shape)


def fill_tile(acc, rows, first_row, other_count, own_count, own_sq, other_sq, tile):
    frames = own_sq.shape[1]
    own_valid = lax.broadcasted_iota(jnp.int32, (8, frames), 1) < own_count
    place = lax.broadcasted_iota(jnp.int32, (8, frames), 0)
    for at in range(0, rows, 8):
        m = [
            [acc[i * rows + at:i * rows + at + 8, j * frames:(j + 1) * frames] * (1.0 / NATOM) for j in range(3)]
            for i in range(3)
        ]
        total = own_sq[...] + other_sq[at:at + 8, 0:1]
        valid = own_valid & (place + (first_row + at) < other_count)
        tile[at:at + 8, :] = jnp.where(valid, deviation(m, total), 0.0)


def near_kernel(info, high_ref, low_ref, own_sq, a, b, c, d, out_a, out_b, tile, turned, left_high, left_low, acc, other_sq):
    low_place, core, own_count, count = info[0], info[1], info[2], info[3]
    lane = pl.multiple_of(core * 128, 128)
    covariance((a, b, c, d), lane, 0, 128, high_ref, low_ref, turned, left_high, left_low, acc, other_sq)
    fill_tile(acc, 128, core * 128, count, own_count, own_sq, other_sq, tile)
    out_a[...] = tile[pl.ds(pl.multiple_of((1 - low_place) * 64, 64), 64), :]
    out_b[...] = tile[pl.ds(pl.multiple_of(low_place * 64, 64), 64), :]


def far_kernel(info, high_ref, low_ref, own_sq, a, b, c, d, near, tile, parts, turned, left_high, left_low, acc, other_sq):
    low_place, core, own_count, count = info[0], info[1], info[2], info[4]
    row = pl.multiple_of(core * 64, 64)
    covariance((a, b, c, d), 0, row, 64, high_ref, low_ref, turned, left_high, left_low, acc, other_sq)
    fill_tile(acc, 64, low_place * 128 + core * 64, count, own_count, own_sq, other_sq, tile)
    parts[:, :, 0:128] = near[...].T.reshape(4, 64, 128)
    parts[:, :, 128:192] = tile[...].T.reshape(4, 64, 64)
    parts[:, :, 192:256] = jnp.zeros((4, 64, 64), jnp.float32)


def finish_kernel(info, got_a, got_b, got_far, parts, behind, ahead):
    odd = info[1] == 1
    one, two = got_a[...], got_b[...]
    behind[0] = jnp.where(odd, two, one)
    behind[1] = got_far[...]
    behind[2] = jnp.where(odd, one, two)
    ahead[0] = jnp.concatenate([parts[2, :, 0:128], parts[3, :, 0:128]], 1)
    ahead[1] = jnp.concatenate([parts[i, :, 128:192] for i in range(4)], 1)
    ahead[2] = jnp.concatenate([parts[0, :, 0:128], parts[1, :, 0:128]], 1)


def call(kernel, out_shapes, scratch=()):
    def run(*args):
        whole = pl.BlockSpec(memory_space=pltpu.VMEM)
        specs = [pl.BlockSpec(memory_space=pltpu.SMEM) if arg.dtype == jnp.int32 else whole for arg in args]
        return pl.pallas_call(
            kernel,
            out_shape=out_shapes,
            in_specs=specs,
            out_specs=jax.tree.map(lambda _: whole, out_shapes),
            scratch_shapes=list(scratch),
            compiler_params=pltpu.CompilerParams(vmem_limit_bytes=VMEM_LIMIT),
        )(*args)

    return run


def f32(*shape):
    return jax.ShapeDtypeStruct(shape, jnp.float32)


def scratch_of(used, frames):
    return (
        pltpu.VMEM((128, DEPTH), jnp.float32),
        pltpu.VMEM((3 * used, DEPTH), jnp.bfloat16),
        pltpu.VMEM((3 * used, DEPTH), jnp.bfloat16),
        pltpu.VMEM((3 * used, 3 * frames), jnp.float32),
        pltpu.VMEM((used, 128), jnp.float32),
    )


def shards(coords, frame_count):
    frames = coords.shape[2]
    rep = lax.axis_index("rep")
    low_place, core = rep // 2, rep % 2
    near_count = route(frame_count, to_neighbour)
    far_count = route(frame_count, lambda block, rep: (block - 2, rep))

    own_chip = route(coords, other_chip)
    near_a = route(coords, to_neighbour)
    own_core = route(coords, other_core)
    near_b = route(own_chip, to_neighbour)
    far_a = route(lax.dynamic_slice_in_dim(near_a, low_place * 128, 128, 2), onward)
    own_both = route(own_chip, other_core)
    near_a_core = route(near_a, other_core)
    far_b = route(lax.dynamic_slice_in_dim(near_b, low_place * 128, 128, 2), onward)
    near_b_core = route(near_b, other_core)
    far_a_core = route(far_a, other_core)
    far_b_core = route(far_b, other_core)

    info = jnp.concatenate([low_place[None], core[None], frame_count, near_count, far_count]).astype(jnp.int32)
    wide = jax.ShapeDtypeStruct((DEPTH, 3 * frames), jnp.bfloat16)
    high, low, own_sq = call(prepare_kernel, (wide, wide, f32(8, frames)))(coords, own_chip, own_core, own_both)
    near_out_a, near_out_b, near_tile = call(
        near_kernel, (f32(64, frames), f32(64, frames), f32(128, frames)), scratch_of(128, frames)
    )(info, high, low, own_sq, near_b, near_a, near_b_core, near_a_core)
    got_a = route(near_out_a, lambda b, r: (b + 1, 2 * (r % 2)) if r >= 2 else (b + 3, 2 * (r % 2) + 1))
    got_b = route(near_out_b, lambda b, r: (b + 1, 2 * (r % 2) + 1) if r >= 2 else (b + 3, 2 * (r % 2)))
    far_tile, parts = call(far_kernel, (f32(64, frames), f32(4, 64, frames)), scratch_of(64, frames))(
        info, high, low, own_sq, far_b, far_a, far_b_core, far_a_core, near_tile
    )
    got_far = route(far_tile, lambda block, rep: (block + 2, 2 * (rep // 2) + rep % 2))
    parts = lax.all_to_all(parts, "rep", 0, 0)
    return call(finish_kernel, (f32(3, 64, frames), f32(3, 64, frames)))(info, got_a, got_b, got_far, parts)


def solution(mesh):
    in_specs = (P(None, "rep", "blk"), P("blk"))
    out_specs = (P(None, ("blk", "rep"), None), P(None, ("blk", "rep"), None))
    return jax.shard_map(shards, mesh=mesh, in_specs=in_specs, out_specs=out_specs, check_vma=False)
```

time: 296 us -> 134 us (0.45)
  waiting for transfers between devices: 199 us -> 64.5 us
  Pallas kernels: 0 us -> 17.8 us
  matrix products: 16.4 us -> 0 us
  blocking collectives: 16.2 us -> 0 us
  between operations: 14.8 us -> 1.37 us
  other arithmetic: 12 us -> 0 us
  starting transfers between devices: 34.4 us -> 45 us
    psum x1 -> x0, waiting for transfers between devices: 115 us -> none  [shards(): covariance = lax.psum(partial_value, 'rep') / NATOM]
    ppermute x12 -> x16, waiting for transfers between devices: 84.5 us -> 64.5 us  [route(): return lax.ppermute(array, ('blk', 'rep'), pairs)]
    pallas_call x0 -> x4, Pallas kernels: none -> 17.8 us  [run(): pl.pallas_call(kernel, out_shape=out_shapes, in_specs=specs, out_specs=ja...]
    dot_general x3 -> x0, matrix products: 16.4 us -> none  [shards(): lax.dot_general(centered, partner_coords, (((1,), (1,)), ((), ())), preci...]
    psum x2 -> x0, blocking collectives: 16.2 us -> none  [the longest x1 8.26 us: shards(): atom_sums = lax.psum(jnp.sum(coords, axis=1), 'rep')]
    ppermute x12 -> x16, starting transfers between devices: 34.3 us -> 41.6 us  [route(): return lax.ppermute(array, ('blk', 'rep'), pairs)]
    select_n x3 -> x0, other arithmetic: 4.23 us -> none  [shards(): jnp.where(mask, deviation(covariance, self_sq, partner_sq), 0.0)]
    all_to_all x0 -> x1, starting transfers between devices: none -> 3.39 us  [shards(): parts = lax.all_to_all(parts, 'rep', 0, 0)]
  transfers between devices with their start and end apart: 13 -> 17, of which waited for: 8 -> 7; matrix products, arithmetic and copies ran while one was open for 6% -> 1% of each run, Pallas kernels for 0% -> 8%
where the time goes in v1:
time: 134 us; the launch traced here: 131 us
  waiting for transfers between devices  64.5 us (48%)
  starting transfers between devices  45 us (34%)
  Pallas kernels  17.8 us (13%)
  local copies, waits for them, and re-layouts  2.58 us (2%)
  between operations  1.37 us (1%)
    ppermute x16, waiting for transfers between devices, route(): return lax.ppermute(array, ('blk', 'rep'), pairs)  64.5 us
    ppermute x16, starting transfers between devices, route(): return lax.ppermute(array, ('blk', 'rep'), pairs)  41.6 us
    pallas_call x4, Pallas kernels, run(): pl.pallas_call(kernel, out_shape=out_shapes, in_specs=specs, out_specs=ja...  17.8 us
    all_to_all x1, starting transfers between devices, shards(): parts = lax.all_to_all(parts, 'rep', 0, 0)  3.39 us
  transfers between devices with their start and end apart: 17, of which 7 were waited for; matrix products, arithmetic and copies ran while one was open for 1% of the time, Pallas kernels for 8%

profile of v1, /device:TPU:1, one launch (start us, length us, event | category | flops | bytes accessed | tf_op | source)
XLA Modules:
  0.0 131.3 jit_solution(2098561261415969956)
XLA Ops:
  0.6 2.6 %collective-permute-start.2 = (f32[3,300,256]{2,1,0:T(8,128)}, f32[3,300,256]{2,1,0:T(8,128)}, u32[]{:S(2)}, u32[]{:S(2)}) collective-permute-start(f32[3,300,256]{2,1,0:T(8,128)} %a_ref.1), channel_id=1, source_target_pairs={{0,2},{1,3},{2,0},{3,1},{4,6},{5,7},{6,4},{7,5},{8,10},{9,11},{10,... | collective-permute-start | bytes 2764808 | tf_op jit(solution)/shard_map/ppermute | solution.py:24
  3.2 9.3 %collective-permute-start.6 = (f32[3,300,256]{2,1,0:T(8,128)}, f32[3,300,256]{2,1,0:T(8,128)S(1)}, u32[]{:S(2)}, u32[]{:S(2)}) collective-permute-start(f32[3,300,256]{2,1,0:T(8,128)} %a_ref.1), channel_id=1, source_target_pairs={{0,254},{1,255},{2,244},{3,245},{4,2},{5,3},{6,248},{7,249},{8,6},... | collective-permute-start | bytes 2764808 | tf_op jit(solution)/shard_map/ppermute | solution.py:24
  12.5 10.4 %collective-permute-done.2.b_ref = f32[3,300,256]{2,1,0:T(8,128)} collective-permute-done((f32[3,300,256]{2,1,0:T(8,128)}, f32[3,300,256]{2,1,0:T(8,128)}, u32[]{:S(2)}, u32[]{:S(2)}) %collective-permute-start.2) | collective-permute-done | bytes 921632 | tf_op jit(solution)/shard_map/ppermute | solution.py:24
  22.9 10.8 %collective-permute-start.5 = (f32[3,300,256]{2,1,0:T(8,128)}, f32[3,300,256]{2,1,0:T(8,128)S(1)}, u32[]{:S(2)}, u32[]{:S(2)}) collective-permute-start(f32[3,300,256]{2,1,0:T(8,128)} %collective-permute-done.2.b_ref), channel_id=1, source_target_pairs={{0,254},{1,255},{2,244},{3,245},{4,2},{5,3},{6,248},{7,249},{8,6},... | collective-permute-start | bytes 2764808 | tf_op jit(solution)/shard_map/ppermute | solution.py:24
  33.7 1.8 %collective-permute-start.3 = (f32[3,300,256]{2,1,0:T(8,128)}, f32[3,300,256]{2,1,0:T(8,128)}, u32[]{:S(2)}, u32[]{:S(2)}) collective-permute-start(f32[3,300,256]{2,1,0:T(8,128)} %a_ref.1), channel_id=1, source_target_pairs={{0,1},{1,0},{2,3},{3,2},{4,5},{5,4},{6,7},{7,6},{8,9},{9,8},{10,11... | collective-permute-start | bytes 2764808 | tf_op jit(solution)/shard_map/ppermute | solution.py:24
  35.5 0.0 collective-permute-start
  35.5 0.0 collective-permute-start.4
  35.5 0.0 collective-permute-done.6.b
  35.5 0.5 collective-permute-start.8
  36.0 16.4 %collective-permute-done.5.a = f32[3,300,256]{2,1,0:T(8,128)S(1)} collective-permute-done((f32[3,300,256]{2,1,0:T(8,128)}, f32[3,300,256]{2,1,0:T(8,128)S(1)}, u32[]{:S(2)}, u32[]{:S(2)}) %collective-permute-start.5) | collective-permute-done | bytes 921632 | tf_op jit(solution)/shard_map/ppermute | solution.py:24
  52.4 2.5 %collective-permute-start.7 = (f32[3,300,256]{2,1,0:T(8,128)S(1)}, f32[3,300,256]{2,1,0:T(8,128)}, u32[]{:S(2)}, u32[]{:S(2)}) collective-permute-start(f32[3,300,256]{2,1,0:T(8,128)S(1)} %collective-permute-done.5.a), channel_id=1, source_target_pairs={{0,1},{1,0},{2,3},{3,2},{4,5},{5,4},{6,7},{7,6},{8,9},{9,8},{10,11... | collective-permute-start | bytes 2764808 | tf_op jit(solution)/shard_map/ppermute | solution.py:24
  54.9 0.0 collective-permute-done
  54.9 8.9 %collective-permute-start.1 = (s32[1]{0:T(128)}, s32[1]{0:T(128)}, u32[]{:S(2)}, u32[]{:S(2)}) collective-permute-start(s32[1]{0:T(128)} %param.3), channel_id=1, source_target_pairs={{0,248},{1,249},{2,250},{3,251},{4,252},{5,253},{6,254},{7,255},{8... | collective-permute-start | bytes 20 | tf_op jit(solution)/shard_map/ppermute | solution.py:24
  63.9 0.9 collective-permute-done.1
  64.7 0.0 collective-permute-start.12
  64.7 0.0 collective-permute-done.3.c_ref
  64.7 0.0 collective-permute-start.11
  64.7 17.7 %collective-permute-done.12.b = f32[3,300,128]{2,1,0:T(8,128)S(1)} collective-permute-done((f32[3,300,128]{2,1,0:T(8,128)S(1)}, f32[3,300,128]{2,1,0:T(8,128)S(1)}, u32[]{:S(2)}, u32[]{:S(2)}) %collective-permute-start.12) | collective-permute-done | bytes 460832 | tf_op jit(solution)/shard_map/ppermute | solution.py:24
  82.4 3.2 %collective-permute-start.14 = (f32[3,300,128]{2,1,0:T(8,128)S(1)}, f32[3,300,128]{2,1,0:T(8,128)}, u32[]{:S(2)}, u32[]{:S(2)}) collective-permute-start(f32[3,300,128]{2,1,0:T(8,128)S(1)} %collective-permute-done.12.b), channel_id=1, source_target_pairs={{0,1},{1,0},{2,3},{3,2},{4,5},{5,4},{6,7},{7,6},{8,9},{9,8},{10,11... | collective-permute-start | bytes 1382408 | tf_op jit(solution)/shard_map/ppermute | solution.py:24
  85.6 6.9 %collective-permute-done.11.a = f32[3,300,128]{2,1,0:T(8,128)} collective-permute-done((f32[3,300,128]{2,1,0:T(8,128)S(1)}, f32[3,300,128]{2,1,0:T(8,128)}, u32[]{:S(2)}, u32[]{:S(2)}) %collective-permute-start.11) | collective-permute-done | bytes 460832 | tf_op jit(solution)/shard_map/ppermute | solution.py:24
  92.5 1.8 %collective-permute-start.13 = (f32[3,300,128]{2,1,0:T(8,128)}, f32[3,300,128]{2,1,0:T(8,128)}, u32[]{:S(2)}, u32[]{:S(2)}) collective-permute-start(f32[3,300,128]{2,1,0:T(8,128)} %collective-permute-done.11.a), channel_id=1, source_target_pairs={{0,1},{1,0},{2,3},{3,2},{4,5},{5,4},{6,7},{7,6},{8,9},{9,8},{10,11... | collective-permute-start | bytes 1382408 | tf_op jit(solution)/shard_map/ppermute | solution.py:24
  94.9 1.3 %concatenate.3.info = s32[5]{0:T(128)S(1)} concatenate(s32[1]{0:T(128)} %bitcast, s32[1]{0:T(128)} %bitcast.1, s32[1]{0:T(128)S(6)} %copy.4, s32[1]{0:T(128)} %collective-permute-done, s32[1]{0:T(128)} %collective-permute-done.1), dimensions={0} | concatenate | bytes 40 | tf_op jit(solution)/shard_map/concatenate | solution.py:222
  96.3 0.0 collective-permute-done.4.d_ref
  96.3 0.0 copy-start
  96.3 1.2 copy-done
  97.5 4.7 %shard_map.41 = (bf16[1280,768]{1,0:T(8,128)(2,1)}, bf16[1280,768]{1,0:T(8,128)(2,1)}, f32[8,256]{1,0:T(8,128)S(1)}) custom-call(f32[3,300,256]{2,1,0:T(8,128)S(1)} %copy-done, f32[3,300,256]{2,1,0:T(8,128)} %collective-permute-done.2.b_ref, f32[3,300,256]{2,1,0:T(8,128)} %collective-permute-done.3.c_ref, f32[3,300,256]{2,1,0:T(8,128)} %collective-permute-done.4.d_ref), custom_call_target="tpu_custom_call" | custom-call | tf_op jit(solution)/shard_map/pallas_call | solution.py:177
  102.1 0.0 collective-permute-done.8.d
  102.1 0.0 collective-permute-done.7.c
  102.2 6.2 %shard_map.42 = (f32[64,256]{1,0:T(8,128)S(1)}, f32[64,256]{1,0:T(8,128)S(1)}, f32[128,256]{1,0:T(8,128)S(1)}) custom-call(s32[5]{0:T(128)S(1)} %concatenate.3.info, bf16[1280,768]{1,0:T(8,128)(2,1)} %get-tuple-element.10.high_ref, bf16[1280,768]{1,0:T(8,128)(2,1)} %get-tuple-element.11.low_ref, f32[8,256]{1,0:T(8,128)S(1)} %get-tuple-element.12.own_sq, ...), custom_call_target="tpu_custom_call" | custom-call | tf_op jit(solution)/shard_map/pallas_call | solution.py:177
  108.3 0.0 collective-permute-done.14.d
  108.3 0.0 collective-permute-done.13.c
  108.3 5.7 %shard_map.43 = (f32[64,256]{1,0:T(8,128)S(1)}, f32[4,64,256]{2,1,0:T(8,128)}) custom-call(s32[5]{0:T(128)S(1)} %concatenate.3.info, bf16[1280,768]{1,0:T(8,128)(2,1)} %get-tuple-element.10.high_ref, bf16[1280,768]{1,0:T(8,128)(2,1)} %get-tuple-element.11.low_ref, f32[8,256]{1,0:T(8,128)S(1)} %get-tuple-element.12.own_sq, ...), custom_call_target="tpu_custom_call" | custom-call | tf_op jit(solution)/shard_map/pallas_call | solution.py:177
  114.0 3.4 %all-to-all-start = ((f32[4,64,256]{2,1,0:T(8,128)}), f32[4,64,256]{2,1,0:T(8,128)S(1)}, u32[]{:S(2)}, u32[]{:S(2)}) async-start(f32[4,64,256]{2,1,0:T(8,128)} %get-tuple-element.17), calls=%async_computation | async-start | bytes 524288 | tf_op jit(solution)/shard_map/all_to_all | solution.py:234
  117.4 0.1 collective-permute-start.10
  117.5 0.1 collective-permute-start.9
  117.6 0.1 collective-permute-start.15
  117.7 11.4 %collective-permute-done.10.got_b = f32[64,256]{1,0:T(8,128)S(1)} collective-permute-done((f32[64,256]{1,0:T(8,128)S(1)}, f32[64,256]{1,0:T(8,128)S(1)}, u32[]{:S(2)}, u32[]{:S(2)}) %collective-permute-start.10) | collective-permute-done | bytes 65568 | tf_op jit(solution)/shard_map/ppermute | solution.py:24
  129.1 0.0 collective-permute-done.9.got_a
  129.1 0.9 collective-permute-done.15.got_far
  130.0 0.0 all-to-all-done.parts
  130.0 1.3 shard_map.44
  (2 shorter events, 0.1 us)
Async XLA Ops:
  0.6 22.2 %collective-permute-start.2 = (f32[3,300,256]{2,1,0:T(8,128)}, f32[3,300,256]{2,1,0:T(8,128)}, u32[]{:S(2)}, u32[]{:S(2)}) collective-permute-start(f32[3,300,256]{2,1,0:T(8,128)} %a_ref.1), channel_id=1, source_target_pairs={{0,2},{1,3},{2,0},{3,1},{4,6},{5,7},{6,4},{7,5},{8,10},{9,11},{10,... | collective-permute-start | bytes 2764808 | tf_op jit(solution)/shard_map/ppermute | solution.py:24
  3.2 32.3 %collective-permute-start.6 = (f32[3,300,256]{2,1,0:T(8,128)}, f32[3,300,256]{2,1,0:T(8,128)S(1)}, u32[]{:S(2)}, u32[]{:S(2)}) collective-permute-start(f32[3,300,256]{2,1,0:T(8,128)} %a_ref.1), channel_id=1, source_target_pairs={{0,254},{1,255},{2,244},{3,245},{4,2},{5,3},{6,248},{7,249},{8,6},... | collective-permute-start | bytes 2764808 | tf_op jit(solution)/shard_map/ppermute | solution.py:24
  22.9 29.5 %collective-permute-start.5 = (f32[3,300,256]{2,1,0:T(8,128)}, f32[3,300,256]{2,1,0:T(8,128)S(1)}, u32[]{:S(2)}, u32[]{:S(2)}) collective-permute-start(f32[3,300,256]{2,1,0:T(8,128)} %collective-permute-done.2.b_ref), channel_id=1, source_target_pairs={{0,254},{1,255},{2,244},{3,245},{4,2},{5,3},{6,248},{7,249},{8,6},... | collective-permute-start | bytes 2764808 | tf_op jit(solution)/shard_map/ppermute | solution.py:24
  33.7 31.1 %collective-permute-start.3 = (f32[3,300,256]{2,1,0:T(8,128)}, f32[3,300,256]{2,1,0:T(8,128)}, u32[]{:S(2)}, u32[]{:S(2)}) collective-permute-start(f32[3,300,256]{2,1,0:T(8,128)} %a_ref.1), channel_id=1, source_target_pairs={{0,1},{1,0},{2,3},{3,2},{4,5},{5,4},{6,7},{7,6},{8,9},{9,8},{10,11... | collective-permute-start | bytes 2764808 | tf_op jit(solution)/shard_map/ppermute | solution.py:24
  35.5 19.4 %collective-permute-start = (s32[1]{0:T(128)}, s32[1]{0:T(128)}, u32[]{:S(2)}, u32[]{:S(2)}) collective-permute-start(s32[1]{0:T(128)} %param.3), channel_id=1, source_target_pairs={{0,254},{1,255},{2,244},{3,245},{4,2},{5,3},{6,248},{7,249},{8,6},... | collective-permute-start | bytes 20 | tf_op jit(solution)/shard_map/ppermute | solution.py:24
  35.5 60.8 %collective-permute-start.4 = (f32[3,300,256]{2,1,0:T(8,128)}, f32[3,300,256]{2,1,0:T(8,128)}, u32[]{:S(2)}, u32[]{:S(2)}) collective-permute-start(f32[3,300,256]{2,1,0:T(8,128)} %collective-permute-done.2.b_ref), channel_id=1, source_target_pairs={{0,1},{1,0},{2,3},{3,2},{4,5},{5,4},{6,7},{7,6},{8,9},{9,8},{10,11... | collective-permute-start | bytes 2764808 | tf_op jit(solution)/shard_map/ppermute | solution.py:24
  35.5 66.6 %collective-permute-start.8 = (f32[3,300,256]{2,1,0:T(8,128)S(1)}, f32[3,300,256]{2,1,0:T(8,128)S(1)}, u32[]{:S(2)}, u32[]{:S(2)}) collective-permute-start(f32[3,300,256]{2,1,0:T(8,128)S(1)} %collective-permute-done.6.b), channel_id=1, source_target_pairs={{0,1},{1,0},{2,3},{3,2},{4,5},{5,4},{6,7},{7,6},{8,9},{9,8},{10,11... | collective-permute-start | bytes 2764808 | tf_op jit(solution)/shard_map/ppermute | solution.py:24
  52.4 49.7 %collective-permute-start.7 = (f32[3,300,256]{2,1,0:T(8,128)S(1)}, f32[3,300,256]{2,1,0:T(8,128)}, u32[]{:S(2)}, u32[]{:S(2)}) collective-permute-start(f32[3,300,256]{2,1,0:T(8,128)S(1)} %collective-permute-done.5.a), channel_id=1, source_target_pairs={{0,1},{1,0},{2,3},{3,2},{4,5},{5,4},{6,7},{7,6},{8,9},{9,8},{10,11... | collective-permute-start | bytes 2764808 | tf_op jit(solution)/shard_map/ppermute | solution.py:24
  54.9 9.8 %collective-permute-start.1 = (s32[1]{0:T(128)}, s32[1]{0:T(128)}, u32[]{:S(2)}, u32[]{:S(2)}) collective-permute-start(s32[1]{0:T(128)} %param.3), channel_id=1, source_target_pairs={{0,248},{1,249},{2,250},{3,251},{4,252},{5,253},{6,254},{7,255},{8... | collective-permute-start | bytes 20 | tf_op jit(solution)/shard_map/ppermute | solution.py:24
  64.7 17.7 %collective-permute-start.12 = (f32[3,300,128]{2,1,0:T(8,128)S(1)}, f32[3,300,128]{2,1,0:T(8,128)S(1)}, u32[]{:S(2)}, u32[]{:S(2)}) collective-permute-start(f32[3,300,128]{2,1,0:T(8,128)S(1)} %constant_dynamic-slice_fusion), channel_id=1, source_target_pairs={{0,4},{1,5},{2,254},{3,255},{4,8},{5,9},{6,2},{7,3},{8,12},{9,13},... | collective-permute-start | bytes 1382408 | tf_op jit(solution)/shard_map/ppermute | solution.py:24
  64.7 27.8 %collective-permute-start.11 = (f32[3,300,128]{2,1,0:T(8,128)S(1)}, f32[3,300,128]{2,1,0:T(8,128)}, u32[]{:S(2)}, u32[]{:S(2)}) collective-permute-start(f32[3,300,128]{2,1,0:T(8,128)S(1)} %constant_dynamic-slice_fusion.1), channel_id=1, source_target_pairs={{0,4},{1,5},{2,254},{3,255},{4,8},{5,9},{6,2},{7,3},{8,12},{9,13},... | collective-permute-start | bytes 1382408 | tf_op jit(solution)/shard_map/ppermute | solution.py:24
  82.4 25.9 %collective-permute-start.14 = (f32[3,300,128]{2,1,0:T(8,128)S(1)}, f32[3,300,128]{2,1,0:T(8,128)}, u32[]{:S(2)}, u32[]{:S(2)}) collective-permute-start(f32[3,300,128]{2,1,0:T(8,128)S(1)} %collective-permute-done.12.b), channel_id=1, source_target_pairs={{0,1},{1,0},{2,3},{3,2},{4,5},{5,4},{6,7},{7,6},{8,9},{9,8},{10,11... | collective-permute-start | bytes 1382408 | tf_op jit(solution)/shard_map/ppermute | solution.py:24
  92.5 15.8 %collective-permute-start.13 = (f32[3,300,128]{2,1,0:T(8,128)}, f32[3,300,128]{2,1,0:T(8,128)}, u32[]{:S(2)}, u32[]{:S(2)}) collective-permute-start(f32[3,300,128]{2,1,0:T(8,128)} %collective-permute-done.11.a), channel_id=1, source_target_pairs={{0,1},{1,0},{2,3},{3,2},{4,5},{5,4},{6,7},{7,6},{8,9},{9,8},{10,11... | collective-permute-start | bytes 1382408 | tf_op jit(solution)/shard_map/ppermute | solution.py:24
  96.3 1.2 copy-start
  114.0 16.0 %all-to-all-start = ((f32[4,64,256]{2,1,0:T(8,128)}), f32[4,64,256]{2,1,0:T(8,128)S(1)}, u32[]{:S(2)}, u32[]{:S(2)}) async-start(f32[4,64,256]{2,1,0:T(8,128)} %get-tuple-element.17), calls=%async_computation | async-start | bytes 524288 | tf_op jit(solution)/shard_map/all_to_all | solution.py:234
  117.4 11.7 %collective-permute-start.10 = (f32[64,256]{1,0:T(8,128)S(1)}, f32[64,256]{1,0:T(8,128)S(1)}, u32[]{:S(2)}, u32[]{:S(2)}) collective-permute-start(f32[64,256]{1,0:T(8,128)S(1)} %get-tuple-element.14), channel_id=1, source_target_pairs={{0,12},{1,14},{2,5},{3,7},{4,16},{5,18},{6,9},{7,11},{8,20},{9,22}... | collective-permute-start | bytes 196616 | tf_op jit(solution)/shard_map/ppermute | solution.py:24
  117.5 11.6 %collective-permute-start.9 = (f32[64,256]{1,0:T(8,128)S(1)}, f32[64,256]{1,0:T(8,128)S(1)}, u32[]{:S(2)}, u32[]{:S(2)}) collective-permute-start(f32[64,256]{1,0:T(8,128)S(1)} %get-tuple-element.13), channel_id=1, source_target_pairs={{0,13},{1,15},{2,4},{3,6},{4,17},{5,19},{6,8},{7,10},{8,21},{9,23}... | collective-permute-start | bytes 196616 | tf_op jit(solution)/shard_map/ppermute | solution.py:24
  117.6 12.4 %collective-permute-start.15 = (f32[64,256]{1,0:T(8,128)S(1)}, f32[64,256]{1,0:T(8,128)S(1)}, u32[]{:S(2)}, u32[]{:S(2)}) collective-permute-start(f32[64,256]{1,0:T(8,128)S(1)} %get-tuple-element.16), channel_id=1, source_target_pairs={{0,8},{1,9},{2,10},{3,11},{4,12},{5,13},{6,14},{7,15},{8,16},{9,17... | collective-permute-start | bytes 196616 | tf_op jit(solution)/shard_map/ppermute | solution.py:24

commit v2 on v1

v2 whole, which is shorter than its diff:
```python
import functools

import jax
import jax.numpy as jnp
from jax import lax
from jax.experimental import pallas as pl
from jax.experimental.pallas import tpu as pltpu
from jax.sharding import PartitionSpec as P

NATOM = 1200
NEWTON = 4
PIECE = 320
DEPTH = 4 * PIECE
VMEM_LIMIT = 12 * 1024 * 1024


def route(array, target):
    blocks, reps = lax.axis_size("blk"), lax.axis_size("rep")
    pairs = []
    for block in range(blocks):
        for rep in range(reps):
            to_block, to_rep = target(block, rep)
            pairs.append((block * reps + rep, (to_block % blocks) * reps + to_rep))
    return lax.ppermute(array, ("blk", "rep"), pairs)


def other_core(block, rep):
    return block, rep ^ 1


def other_chip(block, rep):
    return block, rep ^ 2


def to_neighbour(block, rep):
    return (block - 1, rep + 2) if rep < 2 else (block - 3, rep - 2)


def pair_minor(upper, lower, left, right):
    return upper[left] * lower[right] - upper[right] * lower[left]


def deviation(m, total):
    keyed = [
        [m[0][0] + m[1][1] + m[2][2], m[1][2] - m[2][1], m[2][0] - m[0][2], m[0][1] - m[1][0]],
        [m[1][2] - m[2][1], m[0][0] - m[1][1] - m[2][2], m[0][1] + m[1][0], m[2][0] + m[0][2]],
        [m[2][0] - m[0][2], m[0][1] + m[1][0], -m[0][0] + m[1][1] - m[2][2], m[1][2] + m[2][1]],
        [m[0][1] - m[1][0], m[2][0] + m[0][2], m[1][2] + m[2][1], -m[0][0] - m[1][1] + m[2][2]],
    ]
    top_one, top_two, low_one, low_two = keyed
    det_key = (
        pair_minor(top_one, top_two, 0, 1) * pair_minor(low_one, low_two, 2, 3)
        - pair_minor(top_one, top_two, 0, 2) * pair_minor(low_one, low_two, 1, 3)
        + pair_minor(top_one, top_two, 0, 3) * pair_minor(low_one, low_two, 1, 2)
        + pair_minor(top_one, top_two, 1, 2) * pair_minor(low_one, low_two, 0, 3)
        - pair_minor(top_one, top_two, 1, 3) * pair_minor(low_one, low_two, 0, 2)
        + pair_minor(top_one, top_two, 2, 3) * pair_minor(low_one, low_two, 0, 1)
    )
    det_three = (
        m[0][0] * (m[1][1] * m[2][2] - m[1][2] * m[2][1])
        - m[0][1] * (m[1][0] * m[2][2] - m[1][2] * m[2][0])
        + m[0][2] * (m[1][0] * m[2][1] - m[1][1] * m[2][0])
    )
    square_sum = m[0][0] * m[0][0]
    for first in range(3):
        for second in range(3):
            if first + second > 0:
                square_sum = square_sum + m[first][second] * m[first][second]
    second_coef = -2.0 * square_sum
    first_coef = -8.0 * det_three
    largest = 0.5 * total
    for _ in range(NEWTON):
        squared = largest * largest
        polynomial = squared * squared + second_coef * squared + first_coef * largest + det_key
        derivative = 4.0 * squared * largest + 2.0 * second_coef * largest + first_coef
        largest = largest - polynomial / derivative
    return total - 2.0 * largest


def padded(value):
    return jnp.concatenate([value, jnp.zeros((PIECE - value.shape[0], value.shape[1]), value.dtype)], 0)


def halves(value):
    high = value.astype(jnp.bfloat16)
    return high, (value - high.astype(jnp.float32)).astype(jnp.bfloat16)


def place_of():
    rep = lax.axis_index("rep")
    return rep // 2, rep % 2


def aligned(index, size):
    return pl.ds(pl.multiple_of(index * size, size), size)


def column_sums(pieces):
    return sum(jnp.sum(piece, axis=0, keepdims=True) for piece in pieces)


def products(left_high, left_low, right_high, right_low):
    dot = functools.partial(jnp.dot, preferred_element_type=jnp.float32)
    return dot(left_high, right_high) + dot(left_high, right_low) + dot(left_low, right_high)


def prepare_kernel(a_ref, b_ref, c_ref, d_ref, high_ref, low_ref, square_ref):
    frames = a_ref.shape[2]
    square = jnp.zeros((frames, 1), jnp.float32)
    for comp in range(3):
        pieces = [ref[comp] for ref in (a_ref, b_ref, c_ref, d_ref)]
        centroid = column_sums(pieces) / NATOM
        value = jnp.concatenate([padded(piece - centroid) for piece in pieces], 0).T
        square = square + jnp.sum(value * value, axis=1, keepdims=True)
        high, low = halves(value)
        high_ref[comp * frames:(comp + 1) * frames, :] = high
        low_ref[comp * frames:(comp + 1) * frames, :] = low
    square_ref[...] = jnp.broadcast_to(square / NATOM, square_ref.shape)


def fill_tile(covariance, rows, row_square, column_square, row_limit, column_limit, tile):
    step = 16
    column_valid = lax.broadcasted_iota(jnp.int32, (step, 128), 1) < column_limit
    for at in range(0, rows, step):
        place = lax.broadcasted_iota(jnp.int32, (step, 128), 0) + at
        total = row_square[at:at + step, :] + column_square
        tile[at:at + step, :] = jnp.where(
            (place < row_limit) & column_valid, deviation(covariance(at, at + step), total), 0.0
        )


def right_side(refs, lanes, about, right_high, right_low):
    total, square = [], jnp.zeros((1, 128), jnp.float32)
    for comp in range(3):
        moved = [ref[comp, :, lanes] - about[comp:comp + 1, :] for ref in refs]
        total.append(column_sums(moved))
        square = square + column_sums([value * value for value in moved])
        for place, value in enumerate(moved):
            top, rest = halves(padded(value))
            right_high[place * PIECE:(place + 1) * PIECE, comp * 128:(comp + 1) * 128] = top
            right_low[place * PIECE:(place + 1) * PIECE, comp * 128:(comp + 1) * 128] = rest
    return total, square


def half_facts(refs, out):
    square = 0.0
    for comp in range(3):
        pieces = [ref[comp] for ref in refs]
        mean = column_sums(pieces) / (NATOM / 2)
        square = square + column_sums([(piece - mean) * (piece - mean) for piece in pieces])
        out[comp:comp + 1, :] = mean
    out[3:4, :] = square
    out[4:8, :] = jnp.zeros((4, out.shape[1]), jnp.float32)


def near_first_kernel(high, low, a, b, acc, facts, right_high, right_low):
    half_facts((a, b), facts)
    lanes = aligned(place_of()[1], 128)
    right_side((a, b), lanes, facts[:, lanes], right_high, right_low)
    acc[...] = products(high[:, DEPTH // 2:], low[:, DEPTH // 2:], right_high[...], right_low[...])


def near_kernel(own_count, count, high, low, square, first, facts, a, b, out_a, out_b, parts, right_high, right_low, acc, tile, turned):
    low_place, core = place_of()
    lanes = aligned(core, 128)
    about = facts[:, lanes]
    total, column_square = right_side((a, b), lanes, about, right_high, right_low)
    column_square = (column_square + about[3:4, :]) / NATOM
    for comp in range(3):
        offset = total[comp] / NATOM
        column_square = column_square - offset * offset
    acc[...] = first[...] + products(high[:, :DEPTH // 2], low[:, :DEPTH // 2], right_high[...], right_low[...])
    frames = square.shape[0]

    def covariance(start, stop):
        return [
            [acc[i * frames + start:i * frames + stop, j * 128:(j + 1) * 128] * (1.0 / NATOM) for j in range(3)]
            for i in range(3)
        ]

    fill_tile(covariance, frames, square, column_square, own_count[0], count[0] - core * 128, tile)
    parts[...] = tile[...].reshape(parts.shape)
    turned[...] = tile[...].T
    out_a[...] = turned[aligned(1 - low_place, 64), :]
    out_b[...] = turned[aligned(low_place, 64), :]


def between_kernel(facts, near_a, near_b, else_a, else_b, mine, give, left_high, left_low, right_high, right_low, acc, here, known):
    low_place, core = place_of()
    half_facts((near_a, near_b), here)
    sign = jnp.where(low_place == 0, 1.0, -1.0)
    square = here[3:4, :] + facts[3:4, :]
    known[...] = jnp.zeros_like(known)
    for comp in range(3):
        apart = here[comp:comp + 1, :] - facts[comp:comp + 1, :]
        known[comp:comp + 1, :] = sign * apart
        square = square + (NATOM / 4) * apart * apart
    known[3:4, :] = square / NATOM
    upper = low_place == 1
    lanes = aligned(core, 128)
    for comp in range(3):
        pieces = [
            jnp.where(upper, one[comp, :, lanes], two[comp, :, lanes]) for one, two in ((near_a, else_a), (near_b, else_b))
        ]
        mean = column_sums(pieces) / (NATOM / 2)
        value = jnp.concatenate([padded(piece - mean) for piece in pieces], 0).T
        high, low = halves(value)
        left_high[comp * 128:(comp + 1) * 128, :] = high
        left_low[comp * 128:(comp + 1) * 128, :] = low
        pieces = [jnp.where(upper, two[comp], one[comp]) for one, two in ((near_a, else_a), (near_b, else_b))]
        mean = column_sums(pieces) / (NATOM / 2)
        for place, piece in enumerate(pieces):
            high, low = halves(padded(piece - mean))
            right_high[place * PIECE:(place + 1) * PIECE, comp * 256:(comp + 1) * 256] = high
            right_low[place * PIECE:(place + 1) * PIECE, comp * 256:(comp + 1) * 256] = low
    acc[...] = products(left_high[...], left_low[...], right_high[...], right_low[...])
    for i in range(3):
        for j in range(3):
            to = pl.ds((3 * i + j) * 128, 128)
            mine[to, :] = acc[i * 128:(i + 1) * 128, aligned(2 * j + low_place, 128)]
            give[to, :] = acc[i * 128:(i + 1) * 128, aligned(2 * j + 1 - low_place, 128)]
    mine[1152:1160, :] = known[:, aligned(jnp.where(upper, core, 0), 128)]
    give[1152:1160, :] = known[:, aligned(jnp.where(upper, core, 1), 128)]


def far_kernel(count_one, count_three, mine, got, ahead_a, ahead_b, behind_a, behind_b, tile, square):
    low_place, core = place_of()
    one, two = mine[1152:1160, :], got[1152:1160, :]
    row_facts = jnp.where(low_place == 1, one, two).T
    column_facts = jnp.where(low_place == 1, two, one)
    square[...] = jnp.broadcast_to(row_facts[:, 3:4], square.shape)

    def covariance(start, stop):
        return [
            [
                (mine[(3 * i + j) * 128 + start:(3 * i + j) * 128 + stop, :]
                 + got[(3 * i + j) * 128 + start:(3 * i + j) * 128 + stop, :]) * (1.0 / NATOM)
                + (0.25 * row_facts[start:stop, i:i + 1]) * column_facts[j:j + 1, :]
                for j in range(3)
            ]
            for i in range(3)
        ]

    fill_tile(
        covariance, 128, square, column_facts[3:4, :], count_one[0] - core * 128, count_three[0] - low_place * 128, tile
    )
    ahead_a[...] = tile[aligned(low_place, 64), :]
    ahead_b[...] = tile[aligned(1 - low_place, 64), :]
    tile[...] = tile[...].T
    behind_a[...] = tile[aligned(core, 64), :]
    behind_b[...] = tile[aligned(1 - core, 64), :]


def finish_kernel(got_a, got_b, parts, ahead_a, ahead_b, behind_a, behind_b, behind, ahead):
    core = place_of()[1]

    def ordered(one, two):
        return jnp.where(core == 1, two, one), jnp.where(core == 1, one, two)

    behind[0], behind[2] = ordered(got_a[...], got_b[...])
    behind[1] = jnp.concatenate(ordered(behind_a[...], behind_b[...]), 1)
    ahead[0] = jnp.concatenate([parts[2], parts[3]], 1)
    ahead[1] = jnp.concatenate(ordered(ahead_a[...], ahead_b[...]), 1)
    ahead[2] = jnp.concatenate([parts[0], parts[1]], 1)


def call(kernel, out_shapes, microseconds, scratch=()):
    def run(*args):
        whole = pl.BlockSpec(memory_space=pltpu.VMEM)
        specs = [pl.BlockSpec(memory_space=pltpu.SMEM) if arg.dtype == jnp.int32 else whole for arg in args]
        return pl.pallas_call(
            kernel,
            out_shape=out_shapes,
            in_specs=specs,
            out_specs=jax.tree.map(lambda _: whole, out_shapes),
            scratch_shapes=[pltpu.VMEM(shape, dtype) for shape, dtype in scratch],
            cost_estimate=pl.CostEstimate(flops=0, bytes_accessed=int(microseconds * 3.6e6), transcendentals=0),
            compiler_params=pltpu.CompilerParams(vmem_limit_bytes=VMEM_LIMIT),
        )(*args)

    return run


def f32(*shape):
    return jax.ShapeDtypeStruct(shape, jnp.float32)


def bf16(*shape):
    return jax.ShapeDtypeStruct(shape, jnp.bfloat16)


def shards(coords, frame_count):
    frames = coords.shape[2]
    together = lax.optimization_barrier
    small, wide = jnp.bfloat16, jnp.float32

    own_chip = route(coords, other_chip)
    near_a = route(coords, to_neighbour)
    own_core = route(coords, other_core)
    count_one = route(frame_count, lambda block, rep: (block - 1, rep))
    count_three = route(frame_count, lambda block, rep: (block - 3, rep))
    own_chip, near_a = together((own_chip, near_a))

    near_b = route(own_chip, to_neighbour)
    else_a = route(near_a, other_chip)
    own_both = route(own_chip, other_core)
    near_a_core = route(near_a, other_core)
    high, low, square = call(
        prepare_kernel, (bf16(768, DEPTH), bf16(768, DEPTH), f32(frames, 128)), 4.0
    )(coords, own_core, own_chip, own_both)
    sides = [((DEPTH // 2, 384), small), ((DEPTH // 2, 384), small)]
    near_first, facts = call(near_first_kernel, (f32(768, 384), f32(8, 256)), 4.0, sides)(high, low, near_a, near_a_core)
    near_b, else_a, near_first, facts, count_one, count_three = together(
        (near_b, else_a, near_first, facts, count_one, count_three)
    )

    near_b_core = route(near_b, other_core)
    else_a_core = route(else_a, other_core)
    mine, give = call(
        between_kernel,
        (f32(1160, 128), f32(1160, 128)),
        3.0,
        [((384, DEPTH // 2), small), ((384, DEPTH // 2), small), ((DEPTH // 2, 768), small), ((DEPTH // 2, 768), small),
         ((384, 768), wide), ((8, 256), wide), ((8, 256), wide)],
    )(facts, near_b, near_b_core, else_a, else_a_core)
    got = route(give, other_chip)
    near_first, mine = together((near_first, mine))
    near_count = jnp.where(lax.axis_index("rep") < 2, count_three, count_one)
    near_out_a, near_out_b, parts = call(
        near_kernel,
        (f32(64, frames), f32(64, frames), f32(4, 64, 128)),
        4.0,
        sides + [((768, 384), wide), ((frames, 128), wide), ((128, frames), wide)],
    )(frame_count, near_count, high, low, square, near_first, facts, near_b, near_b_core)
    got_a = route(near_out_a, lambda b, r: (b + 1, 2 * (r % 2)) if r >= 2 else (b + 3, 2 * (r % 2) + 1))
    got_b = route(near_out_b, lambda b, r: (b + 1, 2 * (r % 2) + 1) if r >= 2 else (b + 3, 2 * (r % 2)))
    parts = lax.all_to_all(parts, "rep", 0, 0)
    got, got_a, got_b, parts = together((got, got_a, got_b, parts))

    ahead_a, ahead_b, behind_a, behind_b = call(
        far_kernel,
        (f32(64, 128), f32(64, 128), f32(64, 128), f32(64, 128)),
        1.5,
        [((128, 128), wide), ((128, 128), wide)],
    )(count_one, count_three, mine, got)
    ahead_a = route(ahead_a, lambda block, rep: (block + 1, 2 * (rep % 2) + rep // 2))
    ahead_b = route(ahead_b, lambda block, rep: (block + 1, 2 * (rep % 2) + 1 - rep // 2))
    behind_a = route(behind_a, lambda block, rep: (block + 3, rep))
    behind_b = route(behind_b, lambda block, rep: (block + 3, rep ^ 1))
    return call(finish_kernel, (f32(3, 64, frames), f32(3, 64, frames)), 1.3)(
        got_a, got_b, parts, ahead_a, ahead_b, behind_a, behind_b
    )


def solution(mesh):
    in_specs = (P(None, "rep", "blk"), P("blk"))
    out_specs = (P(None, ("blk", "rep"), None), P(None, ("blk", "rep"), None))
    return jax.shard_map(shards, mesh=mesh, in_specs=in_specs, out_specs=out_specs, check_vma=False)
```

time: 134 us -> 117 us (0.87); the launches traced: 131 us -> 116 us
  starting transfers between devices: 45 us -> 31.6 us
  local copies, waits for them, and re-layouts: 2.58 us -> 8.92 us
  waiting for transfers between devices: 64.5 us -> 59.4 us
  Pallas kernels: 17.8 us -> 13.8 us
    ppermute x16 -> x18, starting transfers between devices: 41.6 us -> 27.7 us  [route(): return lax.ppermute(array, ('blk', 'rep'), pairs)]
    unnamed x2 -> x24, local copies, waits for them, and re-layouts: 1.19 us -> 8.92 us
    ppermute x16 -> x18, waiting for transfers between devices: 64.5 us -> 59.4 us  [route(): return lax.ppermute(array, ('blk', 'rep'), pairs)]
    pallas_call x4 -> x6, Pallas kernels: 17.8 us -> 13.8 us  [run(): pl.pallas_call(kernel, out_shape=out_shapes, in_specs=specs, out_specs=ja...]
  transfers between devices with their start and end apart: 17 -> 19, of which waited for: 7 -> 11; matrix products, arithmetic and copies ran while one was open for 1% -> 0% of each run, Pallas kernels for 8% -> 6%
where the time goes in v2:
time: 117 us; the launch traced here: 116 us
  waiting for transfers between devices  59.4 us (51%)
  starting transfers between devices  31.6 us (27%)
  Pallas kernels  13.8 us (12%)
  local copies, waits for them, and re-layouts  8.92 us (8%)
  between operations  2.67 us (2%)
    ppermute x18, waiting for transfers between devices, route(): return lax.ppermute(array, ('blk', 'rep'), pairs)  59.4 us
    ppermute x18, starting transfers between devices, route(): return lax.ppermute(array, ('blk', 'rep'), pairs)  27.7 us
    pallas_call x6, Pallas kernels, run(): pl.pallas_call(kernel, out_shape=out_shapes, in_specs=specs, out_specs=ja...  13.8 us
    unnamed x24, local copies, waits for them, and re-layouts  8.92 us
    all_to_all x1, starting transfers between devices, shards(): parts = lax.all_to_all(parts, 'rep', 0, 0)  3.91 us
  transfers between devices with their start and end apart: 19, of which 11 were waited for; matrix products, arithmetic and copies ran while one was open for 0% of the time, Pallas kernels for 6%

profile of v2, /device:TPU:1, one launch (start us, length us, event | category | flops | bytes accessed | tf_op | source)
XLA Modules:
  0.0 116.4 jit_solution(16128671112789875204)
XLA Ops:
  0.6 2.6 %collective-permute-start = (f32[3,300,256]{2,1,0:T(8,128)}, f32[3,300,256]{2,1,0:T(8,128)S(1)}, u32[]{:S(2)}, u32[]{:S(2)}) collective-permute-start(f32[3,300,256]{2,1,0:T(8,128)} %a_ref.1), channel_id=1, source_target_pairs={{0,2},{1,3},{2,0},{3,1},{4,6},{5,7},{6,4},{7,5},{8,10},{9,11},{10,... | collective-permute-start | bytes 2764808 | tf_op jit(solution)/shard_map/ppermute | solution.py:24
  3.2 9.3 %collective-permute-start.1 = (f32[3,300,256]{2,1,0:T(8,128)}, f32[3,300,256]{2,1,0:T(8,128)S(1)}, u32[]{:S(2)}, u32[]{:S(2)}) collective-permute-start(f32[3,300,256]{2,1,0:T(8,128)} %a_ref.1), channel_id=1, source_target_pairs={{0,254},{1,255},{2,244},{3,245},{4,2},{5,3},{6,248},{7,249},{8,6},... | collective-permute-start | bytes 2764808 | tf_op jit(solution)/shard_map/ppermute | solution.py:24
  12.5 1.2 %collective-permute-start.4 = (f32[3,300,256]{2,1,0:T(8,128)}, f32[3,300,256]{2,1,0:T(8,128)S(1)}, u32[]{:S(2)}, u32[]{:S(2)}) collective-permute-start(f32[3,300,256]{2,1,0:T(8,128)} %a_ref.1), channel_id=1, source_target_pairs={{0,1},{1,0},{2,3},{3,2},{4,5},{5,4},{6,7},{7,6},{8,9},{9,8},{10,11... | collective-permute-start | bytes 2764808 | tf_op jit(solution)/shard_map/ppermute | solution.py:24
  13.7 9.1 %collective-permute-done.c_ref = f32[3,300,256]{2,1,0:T(8,128)S(1)} collective-permute-done((f32[3,300,256]{2,1,0:T(8,128)}, f32[3,300,256]{2,1,0:T(8,128)S(1)}, u32[]{:S(2)}, u32[]{:S(2)}) %collective-permute-start) | collective-permute-done | bytes 921632 | tf_op jit(solution)/shard_map/ppermute | solution.py:24
  22.9 9.0 %collective-permute-done.1.a = f32[3,300,256]{2,1,0:T(8,128)S(1)} collective-permute-done((f32[3,300,256]{2,1,0:T(8,128)}, f32[3,300,256]{2,1,0:T(8,128)S(1)}, u32[]{:S(2)}, u32[]{:S(2)}) %collective-permute-start.1) | collective-permute-done | bytes 921632 | tf_op jit(solution)/shard_map/ppermute | solution.py:24
  31.9 1.9 %collective-permute-start.5 = (f32[3,300,256]{2,1,0:T(8,128)S(1)}, f32[3,300,256]{2,1,0:T(8,128)S(1)}, u32[]{:S(2)}, u32[]{:S(2)}) collective-permute-start(f32[3,300,256]{2,1,0:T(8,128)S(1)} %collective-permute-done.c_ref), channel_id=1, source_target_pairs={{0,1},{1,0},{2,3},{3,2},{4,5},{5,4},{6,7},{7,6},{8,9},{9,8},{10,11... | collective-permute-start | bytes 2764808 | tf_op jit(solution)/shard_map/ppermute | solution.py:24
  33.7 0.0 collective-permute-start.6
  33.7 7.5 %collective-permute-start.2 = (f32[3,300,256]{2,1,0:T(8,128)S(1)}, f32[3,300,256]{2,1,0:T(8,128)S(1)}, u32[]{:S(2)}, u32[]{:S(2)}) collective-permute-start(f32[3,300,256]{2,1,0:T(8,128)S(1)} %collective-permute-done.c_ref), channel_id=1, source_target_pairs={{0,254},{1,255},{2,244},{3,245},{4,2},{5,3},{6,248},{7,249},{8,6},... | collective-permute-start | bytes 2764808 | tf_op jit(solution)/shard_map/ppermute | solution.py:24
  41.3 0.0 collective-permute-start.3
  41.3 0.0 collective-permute-done.4.b_ref
  41.3 1.2 %collective-permute-start.7 = (s32[1]{0:T(128)}, s32[1]{0:T(128)}, u32[]{:S(2)}, u32[]{:S(2)}) collective-permute-start(s32[1]{0:T(128)} %param.3), channel_id=1, source_target_pairs={{0,252},{1,253},{2,254},{3,255},{4,0},{5,1},{6,2},{7,3},{8,4},{9,5... | collective-permute-start | bytes 20 | tf_op jit(solution)/shard_map/ppermute | solution.py:24
  42.4 0.0 collective-permute-done.5.d_ref
  42.4 0.0 collective-permute-start.8
  42.5 0.0 copy-start.6
  42.5 1.2 %copy-done.6 = f32[3,300,256]{2,1,0:T(8,128)S(1)} copy-done((f32[3,300,256]{2,1,0:T(8,128)S(1)}, f32[3,300,256]{2,1,0:T(8,128)}, u32[]{:S(2)}) %copy-start.6) | copy-done | bytes 921624
  43.6 1.4 %shard_map.41 = (bf16[768,1280]{1,0:T(8,128)(2,1)S(1)}, bf16[768,1280]{1,0:T(8,128)(2,1)S(1)}, f32[256,128]{1,0:T(8,128)S(1)}) custom-call(f32[3,300,256]{2,1,0:T(8,128)S(1)} %copy-done.6, f32[3,300,256]{2,1,0:T(8,128)S(1)} %collective-permute-done.4.b_ref, f32[3,300,256]{2,1,0:T(8,128)S(1)} %collective-permute-done.c_ref, ...), custom_call_target="tpu_custom_call" | custom-call | bytes 14400000 | tf_op jit(solution)/shard_map/pallas_call | solution.py:271
  45.1 0.0 copy-start
  45.1 0.0 copy-start.7
  45.1 0.0 collective-permute-done.6.b
  45.1 2.3 %shard_map.42 = (f32[768,384]{1,0:T(8,128)S(1)}, f32[8,256]{1,0:T(8,128)S(1)}) custom-call(bf16[768,1280]{1,0:T(8,128)(2,1)S(1)} %get-tuple-element.32.high, bf16[768,1280]{1,0:T(8,128)(2,1)S(1)} %get-tuple-element.33.low, f32[3,300,256]{2,1,0:T(8,128)S(1)} %collective-permute-done.1.a, f32[3,300,256]{2,1,0:T(8,128)S(1)} %collective-permute-done.6.b), custom_call_target="tpu_custom_call" | custom-call | bytes 14400000 | tf_op jit(solution)/shard_map/pallas_call | solution.py:271
  47.4 0.0 copy-done
  47.4 0.0 copy-done.7
  47.4 0.0 copy-start.4
  47.5 13.4 %collective-permute-done.7.count_one = s32[1]{0:T(128)} collective-permute-done((s32[1]{0:T(128)}, s32[1]{0:T(128)}, u32[]{:S(2)}, u32[]{:S(2)}) %collective-permute-start.7) | collective-permute-done | bytes 36 | tf_op jit(solution)/shard_map/ppermute | solution.py:24
  60.9 0.0 collective-permute-done.8.count_three
  60.9 0.0 collective-permute-done.2.near_a.a
  60.9 1.8 %collective-permute-done.3.else_a = f32[3,300,256]{2,1,0:T(8,128)S(1)} collective-permute-done((f32[3,300,256]{2,1,0:T(8,128)S(1)}, f32[3,300,256]{2,1,0:T(8,128)S(1)}, u32[]{:S(2)}, u32[]{:S(2)}) %collective-permute-start.3) | collective-permute-done | bytes 921632 | tf_op jit(solution)/shard_map/ppermute | solution.py:24
  62.7 1.7 %collective-permute-start.9 = (f32[3,300,256]{2,1,0:T(8,128)S(1)}, f32[3,300,256]{2,1,0:T(8,128)S(1)}, u32[]{:S(2)}, u32[]{:S(2)}) collective-permute-start(f32[3,300,256]{2,1,0:T(8,128)S(1)} %collective-permute-done.2.near_a.a), channel_id=1, source_target_pairs={{0,1},{1,0},{2,3},{3,2},{4,5},{5,4},{6,7},{7,6},{8,9},{9,8},{10,11... | collective-permute-start | bytes 2764808 | tf_op jit(solution)/shard_map/ppermute | solution.py:24
  64.4 0.0 collective-permute-start.10
  64.4 2.1 %collective-permute-done.9.near_b.b = f32[3,300,256]{2,1,0:T(8,128)S(1)} collective-permute-done((f32[3,300,256]{2,1,0:T(8,128)S(1)}, f32[3,300,256]{2,1,0:T(8,128)S(1)}, u32[]{:S(2)}, u32[]{:S(2)}) %collective-permute-start.9) | collective-permute-done | bytes 921632 | tf_op jit(solution)/shard_map/ppermute | solution.py:24
  66.5 1.3 %collective-permute-done.10.else_b = f32[3,300,256]{2,1,0:T(8,128)S(1)} collective-permute-done((f32[3,300,256]{2,1,0:T(8,128)S(1)}, f32[3,300,256]{2,1,0:T(8,128)S(1)}, u32[]{:S(2)}, u32[]{:S(2)}) %collective-permute-start.10) | collective-permute-done | bytes 921632 | tf_op jit(solution)/shard_map/ppermute | solution.py:24
  67.8 3.3 %shard_map.43 = (f32[1160,128]{1,0:T(8,128)S(1)}, f32[1160,128]{1,0:T(8,128)}) custom-call(f32[8,256]{1,0:T(8,128)S(1)} %get-tuple-element.36.facts, f32[3,300,256]{2,1,0:T(8,128)S(1)} %collective-permute-done.2.near_a.a, f32[3,300,256]{2,1,0:T(8,128)S(1)} %collective-permute-done.9.near_b.b, f32[3,300,256]{2,1,0:T(8,128)S(1)} %collective-permute-done.3.else_a, ...), custom_call_target="tpu_custom_call" | custom-call | bytes 10800000 | tf_op jit(solution)/shard_map/pallas_call | solution.py:271
  71.1 0.0 copy-done.4
  71.1 0.0 copy-start.2
  71.1 0.9 copy-done.2
  72.1 0.6 collective-permute-start.11
  74.6 0.0 copy-start.1
  74.6 1.5 %copy-done.1 = bf16[768,1280]{1,0:T(8,128)(2,1)S(1)} copy-done((bf16[768,1280]{1,0:T(8,128)(2,1)S(1)}, bf16[768,1280]{1,0:T(8,128)(2,1)}, u32[]{:S(2)}) %copy-start.1) | copy-done | bytes 1966104
  76.2 1.2 %copy-done.3 = f32[3,300,256]{2,1,0:T(8,128)S(1)} copy-done((f32[3,300,256]{2,1,0:T(8,128)S(1)}, f32[3,300,256]{2,1,0:T(8,128)}, u32[]{:S(2)}) %copy-start.3) | copy-done | bytes 921624
  77.3 0.0 copy-start.5
  77.3 1.3 %copy-done.5 = f32[768,384]{1,0:T(8,128)S(1)} copy-done((f32[768,384]{1,0:T(8,128)S(1)}, f32[768,384]{1,0:T(8,128)}, u32[]{:S(2)}) %copy-start.5) | copy-done | bytes 1179672
  78.6 0.9 copy-done.8
  79.5 3.0 %shard_map.44 = (f32[64,256]{1,0:T(8,128)S(1)}, f32[64,256]{1,0:T(8,128)S(1)}, f32[4,64,128]{2,1,0:T(8,128)S(1)}) custom-call(s32[1]{0:T(128)S(6)} %copy.4.own_count, s32[1]{0:T(128)S(6)} %select_n.9.count, bf16[768,1280]{1,0:T(8,128)(2,1)S(1)} %get-tuple-element.32.high, bf16[768,1280]{1,0:T(8,128)(2,1)S(1)} %copy-done.1, f32[256,128]{1,0:T(8,128)S(1)} %copy-done.8, ...), custom_call_target="tpu_custom_call" | custom-call | bytes 14400000 | tf_op jit(solution)/shard_map/pallas_call | solution.py:271
  82.5 0.0 copy-start.9
  82.5 0.6 copy-done.9
  83.2 0.6 copy-done.10
  83.8 0.6 copy-done.11
  84.4 3.9 %all-to-all-start = ((f32[4,64,128]{2,1,0:T(8,128)}), f32[4,64,128]{2,1,0:T(8,128)S(1)}, u32[]{:S(2)}, u32[]{:S(2)}) async-start(f32[4,64,128]{2,1,0:T(8,128)} %copy-done.9), calls=%async_computation | async-start | bytes 262144 | tf_op jit(solution)/shard_map/all_to_all | solution.py:337
  88.4 0.0 collective-permute-start.12
  88.4 0.0 collective-permute-start.13
  88.4 9.9 %collective-permute-done.12.got_a = f32[64,256]{1,0:T(8,128)S(1)} collective-permute-done((f32[64,256]{1,0:T(8,128)}, f32[64,256]{1,0:T(8,128)S(1)}, u32[]{:S(2)}, u32[]{:S(2)}) %collective-permute-start.12) | collective-permute-done | bytes 65568 | tf_op jit(solution)/shard_map/ppermute | solution.py:24
  98.3 2.0 %collective-permute-done.13.got_b = f32[64,256]{1,0:T(8,128)S(1)} collective-permute-done((f32[64,256]{1,0:T(8,128)}, f32[64,256]{1,0:T(8,128)S(1)}, u32[]{:S(2)}, u32[]{:S(2)}) %collective-permute-start.13) | collective-permute-done | bytes 65568 | tf_op jit(solution)/shard_map/ppermute | solution.py:24
  100.3 0.0 all-to-all-done.parts
  100.3 0.0 collective-permute-done.11.got
  100.3 3.0 %shard_map.45 = (f32[64,128]{1,0:T(8,128)S(1)}, f32[64,128]{1,0:T(8,128)S(1)}, f32[64,128]{1,0:T(8,128)S(1)}, f32[64,128]{1,0:T(8,128)S(1)}) custom-call(s32[1]{0:T(128)} %collective-permute-done.7.count_one, s32[1]{0:T(128)} %collective-permute-done.8.count_three, f32[1160,128]{1,0:T(8,128)S(1)} %get-tuple-element.52.mine, ...), custom_call_target="tpu_custom_call" | custom-call | bytes 5400000 | tf_op jit(solution)/shard_map/pallas_call | solution.py:271
  103.3 1.7 %collective-permute-start.14 = (f32[64,128]{1,0:T(8,128)S(1)}, f32[64,128]{1,0:T(8,128)S(1)}, u32[]{:S(2)}, u32[]{:S(2)}) collective-permute-start(f32[64,128]{1,0:T(8,128)S(1)} %get-tuple-element.54), channel_id=1, source_target_pairs={{0,4},{1,6},{2,5},{3,7},{4,8},{5,10},{6,9},{7,11},{8,12},{9,14},{1... | collective-permute-start | bytes 98312 | tf_op jit(solution)/shard_map/ppermute | solution.py:24
  105.0 0.0 collective-permute-start.15
  105.0 0.0 collective-permute-start.16
  105.0 0.0 collective-permute-start.17
  105.0 7.1 %collective-permute-done.14.ahead_a = f32[64,128]{1,0:T(8,128)S(1)} collective-permute-done((f32[64,128]{1,0:T(8,128)S(1)}, f32[64,128]{1,0:T(8,128)S(1)}, u32[]{:S(2)}, u32[]{:S(2)}) %collective-permute-start.14) | collective-permute-done | bytes 32800 | tf_op jit(solution)/shard_map/ppermute | solution.py:24
  112.1 2.6 %collective-permute-done.15.ahead_b = f32[64,128]{1,0:T(8,128)S(1)} collective-permute-done((f32[64,128]{1,0:T(8,128)S(1)}, f32[64,128]{1,0:T(8,128)S(1)}, u32[]{:S(2)}, u32[]{:S(2)}) %collective-permute-start.15) | collective-permute-done | bytes 32800 | tf_op jit(solution)/shard_map/ppermute | solution.py:24
  114.8 0.0 collective-permute-done.16.behind_a
  114.8 0.9 collective-permute-done.17.behind_b
  115.6 0.8 shard_map.46
  (4 shorter events, 0.0 us)
Async XLA Ops:
  0.6 22.2 %collective-permute-start = (f32[3,300,256]{2,1,0:T(8,128)}, f32[3,300,256]{2,1,0:T(8,128)S(1)}, u32[]{:S(2)}, u32[]{:S(2)}) collective-permute-start(f32[3,300,256]{2,1,0:T(8,128)} %a_ref.1), channel_id=1, source_target_pairs={{0,2},{1,3},{2,0},{3,1},{4,6},{5,7},{6,4},{7,5},{8,10},{9,11},{10,... | collective-permute-start | bytes 2764808 | tf_op jit(solution)/shard_map/ppermute | solution.py:24
  3.2 28.7 %collective-permute-start.1 = (f32[3,300,256]{2,1,0:T(8,128)}, f32[3,300,256]{2,1,0:T(8,128)S(1)}, u32[]{:S(2)}, u32[]{:S(2)}) collective-permute-start(f32[3,300,256]{2,1,0:T(8,128)} %a_ref.1), channel_id=1, source_target_pairs={{0,254},{1,255},{2,244},{3,245},{4,2},{5,3},{6,248},{7,249},{8,6},... | collective-permute-start | bytes 2764808 | tf_op jit(solution)/shard_map/ppermute | solution.py:24
  12.5 28.8 %collective-permute-start.4 = (f32[3,300,256]{2,1,0:T(8,128)}, f32[3,300,256]{2,1,0:T(8,128)S(1)}, u32[]{:S(2)}, u32[]{:S(2)}) collective-permute-start(f32[3,300,256]{2,1,0:T(8,128)} %a_ref.1), channel_id=1, source_target_pairs={{0,1},{1,0},{2,3},{3,2},{4,5},{5,4},{6,7},{7,6},{8,9},{9,8},{10,11... | collective-permute-start | bytes 2764808 | tf_op jit(solution)/shard_map/ppermute | solution.py:24
  31.9 10.6 %collective-permute-start.5 = (f32[3,300,256]{2,1,0:T(8,128)S(1)}, f32[3,300,256]{2,1,0:T(8,128)S(1)}, u32[]{:S(2)}, u32[]{:S(2)}) collective-permute-start(f32[3,300,256]{2,1,0:T(8,128)S(1)} %collective-permute-done.c_ref), channel_id=1, source_target_pairs={{0,1},{1,0},{2,3},{3,2},{4,5},{5,4},{6,7},{7,6},{8,9},{9,8},{10,11... | collective-permute-start | bytes 2764808 | tf_op jit(solution)/shard_map/ppermute | solution.py:24
  33.7 11.4 %collective-permute-start.6 = (f32[3,300,256]{2,1,0:T(8,128)S(1)}, f32[3,300,256]{2,1,0:T(8,128)S(1)}, u32[]{:S(2)}, u32[]{:S(2)}) collective-permute-start(f32[3,300,256]{2,1,0:T(8,128)S(1)} %collective-permute-done.1.a), channel_id=1, source_target_pairs={{0,1},{1,0},{2,3},{3,2},{4,5},{5,4},{6,7},{7,6},{8,9},{9,8},{10,11... | collective-permute-start | bytes 2764808 | tf_op jit(solution)/shard_map/ppermute | solution.py:24
  33.7 27.1 %collective-permute-start.2 = (f32[3,300,256]{2,1,0:T(8,128)S(1)}, f32[3,300,256]{2,1,0:T(8,128)S(1)}, u32[]{:S(2)}, u32[]{:S(2)}) collective-permute-start(f32[3,300,256]{2,1,0:T(8,128)S(1)} %collective-permute-done.c_ref), channel_id=1, source_target_pairs={{0,254},{1,255},{2,244},{3,245},{4,2},{5,3},{6,248},{7,249},{8,6},... | collective-permute-start | bytes 2764808 | tf_op jit(solution)/shard_map/ppermute | solution.py:24
  41.3 21.4 %collective-permute-start.3 = (f32[3,300,256]{2,1,0:T(8,128)S(1)}, f32[3,300,256]{2,1,0:T(8,128)S(1)}, u32[]{:S(2)}, u32[]{:S(2)}) collective-permute-start(f32[3,300,256]{2,1,0:T(8,128)S(1)} %collective-permute-done.1.a), channel_id=1, source_target_pairs={{0,2},{1,3},{2,0},{3,1},{4,6},{5,7},{6,4},{7,5},{8,10},{9,11},{10,... | collective-permute-start | bytes 2764808 | tf_op jit(solution)/shard_map/ppermute | solution.py:24
  41.3 19.6 %collective-permute-start.7 = (s32[1]{0:T(128)}, s32[1]{0:T(128)}, u32[]{:S(2)}, u32[]{:S(2)}) collective-permute-start(s32[1]{0:T(128)} %param.3), channel_id=1, source_target_pairs={{0,252},{1,253},{2,254},{3,255},{4,0},{5,1},{6,2},{7,3},{8,4},{9,5... | collective-permute-start | bytes 20 | tf_op jit(solution)/shard_map/ppermute | solution.py:24
  42.4 18.4 %collective-permute-start.8 = (s32[1]{0:T(128)}, s32[1]{0:T(128)}, u32[]{:S(2)}, u32[]{:S(2)}) collective-permute-start(s32[1]{0:T(128)} %param.3), channel_id=1, source_target_pairs={{0,244},{1,245},{2,246},{3,247},{4,248},{5,249},{6,250},{7,251},{8... | collective-permute-start | bytes 20 | tf_op jit(solution)/shard_map/ppermute | solution.py:24
  42.5 1.2 %copy-start.6 = (f32[3,300,256]{2,1,0:T(8,128)S(1)}, f32[3,300,256]{2,1,0:T(8,128)}, u32[]{:S(2)}) copy-start(f32[3,300,256]{2,1,0:T(8,128)} %a_ref.1) | copy-start | bytes 2764804
  45.1 2.4 %copy-start = (bf16[768,1280]{1,0:T(8,128)(2,1)}, bf16[768,1280]{1,0:T(8,128)(2,1)S(1)}, u32[]{:S(2)}) copy-start(bf16[768,1280]{1,0:T(8,128)(2,1)S(1)} %get-tuple-element.33.low) | copy-start | bytes 5898244
  45.1 2.4 %copy-start.7 = (f32[256,128]{1,0:T(8,128)}, f32[256,128]{1,0:T(8,128)S(1)}, u32[]{:S(2)}) copy-start(f32[256,128]{1,0:T(8,128)S(1)} %get-tuple-element.42.square) | copy-start | bytes 393220
  47.4 23.7 %copy-start.4 = (f32[768,384]{1,0:T(8,128)}, f32[768,384]{1,0:T(8,128)S(1)}, u32[]{:S(2)}) copy-start(f32[768,384]{1,0:T(8,128)S(1)} %get-tuple-element.45.first) | copy-start | bytes 3538948
  62.7 3.8 %collective-permute-start.9 = (f32[3,300,256]{2,1,0:T(8,128)S(1)}, f32[3,300,256]{2,1,0:T(8,128)S(1)}, u32[]{:S(2)}, u32[]{:S(2)}) collective-permute-start(f32[3,300,256]{2,1,0:T(8,128)S(1)} %collective-permute-done.2.near_a.a), channel_id=1, source_target_pairs={{0,1},{1,0},{2,3},{3,2},{4,5},{5,4},{6,7},{7,6},{8,9},{9,8},{10,11... | collective-permute-start | bytes 2764808 | tf_op jit(solution)/shard_map/ppermute | solution.py:24
  64.4 3.5 %collective-permute-start.10 = (f32[3,300,256]{2,1,0:T(8,128)S(1)}, f32[3,300,256]{2,1,0:T(8,128)S(1)}, u32[]{:S(2)}, u32[]{:S(2)}) collective-permute-start(f32[3,300,256]{2,1,0:T(8,128)S(1)} %collective-permute-done.3.else_a), channel_id=1, source_target_pairs={{0,1},{1,0},{2,3},{3,2},{4,5},{5,4},{6,7},{7,6},{8,9},{9,8},{10,11... | collective-permute-start | bytes 2764808 | tf_op jit(solution)/shard_map/ppermute | solution.py:24
  71.1 0.9 copy-start.2
  72.1 28.2 %collective-permute-start.11 = (f32[1160,128]{1,0:T(8,128)}, f32[1160,128]{1,0:T(8,128)}, u32[]{:S(2)}, u32[]{:S(2)}) collective-permute-start(f32[1160,128]{1,0:T(8,128)} %get-tuple-element.39), channel_id=1, source_target_pairs={{0,2},{1,3},{2,0},{3,1},{4,6},{5,7},{6,4},{7,5},{8,10},{9,11},{10,... | collective-permute-start | bytes 1781768 | tf_op jit(solution)/shard_map/ppermute | solution.py:24
  74.6 1.5 %copy-start.1 = (bf16[768,1280]{1,0:T(8,128)(2,1)S(1)}, bf16[768,1280]{1,0:T(8,128)(2,1)}, u32[]{:S(2)}) copy-start(bf16[768,1280]{1,0:T(8,128)(2,1)} %copy-done) | copy-start | bytes 5898244
  76.2 1.2 %copy-start.3 = (f32[3,300,256]{2,1,0:T(8,128)S(1)}, f32[3,300,256]{2,1,0:T(8,128)}, u32[]{:S(2)}) copy-start(f32[3,300,256]{2,1,0:T(8,128)} %copy-done.2) | copy-start | bytes 2764804
  77.3 1.3 %copy-start.5 = (f32[768,384]{1,0:T(8,128)S(1)}, f32[768,384]{1,0:T(8,128)}, u32[]{:S(2)}) copy-start(f32[768,384]{1,0:T(8,128)} %copy-done.4) | copy-start | bytes 3538948
  78.6 0.9 copy-start.8
  82.5 0.7 copy-start.9
  83.2 0.6 copy-start.10
  83.8 0.6 copy-start.11
  84.4 15.8 %all-to-all-start = ((f32[4,64,128]{2,1,0:T(8,128)}), f32[4,64,128]{2,1,0:T(8,128)S(1)}, u32[]{:S(2)}, u32[]{:S(2)}) async-start(f32[4,64,128]{2,1,0:T(8,128)} %copy-done.9), calls=%async_computation | async-start | bytes 262144 | tf_op jit(solution)/shard_map/all_to_all | solution.py:337
  88.4 9.9 %collective-permute-start.12 = (f32[64,256]{1,0:T(8,128)}, f32[64,256]{1,0:T(8,128)S(1)}, u32[]{:S(2)}, u32[]{:S(2)}) collective-permute-start(f32[64,256]{1,0:T(8,128)} %copy-done.11), channel_id=1, source_target_pairs={{0,13},{1,15},{2,4},{3,6},{4,17},{5,19},{6,8},{7,10},{8,21},{9,23}... | collective-permute-start | bytes 196616 | tf_op jit(solution)/shard_map/ppermute | solution.py:24
  88.4 11.9 %collective-permute-start.13 = (f32[64,256]{1,0:T(8,128)}, f32[64,256]{1,0:T(8,128)S(1)}, u32[]{:S(2)}, u32[]{:S(2)}) collective-permute-start(f32[64,256]{1,0:T(8,128)} %copy-done.10), channel_id=1, source_target_pairs={{0,12},{1,14},{2,5},{3,7},{4,16},{5,18},{6,9},{7,11},{8,20},{9,22}... | collective-permute-start | bytes 196616 | tf_op jit(solution)/shard_map/ppermute | solution.py:24
  103.3 8.8 %collective-permute-start.14 = (f32[64,128]{1,0:T(8,128)S(1)}, f32[64,128]{1,0:T(8,128)S(1)}, u32[]{:S(2)}, u32[]{:S(2)}) collective-permute-start(f32[64,128]{1,0:T(8,128)S(1)} %get-tuple-element.54), channel_id=1, source_target_pairs={{0,4},{1,6},{2,5},{3,7},{4,8},{5,10},{6,9},{7,11},{8,12},{9,14},{1... | collective-permute-start | bytes 98312 | tf_op jit(solution)/shard_map/ppermute | solution.py:24
  105.0 9.8 %collective-permute-start.15 = (f32[64,128]{1,0:T(8,128)S(1)}, f32[64,128]{1,0:T(8,128)S(1)}, u32[]{:S(2)}, u32[]{:S(2)}) collective-permute-start(f32[64,128]{1,0:T(8,128)S(1)} %get-tuple-element.55), channel_id=1, source_target_pairs={{0,5},{1,7},{2,4},{3,6},{4,9},{5,11},{6,8},{7,10},{8,13},{9,15},{1... | collective-permute-start | bytes 98312 | tf_op jit(solution)/shard_map/ppermute | solution.py:24
  105.0 9.8 %collective-permute-start.16 = (f32[64,128]{1,0:T(8,128)S(1)}, f32[64,128]{1,0:T(8,128)S(1)}, u32[]{:S(2)}, u32[]{:S(2)}) collective-permute-start(f32[64,128]{1,0:T(8,128)S(1)} %get-tuple-element.56), channel_id=1, source_target_pairs={{0,12},{1,13},{2,14},{3,15},{4,16},{5,17},{6,18},{7,19},{8,20},{9,... | collective-permute-start | bytes 98312 | tf_op jit(solution)/shard_map/ppermute | solution.py:24
  105.0 10.6 %collective-permute-start.17 = (f32[64,128]{1,0:T(8,128)S(1)}, f32[64,128]{1,0:T(8,128)S(1)}, u32[]{:S(2)}, u32[]{:S(2)}) collective-permute-start(f32[64,128]{1,0:T(8,128)S(1)} %get-tuple-element.57), channel_id=1, source_target_pairs={{0,13},{1,12},{2,15},{3,14},{4,17},{5,16},{6,19},{7,18},{8,21},{9,... | collective-permute-start | bytes 98312 | tf_op jit(solution)/shard_map/ppermute | solution.py:24

commit v3 on v2

--- a/solution.py
+++ b/solution.py
@@ -160,8 +160,9 @@
     acc[...] = products(high[:, DEPTH // 2:], low[:, DEPTH // 2:], right_high[...], right_low[...])
 
 
-def near_kernel(own_count, count, high, low, square, first, facts, a, b, out_a, out_b, parts, right_high, right_low, acc, tile, turned):
+def near_kernel(own_count, count_one, count_three, high, low, square, first, facts, a, b, out_a, out_b, parts, right_high, right_low, acc, tile, turned):
     low_place, core = place_of()
+    count = jnp.where(low_place == 1, count_one[0], count_three[0])
     lanes = aligned(core, 128)
     about = facts[:, lanes]
     total, column_square = right_side((a, b), lanes, about, right_high, right_low)
@@ -178,7 +179,7 @@
             for i in range(3)
         ]
 
-    fill_tile(covariance, frames, square, column_square, own_count[0], count[0] - core * 128, tile)
+    fill_tile(covariance, frames, square, column_square, own_count[0], count - core * 128, tile)
     parts[...] = tile[...].reshape(parts.shape)
     turned[...] = tile[...].T
     out_a[...] = turned[aligned(1 - low_place, 64), :]
@@ -299,7 +300,6 @@
     own_core = route(coords, other_core)
     count_one = route(frame_count, lambda block, rep: (block - 1, rep))
     count_three = route(frame_count, lambda block, rep: (block - 3, rep))
-    own_chip, near_a = together((own_chip, near_a))
 
     near_b = route(own_chip, to_neighbour)
     else_a = route(near_a, other_chip)
@@ -325,17 +325,16 @@
     )(facts, near_b, near_b_core, else_a, else_a_core)
     got = route(give, other_chip)
     near_first, mine = together((near_first, mine))
-    near_count = jnp.where(lax.axis_index("rep") < 2, count_three, count_one)
     near_out_a, near_out_b, parts = call(
         near_kernel,
         (f32(64, frames), f32(64, frames), f32(4, 64, 128)),
         4.0,
         sides + [((768, 384), wide), ((frames, 128), wide), ((128, frames), wide)],
-    )(frame_count, near_count, high, low, square, near_first, facts, near_b, near_b_core)
+    )(frame_count, count_one, count_three, high, low, square, near_first, facts, near_b, near_b_core)
     got_a = route(near_out_a, lambda b, r: (b + 1, 2 * (r % 2)) if r >= 2 else (b + 3, 2 * (r % 2) + 1))
     got_b = route(near_out_b, lambda b, r: (b + 1, 2 * (r % 2) + 1) if r >= 2 else (b + 3, 2 * (r % 2)))
     parts = lax.all_to_all(parts, "rep", 0, 0)
-    got, got_a, got_b, parts = together((got, got_a, got_b, parts))
+    got, near_out_a, near_out_b = together((got, near_out_a, near_out_b))
 
     ahead_a, ahead_b, behind_a, behind_b = call(
         far_kernel,

time: 117 us -> 104 us (0.89)
  local copies, waits for them, and re-layouts: 8.92 us -> 1.18 us
  waiting for transfers between devices: 59.4 us -> 52.1 us
  starting transfers between devices: 31.6 us -> 35 us
  between operations: 2.67 us -> 1.36 us
    unnamed x24 -> x2, local copies, waits for them, and re-layouts: 8.92 us -> 1.18 us
    ppermute x18, waiting for transfers between devices: 59.4 us -> 52.1 us  [route(): return lax.ppermute(array, ('blk', 'rep'), pairs)]
    ppermute x18, starting transfers between devices: 27.7 us -> 31.1 us  [route(): return lax.ppermute(array, ('blk', 'rep'), pairs)]
  transfers between devices with their start and end apart: 19 -> 19, of which waited for: 11 -> 10; matrix products, arithmetic and copies ran while one was open for 0% -> 0% of each run, Pallas kernels for 6% -> 10%
where the time goes in v3:
time: 104 us
  waiting for transfers between devices  52.1 us (50%)
  starting transfers between devices  35 us (34%)
  Pallas kernels  13.9 us (13%)
  between operations  1.36 us (1%)
  local copies, waits for them, and re-layouts  1.18 us (1%)
    ppermute x18, waiting for transfers between devices, route(): return lax.ppermute(array, ('blk', 'rep'), pairs)  52.1 us
    ppermute x18, starting transfers between devices, route(): return lax.ppermute(array, ('blk', 'rep'), pairs)  31.1 us
    pallas_call x6, Pallas kernels, run(): pl.pallas_call(kernel, out_shape=out_shapes, in_specs=specs, out_specs=ja...  13.9 us
    all_to_all x1, starting transfers between devices, shards(): parts = lax.all_to_all(parts, 'rep', 0, 0)  3.91 us
  transfers between devices with their start and end apart: 19, of which 10 were waited for; matrix products, arithmetic and copies ran while one was open for 0% of the time, Pallas kernels for 10%

profile of v3, /device:TPU:1, one launch (start us, length us, event | category | flops | bytes accessed | tf_op | source)
XLA Modules:
  0.0 103.6 jit_solution(14621852090572636252)
XLA Ops:
  0.6 2.6 %collective-permute-start = (f32[3,300,256]{2,1,0:T(8,128)}, f32[3,300,256]{2,1,0:T(8,128)S(1)}, u32[]{:S(2)}, u32[]{:S(2)}) collective-permute-start(f32[3,300,256]{2,1,0:T(8,128)} %a_ref.1), channel_id=1, source_target_pairs={{0,2},{1,3},{2,0},{3,1},{4,6},{5,7},{6,4},{7,5},{8,10},{9,11},{10,... | collective-permute-start | bytes 2764808 | tf_op jit(solution)/shard_map/ppermute | solution.py:24
  3.2 9.3 %collective-permute-start.2 = (f32[3,300,256]{2,1,0:T(8,128)}, f32[3,300,256]{2,1,0:T(8,128)S(1)}, u32[]{:S(2)}, u32[]{:S(2)}) collective-permute-start(f32[3,300,256]{2,1,0:T(8,128)} %a_ref.1), channel_id=1, source_target_pairs={{0,254},{1,255},{2,244},{3,245},{4,2},{5,3},{6,248},{7,249},{8,6},... | collective-permute-start | bytes 2764808 | tf_op jit(solution)/shard_map/ppermute | solution.py:24
  12.5 1.2 %collective-permute-start.4 = (f32[3,300,256]{2,1,0:T(8,128)}, f32[3,300,256]{2,1,0:T(8,128)S(1)}, u32[]{:S(2)}, u32[]{:S(2)}) collective-permute-start(f32[3,300,256]{2,1,0:T(8,128)} %a_ref.1), channel_id=1, source_target_pairs={{0,1},{1,0},{2,3},{3,2},{4,5},{5,4},{6,7},{7,6},{8,9},{9,8},{10,11... | collective-permute-start | bytes 2764808 | tf_op jit(solution)/shard_map/ppermute | solution.py:24
  13.7 9.1 %collective-permute-done.c_ref = f32[3,300,256]{2,1,0:T(8,128)S(1)} collective-permute-done((f32[3,300,256]{2,1,0:T(8,128)}, f32[3,300,256]{2,1,0:T(8,128)S(1)}, u32[]{:S(2)}, u32[]{:S(2)}) %collective-permute-start) | collective-permute-done | bytes 921632 | tf_op jit(solution)/shard_map/ppermute | solution.py:24
  22.9 2.2 %collective-permute-start.5 = (f32[3,300,256]{2,1,0:T(8,128)S(1)}, f32[3,300,256]{2,1,0:T(8,128)S(1)}, u32[]{:S(2)}, u32[]{:S(2)}) collective-permute-start(f32[3,300,256]{2,1,0:T(8,128)S(1)} %collective-permute-done.c_ref), channel_id=1, source_target_pairs={{0,1},{1,0},{2,3},{3,2},{4,5},{5,4},{6,7},{7,6},{8,9},{9,8},{10,11... | collective-permute-start | bytes 2764808 | tf_op jit(solution)/shard_map/ppermute | solution.py:24
  25.0 6.8 %collective-permute-done.2.a = f32[3,300,256]{2,1,0:T(8,128)S(1)} collective-permute-done((f32[3,300,256]{2,1,0:T(8,128)}, f32[3,300,256]{2,1,0:T(8,128)S(1)}, u32[]{:S(2)}, u32[]{:S(2)}) %collective-permute-start.2) | collective-permute-done | bytes 921632 | tf_op jit(solution)/shard_map/ppermute | solution.py:24
  31.9 1.9 %collective-permute-start.6 = (f32[3,300,256]{2,1,0:T(8,128)S(1)}, f32[3,300,256]{2,1,0:T(8,128)S(1)}, u32[]{:S(2)}, u32[]{:S(2)}) collective-permute-start(f32[3,300,256]{2,1,0:T(8,128)S(1)} %collective-permute-done.2.a), channel_id=1, source_target_pairs={{0,1},{1,0},{2,3},{3,2},{4,5},{5,4},{6,7},{7,6},{8,9},{9,8},{10,11... | collective-permute-start | bytes 2764808 | tf_op jit(solution)/shard_map/ppermute | solution.py:24
  33.7 7.5 %collective-permute-start.1 = (f32[3,300,256]{2,1,0:T(8,128)S(1)}, f32[3,300,256]{2,1,0:T(8,128)S(1)}, u32[]{:S(2)}, u32[]{:S(2)}) collective-permute-start(f32[3,300,256]{2,1,0:T(8,128)S(1)} %collective-permute-done.c_ref), channel_id=1, source_target_pairs={{0,254},{1,255},{2,244},{3,245},{4,2},{5,3},{6,248},{7,249},{8,6},... | collective-permute-start | bytes 2764808 | tf_op jit(solution)/shard_map/ppermute | solution.py:24
  41.3 0.0 collective-permute-start.3
  41.3 0.0 collective-permute-done.4.b_ref
  41.3 1.2 %collective-permute-start.7 = (s32[1]{0:T(128)}, s32[1]{0:T(128)}, u32[]{:S(2)}, u32[]{:S(2)}) collective-permute-start(s32[1]{0:T(128)} %param.3), channel_id=1, source_target_pairs={{0,252},{1,253},{2,254},{3,255},{4,0},{5,1},{6,2},{7,3},{8,4},{9,5... | collective-permute-start | bytes 20 | tf_op jit(solution)/shard_map/ppermute | solution.py:24
  42.4 0.0 collective-permute-done.5.d_ref
  42.4 0.0 collective-permute-start.8
  42.4 0.0 copy-start
  42.5 1.2 %copy-done = f32[3,300,256]{2,1,0:T(8,128)S(1)} copy-done((f32[3,300,256]{2,1,0:T(8,128)S(1)}, f32[3,300,256]{2,1,0:T(8,128)}, u32[]{:S(2)}) %copy-start) | copy-done | bytes 921624
  43.6 1.4 %shard_map.41 = (bf16[768,1280]{1,0:T(8,128)(2,1)S(1)}, bf16[768,1280]{1,0:T(8,128)(2,1)S(1)}, f32[256,128]{1,0:T(8,128)S(1)}) custom-call(f32[3,300,256]{2,1,0:T(8,128)S(1)} %copy-done, f32[3,300,256]{2,1,0:T(8,128)S(1)} %collective-permute-done.4.b_ref, f32[3,300,256]{2,1,0:T(8,128)S(1)} %collective-permute-done.c_ref, ...), custom_call_target="tpu_custom_call" | custom-call | bytes 14400000 | tf_op jit(solution)/shard_map/pallas_call | solution.py:272
  45.1 0.0 collective-permute-done.6.b
  45.1 2.3 %shard_map.42 = (f32[768,384]{1,0:T(8,128)S(1)}, f32[8,256]{1,0:T(8,128)S(1)}) custom-call(bf16[768,1280]{1,0:T(8,128)(2,1)S(1)} %get-tuple-element.25.high, bf16[768,1280]{1,0:T(8,128)(2,1)S(1)} %get-tuple-element.26.low, f32[3,300,256]{2,1,0:T(8,128)S(1)} %collective-permute-done.2.a, f32[3,300,256]{2,1,0:T(8,128)S(1)} %collective-permute-done.6.b), custom_call_target="tpu_custom_call" | custom-call | bytes 14400000 | tf_op jit(solution)/shard_map/pallas_call | solution.py:272
  47.4 14.0 %collective-permute-done.7.count_one = s32[1]{0:T(128)} collective-permute-done((s32[1]{0:T(128)}, s32[1]{0:T(128)}, u32[]{:S(2)}, u32[]{:S(2)}) %collective-permute-start.7) | collective-permute-done | bytes 36 | tf_op jit(solution)/shard_map/ppermute | solution.py:24
  61.4 0.0 collective-permute-done.8.count_three
  61.4 0.0 collective-permute-done.1.near_a.a
  61.4 1.8 %collective-permute-done.3.else_a = f32[3,300,256]{2,1,0:T(8,128)S(1)} collective-permute-done((f32[3,300,256]{2,1,0:T(8,128)S(1)}, f32[3,300,256]{2,1,0:T(8,128)S(1)}, u32[]{:S(2)}, u32[]{:S(2)}) %collective-permute-start.3) | collective-permute-done | bytes 921632 | tf_op jit(solution)/shard_map/ppermute | solution.py:24
  63.3 1.1 %collective-permute-start.9 = (f32[3,300,256]{2,1,0:T(8,128)S(1)}, f32[3,300,256]{2,1,0:T(8,128)S(1)}, u32[]{:S(2)}, u32[]{:S(2)}) collective-permute-start(f32[3,300,256]{2,1,0:T(8,128)S(1)} %collective-permute-done.1.near_a.a), channel_id=1, source_target_pairs={{0,1},{1,0},{2,3},{3,2},{4,5},{5,4},{6,7},{7,6},{8,9},{9,8},{10,11... | collective-permute-start | bytes 2764808 | tf_op jit(solution)/shard_map/ppermute | solution.py:24
  64.4 0.0 collective-permute-start.10
  64.4 2.1 %collective-permute-done.9.near_b.b = f32[3,300,256]{2,1,0:T(8,128)S(1)} collective-permute-done((f32[3,300,256]{2,1,0:T(8,128)S(1)}, f32[3,300,256]{2,1,0:T(8,128)S(1)}, u32[]{:S(2)}, u32[]{:S(2)}) %collective-permute-start.9) | collective-permute-done | bytes 921632 | tf_op jit(solution)/shard_map/ppermute | solution.py:24
  66.5 1.3 %collective-permute-done.10.else_b = f32[3,300,256]{2,1,0:T(8,128)S(1)} collective-permute-done((f32[3,300,256]{2,1,0:T(8,128)S(1)}, f32[3,300,256]{2,1,0:T(8,128)S(1)}, u32[]{:S(2)}, u32[]{:S(2)}) %collective-permute-start.10) | collective-permute-done | bytes 921632 | tf_op jit(solution)/shard_map/ppermute | solution.py:24
  67.8 2.6 %shard_map.43 = (f32[1160,128]{1,0:T(8,128)S(1)}, f32[1160,128]{1,0:T(8,128)S(1)}) custom-call(f32[8,256]{1,0:T(8,128)S(1)} %get-tuple-element.33.facts, f32[3,300,256]{2,1,0:T(8,128)S(1)} %collective-permute-done.1.near_a.a, f32[3,300,256]{2,1,0:T(8,128)S(1)} %collective-permute-done.9.near_b.b, f32[3,300,256]{2,1,0:T(8,128)S(1)} %collective-permute-done.3.else_a, ...), custom_call_target="tpu_custom_call" | custom-call | bytes 10800000 | tf_op jit(solution)/shard_map/pallas_call | solution.py:272
  70.5 0.6 collective-permute-start.13
  71.7 4.9 %shard_map.44 = (f32[64,256]{1,0:T(8,128)S(1)}, f32[64,256]{1,0:T(8,128)S(1)}, f32[4,64,128]{2,1,0:T(8,128)}) custom-call(s32[1]{0:T(128)S(6)} %copy.4.own_count, s32[1]{0:T(128)} %collective-permute-done.7.count_one, s32[1]{0:T(128)} %collective-permute-done.8.count_three, bf16[768,1280]{1,0:T(8,128)(2,1)S(1)} %get-tuple-element.25.high, ...), custom_call_target="tpu_custom_call" | custom-call | bytes 14400000 | tf_op jit(solution)/shard_map/pallas_call | solution.py:272
  76.5 3.9 %all-to-all-start = ((f32[4,64,128]{2,1,0:T(8,128)}), f32[4,64,128]{2,1,0:T(8,128)S(1)}, u32[]{:S(2)}, u32[]{:S(2)}) async-start(f32[4,64,128]{2,1,0:T(8,128)} %get-tuple-element.40), calls=%async_computation | async-start | bytes 262144 | tf_op jit(solution)/shard_map/all_to_all | solution.py:336
  80.4 0.0 collective-permute-start.11
  80.4 0.0 collective-permute-start.12
  80.4 6.2 %collective-permute-done.13.got = f32[1160,128]{1,0:T(8,128)S(1)} collective-permute-done((f32[1160,128]{1,0:T(8,128)S(1)}, f32[1160,128]{1,0:T(8,128)S(1)}, u32[]{:S(2)}, u32[]{:S(2)}) %collective-permute-start.13) | collective-permute-done | bytes 593952 | tf_op jit(solution)/shard_map/ppermute | solution.py:24
  86.6 2.0 %shard_map.45 = (f32[64,128]{1,0:T(8,128)S(1)}, f32[64,128]{1,0:T(8,128)S(1)}, f32[64,128]{1,0:T(8,128)S(1)}, f32[64,128]{1,0:T(8,128)S(1)}) custom-call(s32[1]{0:T(128)} %collective-permute-done.7.count_one, s32[1]{0:T(128)} %collective-permute-done.8.count_three, f32[1160,128]{1,0:T(8,128)S(1)} %get-tuple-element.41.mine, ...), custom_call_target="tpu_custom_call" | custom-call | bytes 5400000 | tf_op jit(solution)/shard_map/pallas_call | solution.py:272
  88.6 3.5 %collective-permute-start.14 = (f32[64,128]{1,0:T(8,128)S(1)}, f32[64,128]{1,0:T(8,128)S(1)}, u32[]{:S(2)}, u32[]{:S(2)}) collective-permute-start(f32[64,128]{1,0:T(8,128)S(1)} %get-tuple-element.44), channel_id=1, source_target_pairs={{0,4},{1,6},{2,5},{3,7},{4,8},{5,10},{6,9},{7,11},{8,12},{9,14},{1... | collective-permute-start | bytes 98312 | tf_op jit(solution)/shard_map/ppermute | solution.py:24
  92.0 0.0 collective-permute-start.15
  92.0 0.0 collective-permute-start.16
  92.0 0.0 collective-permute-done.11.got_a
  92.0 0.1 collective-permute-start.17
  92.1 0.0 collective-permute-done.12.got_b
  92.1 0.0 all-to-all-done.parts
  92.2 6.5 %collective-permute-done.14.ahead_a = f32[64,128]{1,0:T(8,128)S(1)} collective-permute-done((f32[64,128]{1,0:T(8,128)S(1)}, f32[64,128]{1,0:T(8,128)S(1)}, u32[]{:S(2)}, u32[]{:S(2)}) %collective-permute-start.14) | collective-permute-done | bytes 32800 | tf_op jit(solution)/shard_map/ppermute | solution.py:24
  98.6 3.9 %collective-permute-done.15.ahead_b = f32[64,128]{1,0:T(8,128)S(1)} collective-permute-done((f32[64,128]{1,0:T(8,128)S(1)}, f32[64,128]{1,0:T(8,128)S(1)}, u32[]{:S(2)}, u32[]{:S(2)}) %collective-permute-start.15) | collective-permute-done | bytes 32800 | tf_op jit(solution)/shard_map/ppermute | solution.py:24
  102.5 0.0 collective-permute-done.16.behind_a
  102.5 0.3 collective-permute-done.17.behind_b
  102.8 0.8 shard_map.46
Async XLA Ops:
  0.6 22.2 %collective-permute-start = (f32[3,300,256]{2,1,0:T(8,128)}, f32[3,300,256]{2,1,0:T(8,128)S(1)}, u32[]{:S(2)}, u32[]{:S(2)}) collective-permute-start(f32[3,300,256]{2,1,0:T(8,128)} %a_ref.1), channel_id=1, source_target_pairs={{0,2},{1,3},{2,0},{3,1},{4,6},{5,7},{6,4},{7,5},{8,10},{9,11},{10,... | collective-permute-start | bytes 2764808 | tf_op jit(solution)/shard_map/ppermute | solution.py:24
  3.2 28.7 %collective-permute-start.2 = (f32[3,300,256]{2,1,0:T(8,128)}, f32[3,300,256]{2,1,0:T(8,128)S(1)}, u32[]{:S(2)}, u32[]{:S(2)}) collective-permute-start(f32[3,300,256]{2,1,0:T(8,128)} %a_ref.1), channel_id=1, source_target_pairs={{0,254},{1,255},{2,244},{3,245},{4,2},{5,3},{6,248},{7,249},{8,6},... | collective-permute-start | bytes 2764808 | tf_op jit(solution)/shard_map/ppermute | solution.py:24
  12.5 28.8 %collective-permute-start.4 = (f32[3,300,256]{2,1,0:T(8,128)}, f32[3,300,256]{2,1,0:T(8,128)S(1)}, u32[]{:S(2)}, u32[]{:S(2)}) collective-permute-start(f32[3,300,256]{2,1,0:T(8,128)} %a_ref.1), channel_id=1, source_target_pairs={{0,1},{1,0},{2,3},{3,2},{4,5},{5,4},{6,7},{7,6},{8,9},{9,8},{10,11... | collective-permute-start | bytes 2764808 | tf_op jit(solution)/shard_map/ppermute | solution.py:24
  22.9 19.6 %collective-permute-start.5 = (f32[3,300,256]{2,1,0:T(8,128)S(1)}, f32[3,300,256]{2,1,0:T(8,128)S(1)}, u32[]{:S(2)}, u32[]{:S(2)}) collective-permute-start(f32[3,300,256]{2,1,0:T(8,128)S(1)} %collective-permute-done.c_ref), channel_id=1, source_target_pairs={{0,1},{1,0},{2,3},{3,2},{4,5},{5,4},{6,7},{7,6},{8,9},{9,8},{10,11... | collective-permute-start | bytes 2764808 | tf_op jit(solution)/shard_map/ppermute | solution.py:24
  31.9 13.2 %collective-permute-start.6 = (f32[3,300,256]{2,1,0:T(8,128)S(1)}, f32[3,300,256]{2,1,0:T(8,128)S(1)}, u32[]{:S(2)}, u32[]{:S(2)}) collective-permute-start(f32[3,300,256]{2,1,0:T(8,128)S(1)} %collective-permute-done.2.a), channel_id=1, source_target_pairs={{0,1},{1,0},{2,3},{3,2},{4,5},{5,4},{6,7},{7,6},{8,9},{9,8},{10,11... | collective-permute-start | bytes 2764808 | tf_op jit(solution)/shard_map/ppermute | solution.py:24
  33.7 27.7 %collective-permute-start.1 = (f32[3,300,256]{2,1,0:T(8,128)S(1)}, f32[3,300,256]{2,1,0:T(8,128)S(1)}, u32[]{:S(2)}, u32[]{:S(2)}) collective-permute-start(f32[3,300,256]{2,1,0:T(8,128)S(1)} %collective-permute-done.c_ref), channel_id=1, source_target_pairs={{0,254},{1,255},{2,244},{3,245},{4,2},{5,3},{6,248},{7,249},{8,6},... | collective-permute-start | bytes 2764808 | tf_op jit(solution)/shard_map/ppermute | solution.py:24
  41.3 22.0 %collective-permute-start.3 = (f32[3,300,256]{2,1,0:T(8,128)S(1)}, f32[3,300,256]{2,1,0:T(8,128)S(1)}, u32[]{:S(2)}, u32[]{:S(2)}) collective-permute-start(f32[3,300,256]{2,1,0:T(8,128)S(1)} %collective-permute-done.2.a), channel_id=1, source_target_pairs={{0,2},{1,3},{2,0},{3,1},{4,6},{5,7},{6,4},{7,5},{8,10},{9,11},{10,... | collective-permute-start | bytes 2764808 | tf_op jit(solution)/shard_map/ppermute | solution.py:24
  41.3 20.2 %collective-permute-start.7 = (s32[1]{0:T(128)}, s32[1]{0:T(128)}, u32[]{:S(2)}, u32[]{:S(2)}) collective-permute-start(s32[1]{0:T(128)} %param.3), channel_id=1, source_target_pairs={{0,252},{1,253},{2,254},{3,255},{4,0},{5,1},{6,2},{7,3},{8,4},{9,5... | collective-permute-start | bytes 20 | tf_op jit(solution)/shard_map/ppermute | solution.py:24
  42.4 19.0 %collective-permute-start.8 = (s32[1]{0:T(128)}, s32[1]{0:T(128)}, u32[]{:S(2)}, u32[]{:S(2)}) collective-permute-start(s32[1]{0:T(128)} %param.3), channel_id=1, source_target_pairs={{0,244},{1,245},{2,246},{3,247},{4,248},{5,249},{6,250},{7,251},{8... | collective-permute-start | bytes 20 | tf_op jit(solution)/shard_map/ppermute | solution.py:24
  42.4 1.2 %copy-start = (f32[3,300,256]{2,1,0:T(8,128)S(1)}, f32[3,300,256]{2,1,0:T(8,128)}, u32[]{:S(2)}) copy-start(f32[3,300,256]{2,1,0:T(8,128)} %a_ref.1) | copy-start | bytes 2764804
  63.3 3.2 %collective-permute-start.9 = (f32[3,300,256]{2,1,0:T(8,128)S(1)}, f32[3,300,256]{2,1,0:T(8,128)S(1)}, u32[]{:S(2)}, u32[]{:S(2)}) collective-permute-start(f32[3,300,256]{2,1,0:T(8,128)S(1)} %collective-permute-done.1.near_a.a), channel_id=1, source_target_pairs={{0,1},{1,0},{2,3},{3,2},{4,5},{5,4},{6,7},{7,6},{8,9},{9,8},{10,11... | collective-permute-start | bytes 2764808 | tf_op jit(solution)/shard_map/ppermute | solution.py:24
  64.4 3.5 %collective-permute-start.10 = (f32[3,300,256]{2,1,0:T(8,128)S(1)}, f32[3,300,256]{2,1,0:T(8,128)S(1)}, u32[]{:S(2)}, u32[]{:S(2)}) collective-permute-start(f32[3,300,256]{2,1,0:T(8,128)S(1)} %collective-permute-done.3.else_a), channel_id=1, source_target_pairs={{0,1},{1,0},{2,3},{3,2},{4,5},{5,4},{6,7},{7,6},{8,9},{9,8},{10,11... | collective-permute-start | bytes 2764808 | tf_op jit(solution)/shard_map/ppermute | solution.py:24
  70.5 16.1 %collective-permute-start.13 = (f32[1160,128]{1,0:T(8,128)S(1)}, f32[1160,128]{1,0:T(8,128)S(1)}, u32[]{:S(2)}, u32[]{:S(2)}) collective-permute-start(f32[1160,128]{1,0:T(8,128)S(1)} %get-tuple-element.42), channel_id=1, source_target_pairs={{0,2},{1,3},{2,0},{3,1},{4,6},{5,7},{6,4},{7,5},{8,10},{9,11},{10,... | collective-permute-start | bytes 1781768 | tf_op jit(solution)/shard_map/ppermute | solution.py:24
  76.5 15.6 %all-to-all-start = ((f32[4,64,128]{2,1,0:T(8,128)}), f32[4,64,128]{2,1,0:T(8,128)S(1)}, u32[]{:S(2)}, u32[]{:S(2)}) async-start(f32[4,64,128]{2,1,0:T(8,128)} %get-tuple-element.40), calls=%async_computation | async-start | bytes 262144 | tf_op jit(solution)/shard_map/all_to_all | solution.py:336
  80.4 11.6 %collective-permute-start.11 = (f32[64,256]{1,0:T(8,128)S(1)}, f32[64,256]{1,0:T(8,128)S(1)}, u32[]{:S(2)}, u32[]{:S(2)}) collective-permute-start(f32[64,256]{1,0:T(8,128)S(1)} %get-tuple-element.38), channel_id=1, source_target_pairs={{0,13},{1,15},{2,4},{3,6},{4,17},{5,19},{6,8},{7,10},{8,21},{9,23}... | collective-permute-start | bytes 196616 | tf_op jit(solution)/shard_map/ppermute | solution.py:24
  80.4 11.7 %collective-permute-start.12 = (f32[64,256]{1,0:T(8,128)S(1)}, f32[64,256]{1,0:T(8,128)S(1)}, u32[]{:S(2)}, u32[]{:S(2)}) collective-permute-start(f32[64,256]{1,0:T(8,128)S(1)} %get-tuple-element.39), channel_id=1, source_target_pairs={{0,12},{1,14},{2,5},{3,7},{4,16},{5,18},{6,9},{7,11},{8,20},{9,22}... | collective-permute-start | bytes 196616 | tf_op jit(solution)/shard_map/ppermute | solution.py:24
  88.6 10.1 %collective-permute-start.14 = (f32[64,128]{1,0:T(8,128)S(1)}, f32[64,128]{1,0:T(8,128)S(1)}, u32[]{:S(2)}, u32[]{:S(2)}) collective-permute-start(f32[64,128]{1,0:T(8,128)S(1)} %get-tuple-element.44), channel_id=1, source_target_pairs={{0,4},{1,6},{2,5},{3,7},{4,8},{5,10},{6,9},{7,11},{8,12},{9,14},{1... | collective-permute-start | bytes 98312 | tf_op jit(solution)/shard_map/ppermute | solution.py:24
  92.0 10.5 %collective-permute-start.15 = (f32[64,128]{1,0:T(8,128)S(1)}, f32[64,128]{1,0:T(8,128)S(1)}, u32[]{:S(2)}, u32[]{:S(2)}) collective-permute-start(f32[64,128]{1,0:T(8,128)S(1)} %get-tuple-element.45), channel_id=1, source_target_pairs={{0,5},{1,7},{2,4},{3,6},{4,9},{5,11},{6,8},{7,10},{8,13},{9,15},{1... | collective-permute-start | bytes 98312 | tf_op jit(solution)/shard_map/ppermute | solution.py:24
  92.0 10.5 %collective-permute-start.16 = (f32[64,128]{1,0:T(8,128)S(1)}, f32[64,128]{1,0:T(8,128)S(1)}, u32[]{:S(2)}, u32[]{:S(2)}) collective-permute-start(f32[64,128]{1,0:T(8,128)S(1)} %get-tuple-element.46), channel_id=1, source_target_pairs={{0,12},{1,13},{2,14},{3,15},{4,16},{5,17},{6,18},{7,19},{8,20},{9,... | collective-permute-start | bytes 98312 | tf_op jit(solution)/shard_map/ppermute | solution.py:24
  92.0 10.8 %collective-permute-start.17 = (f32[64,128]{1,0:T(8,128)S(1)}, f32[64,128]{1,0:T(8,128)S(1)}, u32[]{:S(2)}, u32[]{:S(2)}) collective-permute-start(f32[64,128]{1,0:T(8,128)S(1)} %get-tuple-element.47), channel_id=1, source_target_pairs={{0,13},{1,12},{2,15},{3,14},{4,17},{5,16},{6,19},{7,18},{8,21},{9,... | collective-permute-start | bytes 98312 | tf_op jit(solution)/shard_map/ppermute | solution.py:24

commit v4 on v3

--- a/solution.py
+++ b/solution.py
@@ -160,9 +160,8 @@
     acc[...] = products(high[:, DEPTH // 2:], low[:, DEPTH // 2:], right_high[...], right_low[...])
 
 
-def near_kernel(own_count, count_one, count_three, high, low, square, first, facts, a, b, out_a, out_b, parts, right_high, right_low, acc, tile, turned):
+def near_kernel(own_count, high, low, square, first, facts, a, b, out, keep, give, own_mask, right_high, right_low, acc, tile):
     low_place, core = place_of()
-    count = jnp.where(low_place == 1, count_one[0], count_three[0])
     lanes = aligned(core, 128)
     about = facts[:, lanes]
     total, column_square = right_side((a, b), lanes, about, right_high, right_low)
@@ -179,11 +178,12 @@
             for i in range(3)
         ]
 
-    fill_tile(covariance, frames, square, column_square, own_count[0], count - core * 128, tile)
-    parts[...] = tile[...].reshape(parts.shape)
-    turned[...] = tile[...].T
-    out_a[...] = turned[aligned(1 - low_place, 64), :]
-    out_b[...] = turned[aligned(low_place, 64), :]
+    fill_tile(covariance, frames, square, column_square, own_count[0], 128, tile)
+    out[...] = tile[...].T
+    keep[...] = tile[aligned(low_place, 128), :]
+    give[...] = tile[aligned(1 - low_place, 128), :]
+    row = lax.broadcasted_iota(jnp.int32, own_mask.shape, 0) + 64 * lax.axis_index("rep")
+    own_mask[...] = jnp.where(row < own_count[0], 1.0, 0.0)
 
 
 def between_kernel(facts, near_a, near_b, else_a, else_b, mine, give, left_high, left_low, right_high, right_low, acc, here, known):
@@ -224,7 +224,7 @@
     give[1152:1160, :] = known[:, aligned(jnp.where(upper, core, 1), 128)]
 
 
-def far_kernel(count_one, count_three, mine, got, ahead_a, ahead_b, behind_a, behind_b, tile, square):
+def far_kernel(count_one, count_three, mine, got, tile, turned, other_mask, square):
     low_place, core = place_of()
     one, two = mine[1152:1160, :], got[1152:1160, :]
     row_facts = jnp.where(low_place == 1, one, two).T
@@ -245,24 +245,41 @@
     fill_tile(
         covariance, 128, square, column_facts[3:4, :], count_one[0] - core * 128, count_three[0] - low_place * 128, tile
     )
-    ahead_a[...] = tile[aligned(low_place, 64), :]
-    ahead_b[...] = tile[aligned(1 - low_place, 64), :]
-    tile[...] = tile[...].T
-    behind_a[...] = tile[aligned(core, 64), :]
-    behind_b[...] = tile[aligned(1 - core, 64), :]
-
-
-def finish_kernel(got_a, got_b, parts, ahead_a, ahead_b, behind_a, behind_b, behind, ahead):
+    turned[...] = tile[...].T
+    place = lax.broadcasted_iota(jnp.int32, other_mask.shape, 0)
+    column = lax.broadcasted_iota(jnp.int32, other_mask.shape, 1)
+    other_mask[...] = jnp.where(column < jnp.where(place == 0, count_one[0], count_three[0]), 1.0, 0.0)
+
+
+def for_core(core, near, keep, got, ahead, behind):
+    rows = aligned(core, 64)
+    upper = place_of()[0] == 1
+    one, two = keep[rows, :], got[rows, :]
+    return [near[rows, :], jnp.where(upper, one, two), jnp.where(upper, two, one), ahead[rows, :], behind[rows, :]]
+
+
+def pack_kernel(near, keep, got, ahead, behind, out):
+    out[...] = jnp.concatenate(for_core(1 - place_of()[1], near, keep, got, ahead, behind), 1)
+
+
+def finish_kernel(own_mask, other_mask, near, keep, got, far_ahead, far_behind, other, behind, ahead):
     core = place_of()[1]
-
-    def ordered(one, two):
-        return jnp.where(core == 1, two, one), jnp.where(core == 1, one, two)
-
-    behind[0], behind[2] = ordered(got_a[...], got_b[...])
-    behind[1] = jnp.concatenate(ordered(behind_a[...], behind_b[...]), 1)
-    ahead[0] = jnp.concatenate([parts[2], parts[3]], 1)
-    ahead[1] = jnp.concatenate(ordered(ahead_a[...], ahead_b[...]), 1)
-    ahead[2] = jnp.concatenate([parts[0], parts[1]], 1)
+    mine = for_core(core, near, keep, got, far_ahead, far_behind)
+    bounds = (0, 256, 384, 512, 640, 768)
+    pairs = [(here, other[:, start:stop]) for here, start, stop in zip(mine, bounds, bounds[1:])]
+    first = [jnp.where(core == 0, one, two) for one, two in pairs]
+    second = [jnp.where(core == 0, two, one) for one, two in pairs]
+    valid = own_mask[...] > 0.5
+    for at, rows in ((0, first[0]), (2, second[0])):
+        behind[at, :, 0:128] = jnp.where(valid, rows[:, 0:128], 0.0)
+        behind[at, :, 128:256] = jnp.where(valid, rows[:, 128:256], 0.0)
+    for at, place, which in ((0, 1, 0), (2, 2, 1)):
+        mask = other_mask[which:which + 1, :] > 0.5
+        ahead[at, :, 0:128] = jnp.where(mask[:, 0:128], first[place], 0.0)
+        ahead[at, :, 128:256] = jnp.where(mask[:, 128:256], second[place], 0.0)
+    for out, place in ((ahead, 3), (behind, 4)):
+        out[1, :, 0:128] = first[place]
+        out[1, :, 128:256] = second[place]
 
 
 def call(kernel, out_shapes, microseconds, scratch=()):
@@ -306,13 +323,11 @@
     own_both = route(own_chip, other_core)
     near_a_core = route(near_a, other_core)
     high, low, square = call(
-        prepare_kernel, (bf16(768, DEPTH), bf16(768, DEPTH), f32(frames, 128)), 4.0
+        prepare_kernel, (bf16(768, DEPTH), bf16(768, DEPTH), f32(frames, 128)), 0.3
     )(coords, own_core, own_chip, own_both)
     sides = [((DEPTH // 2, 384), small), ((DEPTH // 2, 384), small)]
-    near_first, facts = call(near_first_kernel, (f32(768, 384), f32(8, 256)), 4.0, sides)(high, low, near_a, near_a_core)
-    near_b, else_a, near_first, facts, count_one, count_three = together(
-        (near_b, else_a, near_first, facts, count_one, count_three)
-    )
+    near_first, facts = call(near_first_kernel, (f32(768, 384), f32(8, 256)), 0.3, sides)(high, low, near_a, near_a_core)
+    near_b, else_a, high = together((near_b, else_a, high))
 
     near_b_core = route(near_b, other_core)
     else_a_core = route(else_a, other_core)
@@ -325,30 +340,26 @@
     )(facts, near_b, near_b_core, else_a, else_a_core)
     got = route(give, other_chip)
     near_first, mine = together((near_first, mine))
-    near_out_a, near_out_b, parts = call(
+    near_out, keep, give_chip, own_mask = call(
         near_kernel,
-        (f32(64, frames), f32(64, frames), f32(4, 64, 128)),
+        (f32(128, frames), f32(128, 128), f32(128, 128), f32(64, 128)),
         4.0,
-        sides + [((768, 384), wide), ((frames, 128), wide), ((128, frames), wide)],
-    )(frame_count, count_one, count_three, high, low, square, near_first, facts, near_b, near_b_core)
-    got_a = route(near_out_a, lambda b, r: (b + 1, 2 * (r % 2)) if r >= 2 else (b + 3, 2 * (r % 2) + 1))
-    got_b = route(near_out_b, lambda b, r: (b + 1, 2 * (r % 2) + 1) if r >= 2 else (b + 3, 2 * (r % 2)))
-    parts = lax.all_to_all(parts, "rep", 0, 0)
-    got, near_out_a, near_out_b = together((got, near_out_a, near_out_b))
-
-    ahead_a, ahead_b, behind_a, behind_b = call(
-        far_kernel,
-        (f32(64, 128), f32(64, 128), f32(64, 128), f32(64, 128)),
-        1.5,
-        [((128, 128), wide), ((128, 128), wide)],
-    )(count_one, count_three, mine, got)
-    ahead_a = route(ahead_a, lambda block, rep: (block + 1, 2 * (rep % 2) + rep // 2))
-    ahead_b = route(ahead_b, lambda block, rep: (block + 1, 2 * (rep % 2) + 1 - rep // 2))
-    behind_a = route(behind_a, lambda block, rep: (block + 3, rep))
-    behind_b = route(behind_b, lambda block, rep: (block + 3, rep ^ 1))
-    return call(finish_kernel, (f32(3, 64, frames), f32(3, 64, frames)), 1.3)(
-        got_a, got_b, parts, ahead_a, ahead_b, behind_a, behind_b
+        sides + [((768, 384), wide), ((frames, 128), wide)],
+    )(frame_count, high, low, square, near_first, facts, near_b, near_b_core)
+    near_got = route(near_out, lambda b, r: (b + 1, 2 * (r % 2)) if r >= 2 else (b + 3, 2 * (r % 2) + 1))
+    keep_got = route(give_chip, other_chip)
+    got, keep, near_out = together((got, keep, near_out))
+
+    far_ahead, far_behind, other_mask = call(
+        far_kernel, (f32(128, 128), f32(128, 128), f32(8, frames)), 1.5, [((128, 128), wide)]
+    )(
+        count_one, count_three, mine, got
     )
+    far_ahead = route(far_ahead, lambda block, rep: (block + 1, 2 * (rep % 2) + rep // 2))
+    far_behind = route(far_behind, lambda block, rep: (block + 3, rep))
+    held = (near_got, keep, keep_got, far_ahead, far_behind)
+    other = route(call(pack_kernel, f32(64, 768), 0.5)(*held), other_core)
+    return call(finish_kernel, (f32(3, 64, frames), f32(3, 64, frames)), 1.3)(own_mask, other_mask, *held, other)
 
 
 def solution(mesh):

time: 104 us -> 98.5 us (0.947)
  waiting for transfers between devices: 52.1 us -> 41.6 us
  starting transfers between devices: 35 us -> 42.1 us
  Pallas kernels: 13.9 us -> 12.1 us
    ppermute x18 -> x17, starting transfers between devices: 31.1 us -> 42.1 us  [route(): return lax.ppermute(array, ('blk', 'rep'), pairs)]
    ppermute x18 -> x17, waiting for transfers between devices: 52.1 us -> 41.6 us  [route(): return lax.ppermute(array, ('blk', 'rep'), pairs)]
    all_to_all x1 -> x0, starting transfers between devices: 3.91 us -> none  [shards(): parts = lax.all_to_all(parts, 'rep', 0, 0)]
    pallas_call x6 -> x7, Pallas kernels: 13.9 us -> 12.1 us  [run(): pl.pallas_call(kernel, out_shape=out_shapes, in_specs=specs, out_specs=ja...]
  transfers between devices with their start and end apart: 19 -> 17, of which waited for: 10 -> 8; matrix products, arithmetic and copies ran while one was open for 0% -> 0% of each run, Pallas kernels for 10% -> 9%
where the time goes in v4:
time: 98.5 us; the launch traced here: 98.3 us
  starting transfers between devices  42.1 us (43%)
  waiting for transfers between devices  41.6 us (42%)
  Pallas kernels  12.1 us (12%)
  between operations  1.35 us (1%)
  local copies, waits for them, and re-layouts  1.18 us (1%)
    ppermute x17, starting transfers between devices, route(): return lax.ppermute(array, ('blk', 'rep'), pairs)  42.1 us
    ppermute x17, waiting for transfers between devices, route(): return lax.ppermute(array, ('blk', 'rep'), pairs)  41.6 us
    pallas_call x7, Pallas kernels, run(): pl.pallas_call(kernel, out_shape=out_shapes, in_specs=specs, out_specs=ja...  12.1 us
  transfers between devices with their start and end apart: 17, of which 8 were waited for; matrix products, arithmetic and copies ran while one was open for 0% of the time, Pallas kernels for 9%

profile of v4, /device:TPU:1, one launch (start us, length us, event | category | flops | bytes accessed | tf_op | source)
XLA Modules:
  0.0 98.3 jit_solution(4143334210547291712)
XLA Ops:
  0.6 2.6 %collective-permute-start = (f32[3,300,256]{2,1,0:T(8,128)}, f32[3,300,256]{2,1,0:T(8,128)S(1)}, u32[]{:S(2)}, u32[]{:S(2)}) collective-permute-start(f32[3,300,256]{2,1,0:T(8,128)} %a_ref.1), channel_id=1, source_target_pairs={{0,2},{1,3},{2,0},{3,1},{4,6},{5,7},{6,4},{7,5},{8,10},{9,11},{10,... | collective-permute-start | bytes 2764808 | tf_op jit(solution)/shard_map/ppermute | solution.py:24
  3.2 9.3 %collective-permute-start.2 = (f32[3,300,256]{2,1,0:T(8,128)}, f32[3,300,256]{2,1,0:T(8,128)S(1)}, u32[]{:S(2)}, u32[]{:S(2)}) collective-permute-start(f32[3,300,256]{2,1,0:T(8,128)} %a_ref.1), channel_id=1, source_target_pairs={{0,254},{1,255},{2,244},{3,245},{4,2},{5,3},{6,248},{7,249},{8,6},... | collective-permute-start | bytes 2764808 | tf_op jit(solution)/shard_map/ppermute | solution.py:24
  12.5 1.2 %collective-permute-start.4 = (f32[3,300,256]{2,1,0:T(8,128)}, f32[3,300,256]{2,1,0:T(8,128)S(1)}, u32[]{:S(2)}, u32[]{:S(2)}) collective-permute-start(f32[3,300,256]{2,1,0:T(8,128)} %a_ref.1), channel_id=1, source_target_pairs={{0,1},{1,0},{2,3},{3,2},{4,5},{5,4},{6,7},{7,6},{8,9},{9,8},{10,11... | collective-permute-start | bytes 2764808 | tf_op jit(solution)/shard_map/ppermute | solution.py:24
  13.7 9.1 %collective-permute-done.c_ref = f32[3,300,256]{2,1,0:T(8,128)S(1)} collective-permute-done((f32[3,300,256]{2,1,0:T(8,128)}, f32[3,300,256]{2,1,0:T(8,128)S(1)}, u32[]{:S(2)}, u32[]{:S(2)}) %collective-permute-start) | collective-permute-done | bytes 921632 | tf_op jit(solution)/shard_map/ppermute | solution.py:24
  22.9 2.2 %collective-permute-start.5 = (f32[3,300,256]{2,1,0:T(8,128)S(1)}, f32[3,300,256]{2,1,0:T(8,128)S(1)}, u32[]{:S(2)}, u32[]{:S(2)}) collective-permute-start(f32[3,300,256]{2,1,0:T(8,128)S(1)} %collective-permute-done.c_ref), channel_id=1, source_target_pairs={{0,1},{1,0},{2,3},{3,2},{4,5},{5,4},{6,7},{7,6},{8,9},{9,8},{10,11... | collective-permute-start | bytes 2764808 | tf_op jit(solution)/shard_map/ppermute | solution.py:24
  25.0 10.0 %collective-permute-start.1 = (f32[3,300,256]{2,1,0:T(8,128)S(1)}, f32[3,300,256]{2,1,0:T(8,128)S(1)}, u32[]{:S(2)}, u32[]{:S(2)}) collective-permute-start(f32[3,300,256]{2,1,0:T(8,128)S(1)} %collective-permute-done.c_ref), channel_id=1, source_target_pairs={{0,254},{1,255},{2,244},{3,245},{4,2},{5,3},{6,248},{7,249},{8,6},... | collective-permute-start | bytes 2764808 | tf_op jit(solution)/shard_map/ppermute | solution.py:24
  35.1 0.0 collective-permute-done.2.a
  35.1 0.0 collective-permute-start.3
  35.1 0.3 collective-permute-start.6
  35.4 0.0 collective-permute-done.4.b_ref
  35.4 0.0 collective-permute-done.5.d_ref
  35.4 0.0 copy-start
  35.4 1.2 %copy-done = f32[3,300,256]{2,1,0:T(8,128)S(1)} copy-done((f32[3,300,256]{2,1,0:T(8,128)S(1)}, f32[3,300,256]{2,1,0:T(8,128)}, u32[]{:S(2)}) %copy-start) | copy-done | bytes 921624
  36.6 1.4 %shard_map.41 = (bf16[768,1280]{1,0:T(8,128)(2,1)S(1)}, bf16[768,1280]{1,0:T(8,128)(2,1)S(1)}, f32[256,128]{1,0:T(8,128)S(1)}) custom-call(f32[3,300,256]{2,1,0:T(8,128)S(1)} %copy-done, f32[3,300,256]{2,1,0:T(8,128)S(1)} %collective-permute-done.4.b_ref, f32[3,300,256]{2,1,0:T(8,128)S(1)} %collective-permute-done.c_ref, ...), custom_call_target="tpu_custom_call" | custom-call | bytes 1080000 | tf_op jit(solution)/shard_map/pallas_call | solution.py:289
  38.0 17.2 %collective-permute-done.1.near_a.a = f32[3,300,256]{2,1,0:T(8,128)S(1)} collective-permute-done((f32[3,300,256]{2,1,0:T(8,128)S(1)}, f32[3,300,256]{2,1,0:T(8,128)S(1)}, u32[]{:S(2)}, u32[]{:S(2)}) %collective-permute-start.1) | collective-permute-done | bytes 921632 | tf_op jit(solution)/shard_map/ppermute | solution.py:24
  55.2 1.9 %collective-permute-done.3.else_a = f32[3,300,256]{2,1,0:T(8,128)S(1)} collective-permute-done((f32[3,300,256]{2,1,0:T(8,128)S(1)}, f32[3,300,256]{2,1,0:T(8,128)S(1)}, u32[]{:S(2)}, u32[]{:S(2)}) %collective-permute-start.3) | collective-permute-done | bytes 921632 | tf_op jit(solution)/shard_map/ppermute | solution.py:24
  57.1 1.1 %collective-permute-start.7 = (f32[3,300,256]{2,1,0:T(8,128)S(1)}, f32[3,300,256]{2,1,0:T(8,128)S(1)}, u32[]{:S(2)}, u32[]{:S(2)}) collective-permute-start(f32[3,300,256]{2,1,0:T(8,128)S(1)} %collective-permute-done.1.near_a.a), channel_id=1, source_target_pairs={{0,1},{1,0},{2,3},{3,2},{4,5},{5,4},{6,7},{7,6},{8,9},{9,8},{10,11... | collective-permute-start | bytes 2764808 | tf_op jit(solution)/shard_map/ppermute | solution.py:24
  58.2 0.0 collective-permute-start.8
  58.2 0.0 collective-permute-done.6.b
  58.2 2.3 %shard_map.42 = (f32[768,384]{1,0:T(8,128)S(1)}, f32[8,256]{1,0:T(8,128)S(1)}) custom-call(bf16[768,1280]{1,0:T(8,128)(2,1)S(1)} %get-tuple-element.24.high, bf16[768,1280]{1,0:T(8,128)(2,1)S(1)} %get-tuple-element.25.low, f32[3,300,256]{2,1,0:T(8,128)S(1)} %collective-permute-done.2.a, f32[3,300,256]{2,1,0:T(8,128)S(1)} %collective-permute-done.6.b), custom_call_target="tpu_custom_call" | custom-call | bytes 1080000 | tf_op jit(solution)/shard_map/pallas_call | solution.py:289
  60.6 0.0 collective-permute-done.7.near_b.b
  60.6 1.1 %collective-permute-done.8.else_b = f32[3,300,256]{2,1,0:T(8,128)S(1)} collective-permute-done((f32[3,300,256]{2,1,0:T(8,128)S(1)}, f32[3,300,256]{2,1,0:T(8,128)S(1)}, u32[]{:S(2)}, u32[]{:S(2)}) %collective-permute-start.8) | collective-permute-done | bytes 921632 | tf_op jit(solution)/shard_map/ppermute | solution.py:24
  61.7 2.6 %shard_map.43 = (f32[1160,128]{1,0:T(8,128)S(1)}, f32[1160,128]{1,0:T(8,128)S(1)}) custom-call(f32[8,256]{1,0:T(8,128)S(1)} %get-tuple-element.28.facts, f32[3,300,256]{2,1,0:T(8,128)S(1)} %collective-permute-done.1.near_a.a, f32[3,300,256]{2,1,0:T(8,128)S(1)} %collective-permute-done.7.near_b.b, f32[3,300,256]{2,1,0:T(8,128)S(1)} %collective-permute-done.3.else_a, ...), custom_call_target="tpu_custom_call" | custom-call | bytes 10800000 | tf_op jit(solution)/shard_map/pallas_call | solution.py:289
  64.3 0.3 collective-permute-start.11
  65.2 3.0 %shard_map.44 = (f32[128,256]{1,0:T(8,128)S(1)}, f32[128,128]{1,0:T(8,128)S(1)}, f32[128,128]{1,0:T(8,128)S(1)}, f32[64,128]{1,0:T(8,128)S(1)}) custom-call(s32[1]{0:T(128)S(6)} %copy.4.own_count, bf16[768,1280]{1,0:T(8,128)(2,1)S(1)} %get-tuple-element.24.high, bf16[768,1280]{1,0:T(8,128)(2,1)S(1)} %get-tuple-element.25.low, ...), custom_call_target="tpu_custom_call" | custom-call | bytes 14400000 | tf_op jit(solution)/shard_map/pallas_call | solution.py:289
  68.2 0.1 collective-permute-start.12
  68.3 6.8 %collective-permute-start.10 = (s32[1]{0:T(128)}, s32[1]{0:T(128)}, u32[]{:S(2)}, u32[]{:S(2)}) collective-permute-start(s32[1]{0:T(128)} %param.3), channel_id=1, source_target_pairs={{0,244},{1,245},{2,246},{3,247},{4,248},{5,249},{6,250},{7,251},{8... | collective-permute-start | bytes 20 | tf_op jit(solution)/shard_map/ppermute | solution.py:24
  75.1 2.1 %collective-permute-start.9 = (s32[1]{0:T(128)}, s32[1]{0:T(128)}, u32[]{:S(2)}, u32[]{:S(2)}) collective-permute-start(s32[1]{0:T(128)} %param.3), channel_id=1, source_target_pairs={{0,252},{1,253},{2,254},{3,255},{4,0},{5,1},{6,2},{7,3},{8,4},{9,5... | collective-permute-start | bytes 20 | tf_op jit(solution)/shard_map/ppermute | solution.py:24
  77.3 0.8 collective-permute-start.13
  78.0 2.6 %collective-permute-done.11.got = f32[1160,128]{1,0:T(8,128)S(1)} collective-permute-done((f32[1160,128]{1,0:T(8,128)S(1)}, f32[1160,128]{1,0:T(8,128)S(1)}, u32[]{:S(2)}, u32[]{:S(2)}) %collective-permute-start.11) | collective-permute-done | bytes 593952 | tf_op jit(solution)/shard_map/ppermute | solution.py:24
  80.6 0.0 collective-permute-done.10.count_three
  80.6 0.0 collective-permute-done.9.count_one
  80.6 1.9 %shard_map.45 = (f32[128,128]{1,0:T(8,128)S(1)}, f32[128,128]{1,0:T(8,128)S(1)}, f32[8,256]{1,0:T(8,128)S(1)}) custom-call(s32[1]{0:T(128)} %collective-permute-done.9.count_one, s32[1]{0:T(128)} %collective-permute-done.10.count_three, f32[1160,128]{1,0:T(8,128)S(1)} %get-tuple-element.34.mine, f32[1160,128]{1,0:T(8,128)S(1)} %collective-permute-done.11.got), custom_call_target="tpu_custom_call" | custom-call | bytes 5400000 | tf_op jit(solution)/shard_map/pallas_call | solution.py:289
  82.5 3.5 %collective-permute-start.14 = (f32[128,128]{1,0:T(8,128)S(1)}, f32[128,128]{1,0:T(8,128)S(1)}, u32[]{:S(2)}, u32[]{:S(2)}) collective-permute-start(f32[128,128]{1,0:T(8,128)S(1)} %get-tuple-element.42), channel_id=1, source_target_pairs={{0,4},{1,6},{2,5},{3,7},{4,8},{5,10},{6,9},{7,11},{8,12},{9,14},{1... | collective-permute-start | bytes 196616 | tf_op jit(solution)/shard_map/ppermute | solution.py:24
  86.1 0.0 collective-permute-start.15
  86.1 0.0 collective-permute-done.13.got
  86.1 0.0 collective-permute-done.12.near
  86.1 6.8 %collective-permute-done.14.ahead.far_ahead = f32[128,128]{1,0:T(8,128)S(1)} collective-permute-done((f32[128,128]{1,0:T(8,128)S(1)}, f32[128,128]{1,0:T(8,128)S(1)}, u32[]{:S(2)}, u32[]{:S(2)}) %collective-permute-start.14) | collective-permute-done | bytes 65568 | tf_op jit(solution)/shard_map/ppermute | solution.py:24
  92.9 1.8 %collective-permute-done.15.behind.far_behind = f32[128,128]{1,0:T(8,128)S(1)} collective-permute-done((f32[128,128]{1,0:T(8,128)S(1)}, f32[128,128]{1,0:T(8,128)S(1)}, u32[]{:S(2)}, u32[]{:S(2)}) %collective-permute-start.15) | collective-permute-done | bytes 65568 | tf_op jit(solution)/shard_map/ppermute | solution.py:24
  94.7 1.8 %collective-permute-start.16 = (f32[64,768]{1,0:T(8,128)S(1)}, f32[64,768]{1,0:T(8,128)S(1)}, u32[]{:S(2)}, u32[]{:S(2)}) collective-permute-start(f32[64,768]{1,0:T(8,128)S(1)} %shard_map.46), channel_id=1, source_target_pairs={{0,1},{1,0},{2,3},{3,2},{4,5},{5,4},{6,7},{7,6},{8,9},{9,8},{10,11... | collective-permute-start | bytes 589832 | tf_op jit(solution)/shard_map/ppermute | solution.py:24
  96.5 1.1 %collective-permute-done.16.other = f32[64,768]{1,0:T(8,128)S(1)} collective-permute-done((f32[64,768]{1,0:T(8,128)S(1)}, f32[64,768]{1,0:T(8,128)S(1)}, u32[]{:S(2)}, u32[]{:S(2)}) %collective-permute-start.16) | collective-permute-done | bytes 196640 | tf_op jit(solution)/shard_map/ppermute | solution.py:24
  97.6 0.8 shard_map.47
  (1 shorter events, 0.0 us)
Async XLA Ops:
  0.6 22.2 %collective-permute-start = (f32[3,300,256]{2,1,0:T(8,128)}, f32[3,300,256]{2,1,0:T(8,128)S(1)}, u32[]{:S(2)}, u32[]{:S(2)}) collective-permute-start(f32[3,300,256]{2,1,0:T(8,128)} %a_ref.1), channel_id=1, source_target_pairs={{0,2},{1,3},{2,0},{3,1},{4,6},{5,7},{6,4},{7,5},{8,10},{9,11},{10,... | collective-permute-start | bytes 2764808 | tf_op jit(solution)/shard_map/ppermute | solution.py:24
  3.2 31.9 %collective-permute-start.2 = (f32[3,300,256]{2,1,0:T(8,128)}, f32[3,300,256]{2,1,0:T(8,128)S(1)}, u32[]{:S(2)}, u32[]{:S(2)}) collective-permute-start(f32[3,300,256]{2,1,0:T(8,128)} %a_ref.1), channel_id=1, source_target_pairs={{0,254},{1,255},{2,244},{3,245},{4,2},{5,3},{6,248},{7,249},{8,6},... | collective-permute-start | bytes 2764808 | tf_op jit(solution)/shard_map/ppermute | solution.py:24
  12.5 22.9 %collective-permute-start.4 = (f32[3,300,256]{2,1,0:T(8,128)}, f32[3,300,256]{2,1,0:T(8,128)S(1)}, u32[]{:S(2)}, u32[]{:S(2)}) collective-permute-start(f32[3,300,256]{2,1,0:T(8,128)} %a_ref.1), channel_id=1, source_target_pairs={{0,1},{1,0},{2,3},{3,2},{4,5},{5,4},{6,7},{7,6},{8,9},{9,8},{10,11... | collective-permute-start | bytes 2764808 | tf_op jit(solution)/shard_map/ppermute | solution.py:24
  22.9 12.5 %collective-permute-start.5 = (f32[3,300,256]{2,1,0:T(8,128)S(1)}, f32[3,300,256]{2,1,0:T(8,128)S(1)}, u32[]{:S(2)}, u32[]{:S(2)}) collective-permute-start(f32[3,300,256]{2,1,0:T(8,128)S(1)} %collective-permute-done.c_ref), channel_id=1, source_target_pairs={{0,1},{1,0},{2,3},{3,2},{4,5},{5,4},{6,7},{7,6},{8,9},{9,8},{10,11... | collective-permute-start | bytes 2764808 | tf_op jit(solution)/shard_map/ppermute | solution.py:24
  25.0 30.2 %collective-permute-start.1 = (f32[3,300,256]{2,1,0:T(8,128)S(1)}, f32[3,300,256]{2,1,0:T(8,128)S(1)}, u32[]{:S(2)}, u32[]{:S(2)}) collective-permute-start(f32[3,300,256]{2,1,0:T(8,128)S(1)} %collective-permute-done.c_ref), channel_id=1, source_target_pairs={{0,254},{1,255},{2,244},{3,245},{4,2},{5,3},{6,248},{7,249},{8,6},... | collective-permute-start | bytes 2764808 | tf_op jit(solution)/shard_map/ppermute | solution.py:24
  35.1 22.0 %collective-permute-start.3 = (f32[3,300,256]{2,1,0:T(8,128)S(1)}, f32[3,300,256]{2,1,0:T(8,128)S(1)}, u32[]{:S(2)}, u32[]{:S(2)}) collective-permute-start(f32[3,300,256]{2,1,0:T(8,128)S(1)} %collective-permute-done.2.a), channel_id=1, source_target_pairs={{0,2},{1,3},{2,0},{3,1},{4,6},{5,7},{6,4},{7,5},{8,10},{9,11},{10,... | collective-permute-start | bytes 2764808 | tf_op jit(solution)/shard_map/ppermute | solution.py:24
  35.1 23.1 %collective-permute-start.6 = (f32[3,300,256]{2,1,0:T(8,128)S(1)}, f32[3,300,256]{2,1,0:T(8,128)S(1)}, u32[]{:S(2)}, u32[]{:S(2)}) collective-permute-start(f32[3,300,256]{2,1,0:T(8,128)S(1)} %collective-permute-done.2.a), channel_id=1, source_target_pairs={{0,1},{1,0},{2,3},{3,2},{4,5},{5,4},{6,7},{7,6},{8,9},{9,8},{10,11... | collective-permute-start | bytes 2764808 | tf_op jit(solution)/shard_map/ppermute | solution.py:24
  35.4 1.2 %copy-start = (f32[3,300,256]{2,1,0:T(8,128)S(1)}, f32[3,300,256]{2,1,0:T(8,128)}, u32[]{:S(2)}) copy-start(f32[3,300,256]{2,1,0:T(8,128)} %a_ref.1) | copy-start | bytes 2764804
  57.1 3.4 %collective-permute-start.7 = (f32[3,300,256]{2,1,0:T(8,128)S(1)}, f32[3,300,256]{2,1,0:T(8,128)S(1)}, u32[]{:S(2)}, u32[]{:S(2)}) collective-permute-start(f32[3,300,256]{2,1,0:T(8,128)S(1)} %collective-permute-done.1.near_a.a), channel_id=1, source_target_pairs={{0,1},{1,0},{2,3},{3,2},{4,5},{5,4},{6,7},{7,6},{8,9},{9,8},{10,11... | collective-permute-start | bytes 2764808 | tf_op jit(solution)/shard_map/ppermute | solution.py:24
  58.2 3.5 %collective-permute-start.8 = (f32[3,300,256]{2,1,0:T(8,128)S(1)}, f32[3,300,256]{2,1,0:T(8,128)S(1)}, u32[]{:S(2)}, u32[]{:S(2)}) collective-permute-start(f32[3,300,256]{2,1,0:T(8,128)S(1)} %collective-permute-done.3.else_a), channel_id=1, source_target_pairs={{0,1},{1,0},{2,3},{3,2},{4,5},{5,4},{6,7},{7,6},{8,9},{9,8},{10,11... | collective-permute-start | bytes 2764808 | tf_op jit(solution)/shard_map/ppermute | solution.py:24
  64.3 16.3 %collective-permute-start.11 = (f32[1160,128]{1,0:T(8,128)S(1)}, f32[1160,128]{1,0:T(8,128)S(1)}, u32[]{:S(2)}, u32[]{:S(2)}) collective-permute-start(f32[1160,128]{1,0:T(8,128)S(1)} %get-tuple-element.35), channel_id=1, source_target_pairs={{0,2},{1,3},{2,0},{3,1},{4,6},{5,7},{6,4},{7,5},{8,10},{9,11},{10,... | collective-permute-start | bytes 1781768 | tf_op jit(solution)/shard_map/ppermute | solution.py:24
  68.2 17.9 %collective-permute-start.12 = (f32[128,256]{1,0:T(8,128)S(1)}, f32[128,256]{1,0:T(8,128)S(1)}, u32[]{:S(2)}, u32[]{:S(2)}) collective-permute-start(f32[128,256]{1,0:T(8,128)S(1)} %get-tuple-element.37), channel_id=1, source_target_pairs={{0,13},{1,15},{2,4},{3,6},{4,17},{5,19},{6,8},{7,10},{8,21},{9,23}... | collective-permute-start | bytes 393224 | tf_op jit(solution)/shard_map/ppermute | solution.py:24
  68.3 12.3 %collective-permute-start.10 = (s32[1]{0:T(128)}, s32[1]{0:T(128)}, u32[]{:S(2)}, u32[]{:S(2)}) collective-permute-start(s32[1]{0:T(128)} %param.3), channel_id=1, source_target_pairs={{0,244},{1,245},{2,246},{3,247},{4,248},{5,249},{6,250},{7,251},{8... | collective-permute-start | bytes 20 | tf_op jit(solution)/shard_map/ppermute | solution.py:24
  75.1 5.5 %collective-permute-start.9 = (s32[1]{0:T(128)}, s32[1]{0:T(128)}, u32[]{:S(2)}, u32[]{:S(2)}) collective-permute-start(s32[1]{0:T(128)} %param.3), channel_id=1, source_target_pairs={{0,252},{1,253},{2,254},{3,255},{4,0},{5,1},{6,2},{7,3},{8,4},{9,5... | collective-permute-start | bytes 20 | tf_op jit(solution)/shard_map/ppermute | solution.py:24
  77.3 8.8 %collective-permute-start.13 = (f32[128,128]{1,0:T(8,128)S(1)}, f32[128,128]{1,0:T(8,128)S(1)}, u32[]{:S(2)}, u32[]{:S(2)}) collective-permute-start(f32[128,128]{1,0:T(8,128)S(1)} %get-tuple-element.41), channel_id=1, source_target_pairs={{0,2},{1,3},{2,0},{3,1},{4,6},{5,7},{6,4},{7,5},{8,10},{9,11},{10,... | collective-permute-start | bytes 196616 | tf_op jit(solution)/shard_map/ppermute | solution.py:24
  82.5 10.3 %collective-permute-start.14 = (f32[128,128]{1,0:T(8,128)S(1)}, f32[128,128]{1,0:T(8,128)S(1)}, u32[]{:S(2)}, u32[]{:S(2)}) collective-permute-start(f32[128,128]{1,0:T(8,128)S(1)} %get-tuple-element.42), channel_id=1, source_target_pairs={{0,4},{1,6},{2,5},{3,7},{4,8},{5,10},{6,9},{7,11},{8,12},{9,14},{1... | collective-permute-start | bytes 196616 | tf_op jit(solution)/shard_map/ppermute | solution.py:24
  86.1 8.7 %collective-permute-start.15 = (f32[128,128]{1,0:T(8,128)S(1)}, f32[128,128]{1,0:T(8,128)S(1)}, u32[]{:S(2)}, u32[]{:S(2)}) collective-permute-start(f32[128,128]{1,0:T(8,128)S(1)} %get-tuple-element.43), channel_id=1, source_target_pairs={{0,12},{1,13},{2,14},{3,15},{4,16},{5,17},{6,18},{7,19},{8,20},{9,... | collective-permute-start | bytes 196616 | tf_op jit(solution)/shard_map/ppermute | solution.py:24
  94.7 2.8 %collective-permute-start.16 = (f32[64,768]{1,0:T(8,128)S(1)}, f32[64,768]{1,0:T(8,128)S(1)}, u32[]{:S(2)}, u32[]{:S(2)}) collective-permute-start(f32[64,768]{1,0:T(8,128)S(1)} %shard_map.46), channel_id=1, source_target_pairs={{0,1},{1,0},{2,3},{3,2},{4,5},{5,4},{6,7},{7,6},{8,9},{9,8},{10,11... | collective-permute-start | bytes 589832 | tf_op jit(solution)/shard_map/ppermute | solution.py:24

commit v5 on v4

--- a/solution.py
+++ b/solution.py
@@ -118,15 +118,13 @@
     square_ref[...] = jnp.broadcast_to(square / NATOM, square_ref.shape)
 
 
-def fill_tile(covariance, rows, row_square, column_square, row_limit, column_limit, tile):
+def fill_tile(covariance, rows, row_square, column_square, valid, tile):
     step = 16
-    column_valid = lax.broadcasted_iota(jnp.int32, (step, 128), 1) < column_limit
+    column = lax.broadcasted_iota(jnp.int32, (step, 128), 1)
     for at in range(0, rows, step):
         place = lax.broadcasted_iota(jnp.int32, (step, 128), 0) + at
         total = row_square[at:at + step, :] + column_square
-        tile[at:at + step, :] = jnp.where(
-            (place < row_limit) & column_valid, deviation(covariance(at, at + step), total), 0.0
-        )
+        tile[at:at + step, :] = jnp.where(valid(place, column), deviation(covariance(at, at + step), total), 0.0)
 
 
 def right_side(refs, lanes, about, right_high, right_low):
@@ -153,8 +151,9 @@
     out[4:8, :] = jnp.zeros((4, out.shape[1]), jnp.float32)
 
 
-def near_first_kernel(high, low, a, b, acc, facts, right_high, right_low):
+def near_first_kernel(count, high, low, a, b, acc, facts, right_high, right_low):
     half_facts((a, b), facts)
+    facts[4:5, :] = jnp.full((1, facts.shape[1]), count[0], jnp.int32).astype(jnp.float32)
     lanes = aligned(place_of()[1], 128)
     right_side((a, b), lanes, facts[:, lanes], right_high, right_low)
     acc[...] = products(high[:, DEPTH // 2:], low[:, DEPTH // 2:], right_high[...], right_low[...])
@@ -178,7 +177,7 @@
             for i in range(3)
         ]
 
-    fill_tile(covariance, frames, square, column_square, own_count[0], 128, tile)
+    fill_tile(covariance, frames, square, column_square, lambda row, column: row < own_count[0], tile)
     out[...] = tile[...].T
     keep[...] = tile[aligned(low_place, 128), :]
     give[...] = tile[aligned(1 - low_place, 128), :]
@@ -197,6 +196,7 @@
         known[comp:comp + 1, :] = sign * apart
         square = square + (NATOM / 4) * apart * apart
     known[3:4, :] = square / NATOM
+    known[4:5, :] = facts[4:5, :]
     upper = low_place == 1
     lanes = aligned(core, 128)
     for comp in range(3):
@@ -224,7 +224,7 @@
     give[1152:1160, :] = known[:, aligned(jnp.where(upper, core, 1), 128)]
 
 
-def far_kernel(count_one, count_three, mine, got, tile, turned, other_mask, square):
+def far_kernel(mine, got, tile, turned, other_mask, square):
     low_place, core = place_of()
     one, two = mine[1152:1160, :], got[1152:1160, :]
     row_facts = jnp.where(low_place == 1, one, two).T
@@ -242,13 +242,22 @@
             for i in range(3)
         ]
 
-    fill_tile(
-        covariance, 128, square, column_facts[3:4, :], count_one[0] - core * 128, count_three[0] - low_place * 128, tile
-    )
+    count_one = jnp.where(low_place == 1, one, two)[4:5, :]
+    count_three = column_facts[4:5, :]
+
+    def valid(row, column):
+        row_valid = (row + core * 128).astype(jnp.float32) < count_one
+        return row_valid & ((column + low_place * 128).astype(jnp.float32) < count_three)
+
+    fill_tile(covariance, 128, square, column_facts[3:4, :], valid, tile)
     turned[...] = tile[...].T
-    place = lax.broadcasted_iota(jnp.int32, other_mask.shape, 0)
-    column = lax.broadcasted_iota(jnp.int32, other_mask.shape, 1)
-    other_mask[...] = jnp.where(column < jnp.where(place == 0, count_one[0], count_three[0]), 1.0, 0.0)
+    for which, count in ((0, count_one), (1, count_three)):
+        for half in range(2):
+            column = lax.broadcasted_iota(jnp.int32, (1, 128), 1) + half * 128
+            other_mask[which:which + 1, half * 128:half * 128 + 128] = jnp.where(
+                column.astype(jnp.float32) < count, 1.0, 0.0
+            )
+    other_mask[2:8, :] = jnp.zeros((6, other_mask.shape[1]), jnp.float32)
 
 
 def for_core(core, near, keep, got, ahead, behind):
@@ -315,8 +324,7 @@
     own_chip = route(coords, other_chip)
     near_a = route(coords, to_neighbour)
     own_core = route(coords, other_core)
-    count_one = route(frame_count, lambda block, rep: (block - 1, rep))
-    count_three = route(frame_count, lambda block, rep: (block - 3, rep))
+    near_count = route(frame_count, to_neighbour)
 
     near_b = route(own_chip, to_neighbour)
     else_a = route(near_a, other_chip)
@@ -326,9 +334,10 @@
         prepare_kernel, (bf16(768, DEPTH), bf16(768, DEPTH), f32(frames, 128)), 0.3
     )(coords, own_core, own_chip, own_both)
     sides = [((DEPTH // 2, 384), small), ((DEPTH // 2, 384), small)]
-    near_first, facts = call(near_first_kernel, (f32(768, 384), f32(8, 256)), 0.3, sides)(high, low, near_a, near_a_core)
-    near_b, else_a, high = together((near_b, else_a, high))
-
+    near_b, high, near_count = together((near_b, high, near_count))
+    near_first, facts = call(near_first_kernel, (f32(768, 384), f32(8, 256)), 0.3, sides)(
+        near_count, high, low, near_a, near_a_core
+    )
     near_b_core = route(near_b, other_core)
     else_a_core = route(else_a, other_core)
     mine, give = call(
@@ -352,9 +361,7 @@
 
     far_ahead, far_behind, other_mask = call(
         far_kernel, (f32(128, 128), f32(128, 128), f32(8, frames)), 1.5, [((128, 128), wide)]
-    )(
-        count_one, count_three, mine, got
-    )
+    )(mine, got)
     far_ahead = route(far_ahead, lambda block, rep: (block + 1, 2 * (rep % 2) + rep // 2))
     far_behind = route(far_behind, lambda block, rep: (block + 3, rep))
     held = (near_got, keep, keep_got, far_ahead, far_behind)

time: 98.5 us -> 96.4 us (0.979)
  starting transfers between devices: 42.1 us -> 39.7 us
  waiting for transfers between devices: 41.6 us -> 42.6 us
    ppermute x17 -> x16, starting transfers between devices: 42.1 us -> 39.7 us  [route(): return lax.ppermute(array, ('blk', 'rep'), pairs)]
    ppermute x17 -> x16, waiting for transfers between devices: 41.6 us -> 42.6 us  [route(): return lax.ppermute(array, ('blk', 'rep'), pairs)]
  transfers between devices with their start and end apart: 17 -> 16, of which waited for: 8 -> 7; matrix products, arithmetic and copies ran while one was open for 0% -> 0% of each run, Pallas kernels for 9% -> 8%
where the time goes in v5:
time: 96.4 us; the launch traced here: 96.3 us
  waiting for transfers between devices  42.6 us (44%)
  starting transfers between devices  39.7 us (41%)
  Pallas kernels  11.5 us (12%)
  between operations  1.35 us (1%)
  local copies, waits for them, and re-layouts  1.19 us (1%)
    ppermute x16, waiting for transfers between devices, route(): return lax.ppermute(array, ('blk', 'rep'), pairs)  42.6 us
    ppermute x16, starting transfers between devices, route(): return lax.ppermute(array, ('blk', 'rep'), pairs)  39.7 us
    pallas_call x7, Pallas kernels, run(): pl.pallas_call(kernel, out_shape=out_shapes, in_specs=specs, out_specs=ja...  11.5 us
  transfers between devices with their start and end apart: 16, of which 7 were waited for; matrix products, arithmetic and copies ran while one was open for 0% of the time, Pallas kernels for 8%

profile of v5, /device:TPU:1, one launch (start us, length us, event | category | flops | bytes accessed | tf_op | source)
XLA Modules:
  0.0 96.3 jit_solution(6771392556266506758)
XLA Ops:
  0.6 2.6 %collective-permute-start = (f32[3,300,256]{2,1,0:T(8,128)}, f32[3,300,256]{2,1,0:T(8,128)S(1)}, u32[]{:S(2)}, u32[]{:S(2)}) collective-permute-start(f32[3,300,256]{2,1,0:T(8,128)} %a_ref.1), channel_id=1, source_target_pairs={{0,2},{1,3},{2,0},{3,1},{4,6},{5,7},{6,4},{7,5},{8,10},{9,11},{10,... | collective-permute-start | bytes 2764808 | tf_op jit(solution)/shard_map/ppermute | solution.py:24
  3.2 9.3 %collective-permute-start.5 = (f32[3,300,256]{2,1,0:T(8,128)}, f32[3,300,256]{2,1,0:T(8,128)S(1)}, u32[]{:S(2)}, u32[]{:S(2)}) collective-permute-start(f32[3,300,256]{2,1,0:T(8,128)} %a_ref.1), channel_id=1, source_target_pairs={{0,254},{1,255},{2,244},{3,245},{4,2},{5,3},{6,248},{7,249},{8,6},... | collective-permute-start | bytes 2764808 | tf_op jit(solution)/shard_map/ppermute | solution.py:24
  12.5 1.2 %collective-permute-start.2 = (f32[3,300,256]{2,1,0:T(8,128)}, f32[3,300,256]{2,1,0:T(8,128)S(1)}, u32[]{:S(2)}, u32[]{:S(2)}) collective-permute-start(f32[3,300,256]{2,1,0:T(8,128)} %a_ref.1), channel_id=1, source_target_pairs={{0,1},{1,0},{2,3},{3,2},{4,5},{5,4},{6,7},{7,6},{8,9},{9,8},{10,11... | collective-permute-start | bytes 2764808 | tf_op jit(solution)/shard_map/ppermute | solution.py:24
  13.7 9.1 %collective-permute-done.c_ref = f32[3,300,256]{2,1,0:T(8,128)S(1)} collective-permute-done((f32[3,300,256]{2,1,0:T(8,128)}, f32[3,300,256]{2,1,0:T(8,128)S(1)}, u32[]{:S(2)}, u32[]{:S(2)}) %collective-permute-start) | collective-permute-done | bytes 921632 | tf_op jit(solution)/shard_map/ppermute | solution.py:24
  22.9 2.2 %collective-permute-start.3 = (f32[3,300,256]{2,1,0:T(8,128)S(1)}, f32[3,300,256]{2,1,0:T(8,128)S(1)}, u32[]{:S(2)}, u32[]{:S(2)}) collective-permute-start(f32[3,300,256]{2,1,0:T(8,128)S(1)} %collective-permute-done.c_ref), channel_id=1, source_target_pairs={{0,1},{1,0},{2,3},{3,2},{4,5},{5,4},{6,7},{7,6},{8,9},{9,8},{10,11... | collective-permute-start | bytes 2764808 | tf_op jit(solution)/shard_map/ppermute | solution.py:24
  25.0 10.0 %collective-permute-start.1 = (f32[3,300,256]{2,1,0:T(8,128)S(1)}, f32[3,300,256]{2,1,0:T(8,128)S(1)}, u32[]{:S(2)}, u32[]{:S(2)}) collective-permute-start(f32[3,300,256]{2,1,0:T(8,128)S(1)} %collective-permute-done.c_ref), channel_id=1, source_target_pairs={{0,254},{1,255},{2,244},{3,245},{4,2},{5,3},{6,248},{7,249},{8,6},... | collective-permute-start | bytes 2764808 | tf_op jit(solution)/shard_map/ppermute | solution.py:24
  35.1 0.0 collective-permute-done.5.a
  35.1 0.0 collective-permute-start.8
  35.1 4.3 %collective-permute-start.4 = (s32[1]{0:T(128)}, s32[1]{0:T(128)}, u32[]{:S(2)}, u32[]{:S(2)}) collective-permute-start(s32[1]{0:T(128)} %param.3), channel_id=1, source_target_pairs={{0,254},{1,255},{2,244},{3,245},{4,2},{5,3},{6,248},{7,249},{8,6},... | collective-permute-start | bytes 20 | tf_op jit(solution)/shard_map/ppermute | solution.py:24
  39.4 0.0 collective-permute-done.2.b_ref
  39.4 2.1 %collective-permute-start.6 = (f32[3,300,256]{2,1,0:T(8,128)S(1)}, f32[3,300,256]{2,1,0:T(8,128)S(1)}, u32[]{:S(2)}, u32[]{:S(2)}) collective-permute-start(f32[3,300,256]{2,1,0:T(8,128)S(1)} %collective-permute-done.5.a), channel_id=1, source_target_pairs={{0,1},{1,0},{2,3},{3,2},{4,5},{5,4},{6,7},{7,6},{8,9},{9,8},{10,11... | collective-permute-start | bytes 2764808 | tf_op jit(solution)/shard_map/ppermute | solution.py:24
  41.5 0.0 collective-permute-done.3.d_ref
  41.5 0.0 copy-start
  41.5 1.2 %copy-done = f32[3,300,256]{2,1,0:T(8,128)S(1)} copy-done((f32[3,300,256]{2,1,0:T(8,128)S(1)}, f32[3,300,256]{2,1,0:T(8,128)}, u32[]{:S(2)}) %copy-start) | copy-done | bytes 921624
  42.7 1.4 %shard_map.41 = (bf16[768,1280]{1,0:T(8,128)(2,1)S(1)}, bf16[768,1280]{1,0:T(8,128)(2,1)S(1)}, f32[256,128]{1,0:T(8,128)S(1)}) custom-call(f32[3,300,256]{2,1,0:T(8,128)S(1)} %copy-done, f32[3,300,256]{2,1,0:T(8,128)S(1)} %collective-permute-done.2.b_ref, f32[3,300,256]{2,1,0:T(8,128)S(1)} %collective-permute-done.c_ref, ...), custom_call_target="tpu_custom_call" | custom-call | bytes 1080000 | tf_op jit(solution)/shard_map/pallas_call | solution.py:298
  44.2 11.1 %collective-permute-done.4.count = s32[1]{0:T(128)} collective-permute-done((s32[1]{0:T(128)}, s32[1]{0:T(128)}, u32[]{:S(2)}, u32[]{:S(2)}) %collective-permute-start.4) | collective-permute-done | bytes 36 | tf_op jit(solution)/shard_map/ppermute | solution.py:24
  55.3 0.0 collective-permute-done.1.near_a.a
  55.3 0.8 collective-permute-start.7
  56.1 1.1 %collective-permute-done.8.else_a = f32[3,300,256]{2,1,0:T(8,128)S(1)} collective-permute-done((f32[3,300,256]{2,1,0:T(8,128)S(1)}, f32[3,300,256]{2,1,0:T(8,128)S(1)}, u32[]{:S(2)}, u32[]{:S(2)}) %collective-permute-start.8) | collective-permute-done | bytes 921632 | tf_op jit(solution)/shard_map/ppermute | solution.py:24
  57.1 1.1 %collective-permute-start.9 = (f32[3,300,256]{2,1,0:T(8,128)S(1)}, f32[3,300,256]{2,1,0:T(8,128)S(1)}, u32[]{:S(2)}, u32[]{:S(2)}) collective-permute-start(f32[3,300,256]{2,1,0:T(8,128)S(1)} %collective-permute-done.8.else_a), channel_id=1, source_target_pairs={{0,1},{1,0},{2,3},{3,2},{4,5},{5,4},{6,7},{7,6},{8,9},{9,8},{10,11... | collective-permute-start | bytes 2764808 | tf_op jit(solution)/shard_map/ppermute | solution.py:24
  58.2 0.0 collective-permute-done.6.b
  58.2 2.9 %shard_map.42 = (f32[768,384]{1,0:T(8,128)S(1)}, f32[8,256]{1,0:T(8,128)S(1)}) custom-call(s32[1]{0:T(128)} %collective-permute-done.4.count, bf16[768,1280]{1,0:T(8,128)(2,1)S(1)} %get-tuple-element.24.high, bf16[768,1280]{1,0:T(8,128)(2,1)S(1)} %get-tuple-element.25.low, f32[3,300,256]{2,1,0:T(8,128)S(1)} %collective-permute-done.5.a, ...), custom_call_target="tpu_custom_call" | custom-call | bytes 1080000 | tf_op jit(solution)/shard_map/pallas_call | solution.py:298
  61.2 0.0 collective-permute-done.7.near_b.b
  61.2 0.0 collective-permute-done.9.else_b
  61.2 2.6 %shard_map.43 = (f32[1160,128]{1,0:T(8,128)S(1)}, f32[1160,128]{1,0:T(8,128)S(1)}) custom-call(f32[8,256]{1,0:T(8,128)S(1)} %get-tuple-element.29.facts, f32[3,300,256]{2,1,0:T(8,128)S(1)} %collective-permute-done.1.near_a.a, f32[3,300,256]{2,1,0:T(8,128)S(1)} %collective-permute-done.7.near_b.b, f32[3,300,256]{2,1,0:T(8,128)S(1)} %collective-permute-done.8.else_a, ...), custom_call_target="tpu_custom_call" | custom-call | bytes 10800000 | tf_op jit(solution)/shard_map/pallas_call | solution.py:298
  63.8 0.3 collective-permute-start.10
  64.7 3.0 %shard_map.44 = (f32[128,256]{1,0:T(8,128)S(1)}, f32[128,128]{1,0:T(8,128)S(1)}, f32[128,128]{1,0:T(8,128)S(1)}, f32[64,128]{1,0:T(8,128)S(1)}) custom-call(s32[1]{0:T(128)S(6)} %copy.4.own_count, bf16[768,1280]{1,0:T(8,128)(2,1)S(1)} %get-tuple-element.24.high, bf16[768,1280]{1,0:T(8,128)(2,1)S(1)} %get-tuple-element.25.low, ...), custom_call_target="tpu_custom_call" | custom-call | bytes 14400000 | tf_op jit(solution)/shard_map/pallas_call | solution.py:298
  67.8 0.1 collective-permute-start.11
  67.9 2.0 %collective-permute-start.12 = (f32[128,128]{1,0:T(8,128)S(1)}, f32[128,128]{1,0:T(8,128)S(1)}, u32[]{:S(2)}, u32[]{:S(2)}) collective-permute-start(f32[128,128]{1,0:T(8,128)S(1)} %get-tuple-element.41), channel_id=1, source_target_pairs={{0,2},{1,3},{2,0},{3,1},{4,6},{5,7},{6,4},{7,5},{8,10},{9,11},{10,... | collective-permute-start | bytes 196616 | tf_op jit(solution)/shard_map/ppermute | solution.py:24
  69.9 10.7 %collective-permute-done.10.got = f32[1160,128]{1,0:T(8,128)S(1)} collective-permute-done((f32[1160,128]{1,0:T(8,128)S(1)}, f32[1160,128]{1,0:T(8,128)S(1)}, u32[]{:S(2)}, u32[]{:S(2)}) %collective-permute-start.10) | collective-permute-done | bytes 593952 | tf_op jit(solution)/shard_map/ppermute | solution.py:24
  80.6 0.7 shard_map.45
  81.2 2.7 %collective-permute-start.13 = (f32[128,128]{1,0:T(8,128)S(1)}, f32[128,128]{1,0:T(8,128)S(1)}, u32[]{:S(2)}, u32[]{:S(2)}) collective-permute-start(f32[128,128]{1,0:T(8,128)S(1)} %get-tuple-element.42), channel_id=1, source_target_pairs={{0,4},{1,6},{2,5},{3,7},{4,8},{5,10},{6,9},{7,11},{8,12},{9,14},{1... | collective-permute-start | bytes 196616 | tf_op jit(solution)/shard_map/ppermute | solution.py:24
  83.9 0.0 collective-permute-start.14
  83.9 0.0 collective-permute-done.12.got
  83.9 0.0 collective-permute-done.11.near
  83.9 6.7 %collective-permute-done.13.ahead.far_ahead = f32[128,128]{1,0:T(8,128)S(1)} collective-permute-done((f32[128,128]{1,0:T(8,128)S(1)}, f32[128,128]{1,0:T(8,128)S(1)}, u32[]{:S(2)}, u32[]{:S(2)}) %collective-permute-start.13) | collective-permute-done | bytes 65568 | tf_op jit(solution)/shard_map/ppermute | solution.py:24
  90.7 2.8 %collective-permute-done.14.behind.far_behind = f32[128,128]{1,0:T(8,128)S(1)} collective-permute-done((f32[128,128]{1,0:T(8,128)S(1)}, f32[128,128]{1,0:T(8,128)S(1)}, u32[]{:S(2)}, u32[]{:S(2)}) %collective-permute-start.14) | collective-permute-done | bytes 65568 | tf_op jit(solution)/shard_map/ppermute | solution.py:24
  93.5 1.0 %collective-permute-start.15 = (f32[64,768]{1,0:T(8,128)S(1)}, f32[64,768]{1,0:T(8,128)S(1)}, u32[]{:S(2)}, u32[]{:S(2)}) collective-permute-start(f32[64,768]{1,0:T(8,128)S(1)} %shard_map.46), channel_id=1, source_target_pairs={{0,1},{1,0},{2,3},{3,2},{4,5},{5,4},{6,7},{7,6},{8,9},{9,8},{10,11... | collective-permute-start | bytes 589832 | tf_op jit(solution)/shard_map/ppermute | solution.py:24
  94.5 1.1 %collective-permute-done.15.other = f32[64,768]{1,0:T(8,128)S(1)} collective-permute-done((f32[64,768]{1,0:T(8,128)S(1)}, f32[64,768]{1,0:T(8,128)S(1)}, u32[]{:S(2)}, u32[]{:S(2)}) %collective-permute-start.15) | collective-permute-done | bytes 196640 | tf_op jit(solution)/shard_map/ppermute | solution.py:24
  95.5 0.8 shard_map.47
  (1 shorter events, 0.0 us)
Async XLA Ops:
  0.6 22.2 %collective-permute-start = (f32[3,300,256]{2,1,0:T(8,128)}, f32[3,300,256]{2,1,0:T(8,128)S(1)}, u32[]{:S(2)}, u32[]{:S(2)}) collective-permute-start(f32[3,300,256]{2,1,0:T(8,128)} %a_ref.1), channel_id=1, source_target_pairs={{0,2},{1,3},{2,0},{3,1},{4,6},{5,7},{6,4},{7,5},{8,10},{9,11},{10,... | collective-permute-start | bytes 2764808 | tf_op jit(solution)/shard_map/ppermute | solution.py:24
  3.2 31.9 %collective-permute-start.5 = (f32[3,300,256]{2,1,0:T(8,128)}, f32[3,300,256]{2,1,0:T(8,128)S(1)}, u32[]{:S(2)}, u32[]{:S(2)}) collective-permute-start(f32[3,300,256]{2,1,0:T(8,128)} %a_ref.1), channel_id=1, source_target_pairs={{0,254},{1,255},{2,244},{3,245},{4,2},{5,3},{6,248},{7,249},{8,6},... | collective-permute-start | bytes 2764808 | tf_op jit(solution)/shard_map/ppermute | solution.py:24
  12.5 26.9 %collective-permute-start.2 = (f32[3,300,256]{2,1,0:T(8,128)}, f32[3,300,256]{2,1,0:T(8,128)S(1)}, u32[]{:S(2)}, u32[]{:S(2)}) collective-permute-start(f32[3,300,256]{2,1,0:T(8,128)} %a_ref.1), channel_id=1, source_target_pairs={{0,1},{1,0},{2,3},{3,2},{4,5},{5,4},{6,7},{7,6},{8,9},{9,8},{10,11... | collective-permute-start | bytes 2764808 | tf_op jit(solution)/shard_map/ppermute | solution.py:24
  22.9 18.7 %collective-permute-start.3 = (f32[3,300,256]{2,1,0:T(8,128)S(1)}, f32[3,300,256]{2,1,0:T(8,128)S(1)}, u32[]{:S(2)}, u32[]{:S(2)}) collective-permute-start(f32[3,300,256]{2,1,0:T(8,128)S(1)} %collective-permute-done.c_ref), channel_id=1, source_target_pairs={{0,1},{1,0},{2,3},{3,2},{4,5},{5,4},{6,7},{7,6},{8,9},{9,8},{10,11... | collective-permute-start | bytes 2764808 | tf_op jit(solution)/shard_map/ppermute | solution.py:24
  25.0 30.2 %collective-permute-start.1 = (f32[3,300,256]{2,1,0:T(8,128)S(1)}, f32[3,300,256]{2,1,0:T(8,128)S(1)}, u32[]{:S(2)}, u32[]{:S(2)}) collective-permute-start(f32[3,300,256]{2,1,0:T(8,128)S(1)} %collective-permute-done.c_ref), channel_id=1, source_target_pairs={{0,254},{1,255},{2,244},{3,245},{4,2},{5,3},{6,248},{7,249},{8,6},... | collective-permute-start | bytes 2764808 | tf_op jit(solution)/shard_map/ppermute | solution.py:24
  35.1 22.0 %collective-permute-start.8 = (f32[3,300,256]{2,1,0:T(8,128)S(1)}, f32[3,300,256]{2,1,0:T(8,128)S(1)}, u32[]{:S(2)}, u32[]{:S(2)}) collective-permute-start(f32[3,300,256]{2,1,0:T(8,128)S(1)} %collective-permute-done.5.a), channel_id=1, source_target_pairs={{0,2},{1,3},{2,0},{3,1},{4,6},{5,7},{6,4},{7,5},{8,10},{9,11},{10,... | collective-permute-start | bytes 2764808 | tf_op jit(solution)/shard_map/ppermute | solution.py:24
  35.1 20.2 %collective-permute-start.4 = (s32[1]{0:T(128)}, s32[1]{0:T(128)}, u32[]{:S(2)}, u32[]{:S(2)}) collective-permute-start(s32[1]{0:T(128)} %param.3), channel_id=1, source_target_pairs={{0,254},{1,255},{2,244},{3,245},{4,2},{5,3},{6,248},{7,249},{8,6},... | collective-permute-start | bytes 20 | tf_op jit(solution)/shard_map/ppermute | solution.py:24
  39.4 18.8 %collective-permute-start.6 = (f32[3,300,256]{2,1,0:T(8,128)S(1)}, f32[3,300,256]{2,1,0:T(8,128)S(1)}, u32[]{:S(2)}, u32[]{:S(2)}) collective-permute-start(f32[3,300,256]{2,1,0:T(8,128)S(1)} %collective-permute-done.5.a), channel_id=1, source_target_pairs={{0,1},{1,0},{2,3},{3,2},{4,5},{5,4},{6,7},{7,6},{8,9},{9,8},{10,11... | collective-permute-start | bytes 2764808 | tf_op jit(solution)/shard_map/ppermute | solution.py:24
  41.5 1.2 %copy-start = (f32[3,300,256]{2,1,0:T(8,128)S(1)}, f32[3,300,256]{2,1,0:T(8,128)}, u32[]{:S(2)}) copy-start(f32[3,300,256]{2,1,0:T(8,128)} %a_ref.1) | copy-start | bytes 2764804
  55.3 5.9 %collective-permute-start.7 = (f32[3,300,256]{2,1,0:T(8,128)S(1)}, f32[3,300,256]{2,1,0:T(8,128)S(1)}, u32[]{:S(2)}, u32[]{:S(2)}) collective-permute-start(f32[3,300,256]{2,1,0:T(8,128)S(1)} %collective-permute-done.1.near_a.a), channel_id=1, source_target_pairs={{0,1},{1,0},{2,3},{3,2},{4,5},{5,4},{6,7},{7,6},{8,9},{9,8},{10,11... | collective-permute-start | bytes 2764808 | tf_op jit(solution)/shard_map/ppermute | solution.py:24
  57.1 4.1 %collective-permute-start.9 = (f32[3,300,256]{2,1,0:T(8,128)S(1)}, f32[3,300,256]{2,1,0:T(8,128)S(1)}, u32[]{:S(2)}, u32[]{:S(2)}) collective-permute-start(f32[3,300,256]{2,1,0:T(8,128)S(1)} %collective-permute-done.8.else_a), channel_id=1, source_target_pairs={{0,1},{1,0},{2,3},{3,2},{4,5},{5,4},{6,7},{7,6},{8,9},{9,8},{10,11... | collective-permute-start | bytes 2764808 | tf_op jit(solution)/shard_map/ppermute | solution.py:24
  63.8 16.8 %collective-permute-start.10 = (f32[1160,128]{1,0:T(8,128)S(1)}, f32[1160,128]{1,0:T(8,128)S(1)}, u32[]{:S(2)}, u32[]{:S(2)}) collective-permute-start(f32[1160,128]{1,0:T(8,128)S(1)} %get-tuple-element.35), channel_id=1, source_target_pairs={{0,2},{1,3},{2,0},{3,1},{4,6},{5,7},{6,4},{7,5},{8,10},{9,11},{10,... | collective-permute-start | bytes 1781768 | tf_op jit(solution)/shard_map/ppermute | solution.py:24
  67.8 16.1 %collective-permute-start.11 = (f32[128,256]{1,0:T(8,128)S(1)}, f32[128,256]{1,0:T(8,128)S(1)}, u32[]{:S(2)}, u32[]{:S(2)}) collective-permute-start(f32[128,256]{1,0:T(8,128)S(1)} %get-tuple-element.37), channel_id=1, source_target_pairs={{0,13},{1,15},{2,4},{3,6},{4,17},{5,19},{6,8},{7,10},{8,21},{9,23}... | collective-permute-start | bytes 393224 | tf_op jit(solution)/shard_map/ppermute | solution.py:24
  67.9 16.0 %collective-permute-start.12 = (f32[128,128]{1,0:T(8,128)S(1)}, f32[128,128]{1,0:T(8,128)S(1)}, u32[]{:S(2)}, u32[]{:S(2)}) collective-permute-start(f32[128,128]{1,0:T(8,128)S(1)} %get-tuple-element.41), channel_id=1, source_target_pairs={{0,2},{1,3},{2,0},{3,1},{4,6},{5,7},{6,4},{7,5},{8,10},{9,11},{10,... | collective-permute-start | bytes 196616 | tf_op jit(solution)/shard_map/ppermute | solution.py:24
  81.2 9.4 %collective-permute-start.13 = (f32[128,128]{1,0:T(8,128)S(1)}, f32[128,128]{1,0:T(8,128)S(1)}, u32[]{:S(2)}, u32[]{:S(2)}) collective-permute-start(f32[128,128]{1,0:T(8,128)S(1)} %get-tuple-element.42), channel_id=1, source_target_pairs={{0,4},{1,6},{2,5},{3,7},{4,8},{5,10},{6,9},{7,11},{8,12},{9,14},{1... | collective-permute-start | bytes 196616 | tf_op jit(solution)/shard_map/ppermute | solution.py:24
  83.9 9.5 %collective-permute-start.14 = (f32[128,128]{1,0:T(8,128)S(1)}, f32[128,128]{1,0:T(8,128)S(1)}, u32[]{:S(2)}, u32[]{:S(2)}) collective-permute-start(f32[128,128]{1,0:T(8,128)S(1)} %get-tuple-element.43), channel_id=1, source_target_pairs={{0,12},{1,13},{2,14},{3,15},{4,16},{5,17},{6,18},{7,19},{8,20},{9,... | collective-permute-start | bytes 196616 | tf_op jit(solution)/shard_map/ppermute | solution.py:24
  93.5 2.1 %collective-permute-start.15 = (f32[64,768]{1,0:T(8,128)S(1)}, f32[64,768]{1,0:T(8,128)S(1)}, u32[]{:S(2)}, u32[]{:S(2)}) collective-permute-start(f32[64,768]{1,0:T(8,128)S(1)} %shard_map.46), channel_id=1, source_target_pairs={{0,1},{1,0},{2,3},{3,2},{4,5},{5,4},{6,7},{7,6},{8,9},{9,8},{10,11... | collective-permute-start | bytes 589832 | tf_op jit(solution)/shard_map/ppermute | solution.py:24

commit v6 on v5

--- a/solution.py
+++ b/solution.py
@@ -127,19 +127,6 @@
         tile[at:at + step, :] = jnp.where(valid(place, column), deviation(covariance(at, at + step), total), 0.0)
 
 
-def right_side(refs, lanes, about, right_high, right_low):
-    total, square = [], jnp.zeros((1, 128), jnp.float32)
-    for comp in range(3):
-        moved = [ref[comp, :, lanes] - about[comp:comp + 1, :] for ref in refs]
-        total.append(column_sums(moved))
-        square = square + column_sums([value * value for value in moved])
-        for place, value in enumerate(moved):
-            top, rest = halves(padded(value))
-            right_high[place * PIECE:(place + 1) * PIECE, comp * 128:(comp + 1) * 128] = top
-            right_low[place * PIECE:(place + 1) * PIECE, comp * 128:(comp + 1) * 128] = rest
-    return total, square
-
-
 def half_facts(refs, out):
     square = 0.0
     for comp in range(3):
@@ -151,24 +138,26 @@
     out[4:8, :] = jnp.zeros((4, out.shape[1]), jnp.float32)
 
 
-def near_first_kernel(count, high, low, a, b, acc, facts, right_high, right_low):
+def facts_kernel(count, a, b, facts):
     half_facts((a, b), facts)
     facts[4:5, :] = jnp.full((1, facts.shape[1]), count[0], jnp.int32).astype(jnp.float32)
-    lanes = aligned(place_of()[1], 128)
-    right_side((a, b), lanes, facts[:, lanes], right_high, right_low)
-    acc[...] = products(high[:, DEPTH // 2:], low[:, DEPTH // 2:], right_high[...], right_low[...])
-
-
-def near_kernel(own_count, high, low, square, first, facts, a, b, out, keep, give, own_mask, right_high, right_low, acc, tile):
+
+
+def near_kernel(own_count, high, low, square, a, b, c, d, out, keep, give, own_mask, right_high, right_low, acc, tile):
     low_place, core = place_of()
     lanes = aligned(core, 128)
-    about = facts[:, lanes]
-    total, column_square = right_side((a, b), lanes, about, right_high, right_low)
-    column_square = (column_square + about[3:4, :]) / NATOM
-    for comp in range(3):
-        offset = total[comp] / NATOM
-        column_square = column_square - offset * offset
-    acc[...] = first[...] + products(high[:, :DEPTH // 2], low[:, :DEPTH // 2], right_high[...], right_low[...])
+    column_square = jnp.zeros((1, 128), jnp.float32)
+    for comp in range(3):
+        pieces = [ref[comp, :, lanes] for ref in (a, b, c, d)]
+        centroid = column_sums(pieces) / NATOM
+        for place, piece in enumerate(pieces):
+            value = piece - centroid
+            column_square = column_square + column_sums([value * value])
+            top, rest = halves(padded(value))
+            right_high[place * PIECE:(place + 1) * PIECE, comp * 128:(comp + 1) * 128] = top
+            right_low[place * PIECE:(place + 1) * PIECE, comp * 128:(comp + 1) * 128] = rest
+    column_square = column_square / NATOM
+    acc[...] = products(high[...], low[...], right_high[...], right_low[...])
     frames = square.shape[0]
 
     def covariance(start, stop):
@@ -333,11 +322,8 @@
     high, low, square = call(
         prepare_kernel, (bf16(768, DEPTH), bf16(768, DEPTH), f32(frames, 128)), 0.3
     )(coords, own_core, own_chip, own_both)
-    sides = [((DEPTH // 2, 384), small), ((DEPTH // 2, 384), small)]
     near_b, high, near_count = together((near_b, high, near_count))
-    near_first, facts = call(near_first_kernel, (f32(768, 384), f32(8, 256)), 0.3, sides)(
-        near_count, high, low, near_a, near_a_core
-    )
+    facts = call(facts_kernel, f32(8, 256), 0.3)(near_count, near_a, near_a_core)
     near_b_core = route(near_b, other_core)
     else_a_core = route(else_a, other_core)
     mine, give = call(
@@ -348,13 +334,13 @@
          ((384, 768), wide), ((8, 256), wide), ((8, 256), wide)],
     )(facts, near_b, near_b_core, else_a, else_a_core)
     got = route(give, other_chip)
-    near_first, mine = together((near_first, mine))
+    high, mine = together((high, mine))
     near_out, keep, give_chip, own_mask = call(
         near_kernel,
         (f32(128, frames), f32(128, 128), f32(128, 128), f32(64, 128)),
         4.0,
-        sides + [((768, 384), wide), ((frames, 128), wide)],
-    )(frame_count, high, low, square, near_first, facts, near_b, near_b_core)
+        [((DEPTH, 384), small), ((DEPTH, 384), small), ((768, 384), wide), ((frames, 128), wide)],
+    )(frame_count, high, low, square, near_b, near_b_core, near_a, near_a_core)
     near_got = route(near_out, lambda b, r: (b + 1, 2 * (r % 2)) if r >= 2 else (b + 3, 2 * (r % 2) + 1))
     keep_got = route(give_chip, other_chip)
     got, keep, near_out = together((got, keep, near_out))

time: 96.4 us -> 95.8 us (level)
  starting transfers between devices: 39.7 us -> 41.8 us
  waiting for transfers between devices: 42.6 us -> 40.6 us
    ppermute x16, starting transfers between devices: 39.7 us -> 41.8 us  [route(): return lax.ppermute(array, ('blk', 'rep'), pairs)]
    ppermute x16, waiting for transfers between devices: 42.6 us -> 40.6 us  [route(): return lax.ppermute(array, ('blk', 'rep'), pairs)]
  transfers between devices with their start and end apart: 16 -> 16, of which waited for: 7 -> 8; matrix products, arithmetic and copies ran while one was open for 0% -> 0% of each run, Pallas kernels for 8% -> 8%
where the time goes in v6:
time: 95.8 us; the launch traced here: 95.7 us
  starting transfers between devices  41.8 us (44%)
  waiting for transfers between devices  40.6 us (42%)
  Pallas kernels  10.8 us (11%)
  between operations  1.34 us (1%)
  local copies, waits for them, and re-layouts  1.19 us (1%)
    ppermute x16, starting transfers between devices, route(): return lax.ppermute(array, ('blk', 'rep'), pairs)  41.8 us
    ppermute x16, waiting for transfers between devices, route(): return lax.ppermute(array, ('blk', 'rep'), pairs)  40.6 us
    pallas_call x7, Pallas kernels, run(): pl.pallas_call(kernel, out_shape=out_shapes, in_specs=specs, out_specs=ja...  10.8 us
  transfers between devices with their start and end apart: 16, of which 8 were waited for; matrix products, arithmetic and copies ran while one was open for 0% of the time, Pallas kernels for 8%

profile of v6, /device:TPU:1, one launch (start us, length us, event | category | flops | bytes accessed | tf_op | source)
XLA Modules:
  0.0 95.7 jit_solution(11105738296779476880)
XLA Ops:
  0.6 2.6 %collective-permute-start = (f32[3,300,256]{2,1,0:T(8,128)}, f32[3,300,256]{2,1,0:T(8,128)S(1)}, u32[]{:S(2)}, u32[]{:S(2)}) collective-permute-start(f32[3,300,256]{2,1,0:T(8,128)} %a_ref.1), channel_id=1, source_target_pairs={{0,2},{1,3},{2,0},{3,1},{4,6},{5,7},{6,4},{7,5},{8,10},{9,11},{10,... | collective-permute-start | bytes 2764808 | tf_op jit(solution)/shard_map/ppermute | solution.py:24
  3.2 9.3 %collective-permute-start.5 = (f32[3,300,256]{2,1,0:T(8,128)}, f32[3,300,256]{2,1,0:T(8,128)S(1)}, u32[]{:S(2)}, u32[]{:S(2)}) collective-permute-start(f32[3,300,256]{2,1,0:T(8,128)} %a_ref.1), channel_id=1, source_target_pairs={{0,254},{1,255},{2,244},{3,245},{4,2},{5,3},{6,248},{7,249},{8,6},... | collective-permute-start | bytes 2764808 | tf_op jit(solution)/shard_map/ppermute | solution.py:24
  12.5 1.2 %collective-permute-start.2 = (f32[3,300,256]{2,1,0:T(8,128)}, f32[3,300,256]{2,1,0:T(8,128)S(1)}, u32[]{:S(2)}, u32[]{:S(2)}) collective-permute-start(f32[3,300,256]{2,1,0:T(8,128)} %a_ref.1), channel_id=1, source_target_pairs={{0,1},{1,0},{2,3},{3,2},{4,5},{5,4},{6,7},{7,6},{8,9},{9,8},{10,11... | collective-permute-start | bytes 2764808 | tf_op jit(solution)/shard_map/ppermute | solution.py:24
  13.7 9.1 %collective-permute-done.c_ref = f32[3,300,256]{2,1,0:T(8,128)S(1)} collective-permute-done((f32[3,300,256]{2,1,0:T(8,128)}, f32[3,300,256]{2,1,0:T(8,128)S(1)}, u32[]{:S(2)}, u32[]{:S(2)}) %collective-permute-start) | collective-permute-done | bytes 921632 | tf_op jit(solution)/shard_map/ppermute | solution.py:24
  22.9 2.2 %collective-permute-start.3 = (f32[3,300,256]{2,1,0:T(8,128)S(1)}, f32[3,300,256]{2,1,0:T(8,128)S(1)}, u32[]{:S(2)}, u32[]{:S(2)}) collective-permute-start(f32[3,300,256]{2,1,0:T(8,128)S(1)} %collective-permute-done.c_ref), channel_id=1, source_target_pairs={{0,1},{1,0},{2,3},{3,2},{4,5},{5,4},{6,7},{7,6},{8,9},{9,8},{10,11... | collective-permute-start | bytes 2764808 | tf_op jit(solution)/shard_map/ppermute | solution.py:24
  25.0 10.0 %collective-permute-start.1 = (f32[3,300,256]{2,1,0:T(8,128)S(1)}, f32[3,300,256]{2,1,0:T(8,128)S(1)}, u32[]{:S(2)}, u32[]{:S(2)}) collective-permute-start(f32[3,300,256]{2,1,0:T(8,128)S(1)} %collective-permute-done.c_ref), channel_id=1, source_target_pairs={{0,254},{1,255},{2,244},{3,245},{4,2},{5,3},{6,248},{7,249},{8,6},... | collective-permute-start | bytes 2764808 | tf_op jit(solution)/shard_map/ppermute | solution.py:24
  35.1 0.0 collective-permute-done.5.a.c
  35.1 0.0 collective-permute-start.8
  35.1 4.3 %collective-permute-start.4 = (s32[1]{0:T(128)}, s32[1]{0:T(128)}, u32[]{:S(2)}, u32[]{:S(2)}) collective-permute-start(s32[1]{0:T(128)} %param.3), channel_id=1, source_target_pairs={{0,254},{1,255},{2,244},{3,245},{4,2},{5,3},{6,248},{7,249},{8,6},... | collective-permute-start | bytes 20 | tf_op jit(solution)/shard_map/ppermute | solution.py:24
  39.4 0.0 collective-permute-done.2.b_ref
  39.4 2.1 %collective-permute-start.6 = (f32[3,300,256]{2,1,0:T(8,128)S(1)}, f32[3,300,256]{2,1,0:T(8,128)S(1)}, u32[]{:S(2)}, u32[]{:S(2)}) collective-permute-start(f32[3,300,256]{2,1,0:T(8,128)S(1)} %collective-permute-done.5.a.c), channel_id=1, source_target_pairs={{0,1},{1,0},{2,3},{3,2},{4,5},{5,4},{6,7},{7,6},{8,9},{9,8},{10,11... | collective-permute-start | bytes 2764808 | tf_op jit(solution)/shard_map/ppermute | solution.py:24
  41.5 0.0 collective-permute-done.3.d_ref
  41.5 0.0 copy-start
  41.5 1.2 %copy-done = f32[3,300,256]{2,1,0:T(8,128)S(1)} copy-done((f32[3,300,256]{2,1,0:T(8,128)S(1)}, f32[3,300,256]{2,1,0:T(8,128)}, u32[]{:S(2)}) %copy-start) | copy-done | bytes 921624
  42.7 1.4 %shard_map.41 = (bf16[768,1280]{1,0:T(8,128)(2,1)S(1)}, bf16[768,1280]{1,0:T(8,128)(2,1)S(1)}, f32[256,128]{1,0:T(8,128)S(1)}) custom-call(f32[3,300,256]{2,1,0:T(8,128)S(1)} %copy-done, f32[3,300,256]{2,1,0:T(8,128)S(1)} %collective-permute-done.2.b_ref, f32[3,300,256]{2,1,0:T(8,128)S(1)} %collective-permute-done.c_ref, ...), custom_call_target="tpu_custom_call" | custom-call | bytes 1080000 | tf_op jit(solution)/shard_map/pallas_call | solution.py:287
  44.2 11.1 %collective-permute-done.4.count = s32[1]{0:T(128)} collective-permute-done((s32[1]{0:T(128)}, s32[1]{0:T(128)}, u32[]{:S(2)}, u32[]{:S(2)}) %collective-permute-start.4) | collective-permute-done | bytes 36 | tf_op jit(solution)/shard_map/ppermute | solution.py:24
  55.3 0.0 collective-permute-done.1.near_a.a
  55.3 0.8 collective-permute-start.7
  56.1 1.1 %collective-permute-done.8.else_a = f32[3,300,256]{2,1,0:T(8,128)S(1)} collective-permute-done((f32[3,300,256]{2,1,0:T(8,128)S(1)}, f32[3,300,256]{2,1,0:T(8,128)S(1)}, u32[]{:S(2)}, u32[]{:S(2)}) %collective-permute-start.8) | collective-permute-done | bytes 921632 | tf_op jit(solution)/shard_map/ppermute | solution.py:24
  57.1 1.1 %collective-permute-start.9 = (f32[3,300,256]{2,1,0:T(8,128)S(1)}, f32[3,300,256]{2,1,0:T(8,128)S(1)}, u32[]{:S(2)}, u32[]{:S(2)}) collective-permute-start(f32[3,300,256]{2,1,0:T(8,128)S(1)} %collective-permute-done.8.else_a), channel_id=1, source_target_pairs={{0,1},{1,0},{2,3},{3,2},{4,5},{5,4},{6,7},{7,6},{8,9},{9,8},{10,11... | collective-permute-start | bytes 2764808 | tf_op jit(solution)/shard_map/ppermute | solution.py:24
  58.2 0.0 collective-permute-done.6.b.d
  58.2 0.9 shard_map.42.facts
  59.1 0.0 collective-permute-done.7.near_b.b
  59.2 1.2 %collective-permute-done.9.else_b = f32[3,300,256]{2,1,0:T(8,128)S(1)} collective-permute-done((f32[3,300,256]{2,1,0:T(8,128)S(1)}, f32[3,300,256]{2,1,0:T(8,128)S(1)}, u32[]{:S(2)}, u32[]{:S(2)}) %collective-permute-start.9) | collective-permute-done | bytes 921632 | tf_op jit(solution)/shard_map/ppermute | solution.py:24
  60.3 2.5 %shard_map.43 = (f32[1160,128]{1,0:T(8,128)S(1)}, f32[1160,128]{1,0:T(8,128)S(1)}) custom-call(f32[8,256]{1,0:T(8,128)S(1)} %shard_map.42.facts, f32[3,300,256]{2,1,0:T(8,128)S(1)} %collective-permute-done.1.near_a.a, f32[3,300,256]{2,1,0:T(8,128)S(1)} %collective-permute-done.7.near_b.b, f32[3,300,256]{2,1,0:T(8,128)S(1)} %collective-permute-done.8.else_a, ...), custom_call_target="tpu_custom_call" | custom-call | bytes 10800000 | tf_op jit(solution)/shard_map/pallas_call | solution.py:287
  62.8 0.3 collective-permute-start.10
  63.8 4.5 %shard_map.44 = (f32[128,256]{1,0:T(8,128)S(1)}, f32[128,128]{1,0:T(8,128)S(1)}, f32[128,128]{1,0:T(8,128)S(1)}, f32[64,128]{1,0:T(8,128)S(1)}) custom-call(s32[1]{0:T(128)S(6)} %copy.4.own_count, bf16[768,1280]{1,0:T(8,128)(2,1)S(1)} %get-tuple-element.26.high, bf16[768,1280]{1,0:T(8,128)(2,1)S(1)} %get-tuple-element.27.low, ...), custom_call_target="tpu_custom_call" | custom-call | bytes 14400000 | tf_op jit(solution)/shard_map/pallas_call | solution.py:287
  68.3 0.1 collective-permute-start.11
  68.4 2.4 %collective-permute-start.12 = (f32[128,128]{1,0:T(8,128)S(1)}, f32[128,128]{1,0:T(8,128)S(1)}, u32[]{:S(2)}, u32[]{:S(2)}) collective-permute-start(f32[128,128]{1,0:T(8,128)S(1)} %get-tuple-element.37), channel_id=1, source_target_pairs={{0,2},{1,3},{2,0},{3,1},{4,6},{5,7},{6,4},{7,5},{8,10},{9,11},{10,... | collective-permute-start | bytes 196616 | tf_op jit(solution)/shard_map/ppermute | solution.py:24
  70.7 8.4 %collective-permute-done.10.got = f32[1160,128]{1,0:T(8,128)S(1)} collective-permute-done((f32[1160,128]{1,0:T(8,128)S(1)}, f32[1160,128]{1,0:T(8,128)S(1)}, u32[]{:S(2)}, u32[]{:S(2)}) %collective-permute-start.10) | collective-permute-done | bytes 593952 | tf_op jit(solution)/shard_map/ppermute | solution.py:24
  79.2 0.7 shard_map.45
  79.8 3.5 %collective-permute-start.13 = (f32[128,128]{1,0:T(8,128)S(1)}, f32[128,128]{1,0:T(8,128)S(1)}, u32[]{:S(2)}, u32[]{:S(2)}) collective-permute-start(f32[128,128]{1,0:T(8,128)S(1)} %get-tuple-element.38), channel_id=1, source_target_pairs={{0,4},{1,6},{2,5},{3,7},{4,8},{5,10},{6,9},{7,11},{8,12},{9,14},{1... | collective-permute-start | bytes 196616 | tf_op jit(solution)/shard_map/ppermute | solution.py:24
  83.3 0.0 collective-permute-start.14
  83.3 0.0 collective-permute-done.12.got
  83.3 0.0 collective-permute-done.11.near
  83.3 7.7 %collective-permute-done.13.ahead.far_ahead = f32[128,128]{1,0:T(8,128)S(1)} collective-permute-done((f32[128,128]{1,0:T(8,128)S(1)}, f32[128,128]{1,0:T(8,128)S(1)}, u32[]{:S(2)}, u32[]{:S(2)}) %collective-permute-start.13) | collective-permute-done | bytes 65568 | tf_op jit(solution)/shard_map/ppermute | solution.py:24
  91.0 0.8 collective-permute-done.14.behind.far_behind
  91.9 1.9 %collective-permute-start.15 = (f32[64,768]{1,0:T(8,128)S(1)}, f32[64,768]{1,0:T(8,128)S(1)}, u32[]{:S(2)}, u32[]{:S(2)}) collective-permute-start(f32[64,768]{1,0:T(8,128)S(1)} %shard_map.46), channel_id=1, source_target_pairs={{0,1},{1,0},{2,3},{3,2},{4,5},{5,4},{6,7},{7,6},{8,9},{9,8},{10,11... | collective-permute-start | bytes 589832 | tf_op jit(solution)/shard_map/ppermute | solution.py:24
  93.8 1.1 %collective-permute-done.15.other = f32[64,768]{1,0:T(8,128)S(1)} collective-permute-done((f32[64,768]{1,0:T(8,128)S(1)}, f32[64,768]{1,0:T(8,128)S(1)}, u32[]{:S(2)}, u32[]{:S(2)}) %collective-permute-start.15) | collective-permute-done | bytes 196640 | tf_op jit(solution)/shard_map/ppermute | solution.py:24
  94.9 0.8 shard_map.47
  (1 shorter events, 0.0 us)
Async XLA Ops:
  0.6 22.2 %collective-permute-start = (f32[3,300,256]{2,1,0:T(8,128)}, f32[3,300,256]{2,1,0:T(8,128)S(1)}, u32[]{:S(2)}, u32[]{:S(2)}) collective-permute-start(f32[3,300,256]{2,1,0:T(8,128)} %a_ref.1), channel_id=1, source_target_pairs={{0,2},{1,3},{2,0},{3,1},{4,6},{5,7},{6,4},{7,5},{8,10},{9,11},{10,... | collective-permute-start | bytes 2764808 | tf_op jit(solution)/shard_map/ppermute | solution.py:24
  3.2 31.9 %collective-permute-start.5 = (f32[3,300,256]{2,1,0:T(8,128)}, f32[3,300,256]{2,1,0:T(8,128)S(1)}, u32[]{:S(2)}, u32[]{:S(2)}) collective-permute-start(f32[3,300,256]{2,1,0:T(8,128)} %a_ref.1), channel_id=1, source_target_pairs={{0,254},{1,255},{2,244},{3,245},{4,2},{5,3},{6,248},{7,249},{8,6},... | collective-permute-start | bytes 2764808 | tf_op jit(solution)/shard_map/ppermute | solution.py:24
  12.5 26.9 %collective-permute-start.2 = (f32[3,300,256]{2,1,0:T(8,128)}, f32[3,300,256]{2,1,0:T(8,128)S(1)}, u32[]{:S(2)}, u32[]{:S(2)}) collective-permute-start(f32[3,300,256]{2,1,0:T(8,128)} %a_ref.1), channel_id=1, source_target_pairs={{0,1},{1,0},{2,3},{3,2},{4,5},{5,4},{6,7},{7,6},{8,9},{9,8},{10,11... | collective-permute-start | bytes 2764808 | tf_op jit(solution)/shard_map/ppermute | solution.py:24
  22.9 18.7 %collective-permute-start.3 = (f32[3,300,256]{2,1,0:T(8,128)S(1)}, f32[3,300,256]{2,1,0:T(8,128)S(1)}, u32[]{:S(2)}, u32[]{:S(2)}) collective-permute-start(f32[3,300,256]{2,1,0:T(8,128)S(1)} %collective-permute-done.c_ref), channel_id=1, source_target_pairs={{0,1},{1,0},{2,3},{3,2},{4,5},{5,4},{6,7},{7,6},{8,9},{9,8},{10,11... | collective-permute-start | bytes 2764808 | tf_op jit(solution)/shard_map/ppermute | solution.py:24
  25.0 30.2 %collective-permute-start.1 = (f32[3,300,256]{2,1,0:T(8,128)S(1)}, f32[3,300,256]{2,1,0:T(8,128)S(1)}, u32[]{:S(2)}, u32[]{:S(2)}) collective-permute-start(f32[3,300,256]{2,1,0:T(8,128)S(1)} %collective-permute-done.c_ref), channel_id=1, source_target_pairs={{0,254},{1,255},{2,244},{3,245},{4,2},{5,3},{6,248},{7,249},{8,6},... | collective-permute-start | bytes 2764808 | tf_op jit(solution)/shard_map/ppermute | solution.py:24
  35.1 22.0 %collective-permute-start.8 = (f32[3,300,256]{2,1,0:T(8,128)S(1)}, f32[3,300,256]{2,1,0:T(8,128)S(1)}, u32[]{:S(2)}, u32[]{:S(2)}) collective-permute-start(f32[3,300,256]{2,1,0:T(8,128)S(1)} %collective-permute-done.5.a.c), channel_id=1, source_target_pairs={{0,2},{1,3},{2,0},{3,1},{4,6},{5,7},{6,4},{7,5},{8,10},{9,11},{10,... | collective-permute-start | bytes 2764808 | tf_op jit(solution)/shard_map/ppermute | solution.py:24
  35.1 20.2 %collective-permute-start.4 = (s32[1]{0:T(128)}, s32[1]{0:T(128)}, u32[]{:S(2)}, u32[]{:S(2)}) collective-permute-start(s32[1]{0:T(128)} %param.3), channel_id=1, source_target_pairs={{0,254},{1,255},{2,244},{3,245},{4,2},{5,3},{6,248},{7,249},{8,6},... | collective-permute-start | bytes 20 | tf_op jit(solution)/shard_map/ppermute | solution.py:24
  39.4 18.8 %collective-permute-start.6 = (f32[3,300,256]{2,1,0:T(8,128)S(1)}, f32[3,300,256]{2,1,0:T(8,128)S(1)}, u32[]{:S(2)}, u32[]{:S(2)}) collective-permute-start(f32[3,300,256]{2,1,0:T(8,128)S(1)} %collective-permute-done.5.a.c), channel_id=1, source_target_pairs={{0,1},{1,0},{2,3},{3,2},{4,5},{5,4},{6,7},{7,6},{8,9},{9,8},{10,11... | collective-permute-start | bytes 2764808 | tf_op jit(solution)/shard_map/ppermute | solution.py:24
  41.5 1.2 %copy-start = (f32[3,300,256]{2,1,0:T(8,128)S(1)}, f32[3,300,256]{2,1,0:T(8,128)}, u32[]{:S(2)}) copy-start(f32[3,300,256]{2,1,0:T(8,128)} %a_ref.1) | copy-start | bytes 2764804
  55.3 3.9 %collective-permute-start.7 = (f32[3,300,256]{2,1,0:T(8,128)S(1)}, f32[3,300,256]{2,1,0:T(8,128)S(1)}, u32[]{:S(2)}, u32[]{:S(2)}) collective-permute-start(f32[3,300,256]{2,1,0:T(8,128)S(1)} %collective-permute-done.1.near_a.a), channel_id=1, source_target_pairs={{0,1},{1,0},{2,3},{3,2},{4,5},{5,4},{6,7},{7,6},{8,9},{9,8},{10,11... | collective-permute-start | bytes 2764808 | tf_op jit(solution)/shard_map/ppermute | solution.py:24
  57.1 3.2 %collective-permute-start.9 = (f32[3,300,256]{2,1,0:T(8,128)S(1)}, f32[3,300,256]{2,1,0:T(8,128)S(1)}, u32[]{:S(2)}, u32[]{:S(2)}) collective-permute-start(f32[3,300,256]{2,1,0:T(8,128)S(1)} %collective-permute-done.8.else_a), channel_id=1, source_target_pairs={{0,1},{1,0},{2,3},{3,2},{4,5},{5,4},{6,7},{7,6},{8,9},{9,8},{10,11... | collective-permute-start | bytes 2764808 | tf_op jit(solution)/shard_map/ppermute | solution.py:24
  62.8 16.3 %collective-permute-start.10 = (f32[1160,128]{1,0:T(8,128)S(1)}, f32[1160,128]{1,0:T(8,128)S(1)}, u32[]{:S(2)}, u32[]{:S(2)}) collective-permute-start(f32[1160,128]{1,0:T(8,128)S(1)} %get-tuple-element.31), channel_id=1, source_target_pairs={{0,2},{1,3},{2,0},{3,1},{4,6},{5,7},{6,4},{7,5},{8,10},{9,11},{10,... | collective-permute-start | bytes 1781768 | tf_op jit(solution)/shard_map/ppermute | solution.py:24
  68.3 15.0 %collective-permute-start.11 = (f32[128,256]{1,0:T(8,128)S(1)}, f32[128,256]{1,0:T(8,128)S(1)}, u32[]{:S(2)}, u32[]{:S(2)}) collective-permute-start(f32[128,256]{1,0:T(8,128)S(1)} %get-tuple-element.33), channel_id=1, source_target_pairs={{0,13},{1,15},{2,4},{3,6},{4,17},{5,19},{6,8},{7,10},{8,21},{9,23}... | collective-permute-start | bytes 393224 | tf_op jit(solution)/shard_map/ppermute | solution.py:24
  68.4 14.9 %collective-permute-start.12 = (f32[128,128]{1,0:T(8,128)S(1)}, f32[128,128]{1,0:T(8,128)S(1)}, u32[]{:S(2)}, u32[]{:S(2)}) collective-permute-start(f32[128,128]{1,0:T(8,128)S(1)} %get-tuple-element.37), channel_id=1, source_target_pairs={{0,2},{1,3},{2,0},{3,1},{4,6},{5,7},{6,4},{7,5},{8,10},{9,11},{10,... | collective-permute-start | bytes 196616 | tf_op jit(solution)/shard_map/ppermute | solution.py:24
  79.8 11.2 %collective-permute-start.13 = (f32[128,128]{1,0:T(8,128)S(1)}, f32[128,128]{1,0:T(8,128)S(1)}, u32[]{:S(2)}, u32[]{:S(2)}) collective-permute-start(f32[128,128]{1,0:T(8,128)S(1)} %get-tuple-element.38), channel_id=1, source_target_pairs={{0,4},{1,6},{2,5},{3,7},{4,8},{5,10},{6,9},{7,11},{8,12},{9,14},{1... | collective-permute-start | bytes 196616 | tf_op jit(solution)/shard_map/ppermute | solution.py:24
  83.3 8.6 %collective-permute-start.14 = (f32[128,128]{1,0:T(8,128)S(1)}, f32[128,128]{1,0:T(8,128)S(1)}, u32[]{:S(2)}, u32[]{:S(2)}) collective-permute-start(f32[128,128]{1,0:T(8,128)S(1)} %get-tuple-element.39), channel_id=1, source_target_pairs={{0,12},{1,13},{2,14},{3,15},{4,16},{5,17},{6,18},{7,19},{8,20},{9,... | collective-permute-start | bytes 196616 | tf_op jit(solution)/shard_map/ppermute | solution.py:24
  91.9 3.0 %collective-permute-start.15 = (f32[64,768]{1,0:T(8,128)S(1)}, f32[64,768]{1,0:T(8,128)S(1)}, u32[]{:S(2)}, u32[]{:S(2)}) collective-permute-start(f32[64,768]{1,0:T(8,128)S(1)} %shard_map.46), channel_id=1, source_target_pairs={{0,1},{1,0},{2,3},{3,2},{4,5},{5,4},{6,7},{7,6},{8,9},{9,8},{10,11... | collective-permute-start | bytes 589832 | tf_op jit(solution)/shard_map/ppermute | solution.py:24
